TPU v7x, 32 devices: a whole 2x2x4 slice. The times are simulated.
32 devices in a mesh: dp: 8 (over z, x), chan: 4 (over y, core).
Axes of the slice: x: 2, y: 2, z: 4, core: 2. Of those that a mesh axis runs over, the one named last changes fastest.
Arguments:
- tokens: bfloat16 [75264, 1024], P(('dp', 'chan')), may hold values from -6 to 6
- frame_counts: int32 [8], P('dp'), may hold values from 2 to 12, as said below
- cotangent: bfloat16 [75264, 1024], P(('dp', 'chan')), may hold values from -6 to 6
- w_reduce: float32 [2, 1024, 256], P(None, None, 'chan'), may hold values from -0.1875 to 0.1875
- w_mix: float32 [2, 256, 256], P(None, None, 'chan'), may hold values from -0.375 to 0.375
- w_depth: float32 [2, 27, 256], P(None, None, 'chan'), may hold values from -1.25 to 1.25
- w_expand: float32 [2, 256, 1024], P(None, 'chan'), may hold values from -0.375 to 0.375
- norm_mid: float32 [2, 3, 2, 256], P(None, None, None, 'chan'), may hold values from -1.2 to 1.4
- norm_out: float32 [2, 2, 1024], replicated, may hold values from -1.2 to 1.4
- moment_reduce: float32 [2, 1024, 256], P(None, None, 'chan'), may hold values from -2352 to 2352
- moment_mix: float32 [2, 256, 256], P(None, None, 'chan'), may hold values from -2352 to 2352
- moment_depth: float32 [2, 27, 256], P(None, None, 'chan'), may hold values from -2352 to 2352
- moment_expand: float32 [2, 256, 1024], P(None, 'chan'), may hold values from -2352 to 2352
- moment_mid: float32 [2, 3, 2, 256], P(None, None, None, 'chan'), may hold values from -2352 to 2352
- moment_out: float32 [2, 2, 1024], replicated, may hold values from -2352 to 2352
Outputs:
- output: bfloat16 [75264, 1024], P(('dp', 'chan'))
- grad_tokens: bfloat16 [75264, 1024], P(('dp', 'chan'))
- grad_reduce: float32 [2, 1024, 256], P(None, None, 'chan')
- grad_mix: float32 [2, 256, 256], P(None, None, 'chan')
- grad_depth: float32 [2, 27, 256], P(None, None, 'chan')
- grad_expand: float32 [2, 256, 1024], P(None, 'chan')
- grad_mid: float32 [2, 3, 2, 256], P(None, None, None, 'chan')
- grad_out: float32 [2, 2, 1024], replicated
- new_reduce: float32 [2, 1024, 256], P(None, None, 'chan')
- new_mix: float32 [2, 256, 256], P(None, None, 'chan')
- new_depth: float32 [2, 27, 256], P(None, None, 'chan')
- new_expand: float32 [2, 256, 1024], P(None, 'chan')
- new_mid: float32 [2, 3, 2, 256], P(None, None, None, 'chan')
- new_out: float32 [2, 2, 1024], replicated
- new_moment_reduce: float32 [2, 1024, 256], P(None, None, 'chan')
- new_moment_mix: float32 [2, 256, 256], P(None, None, 'chan')
- new_moment_depth: float32 [2, 27, 256], P(None, None, 'chan')
- new_moment_expand: float32 [2, 256, 1024], P(None, 'chan')
- new_moment_mid: float32 [2, 3, 2, 256], P(None, None, None, 'chan')
- new_moment_out: float32 [2, 2, 1024], replicated
Inputs may be any that keep to these rules, and one draw needn't show every extreme that they name: `frame_counts`: each clip has 2 to 12 real frames; some clip has exactly 12 and some exactly 2.
All inputs are finite; a program needn't handle non-finite values.
Results may differ from a plain program's by a relative error of at most 0.018.
Values may be sent and summed in bfloat16 or wider, within the bound.
A program may use at most 384 MiB of HBM per device.

v0:
```python
import jax
import jax.numpy as jnp
from jax import lax
from jax.sharding import PartitionSpec as P

FRAMES = 12
HH = 28
WW = 28
BLOCKS = 2


EPS = 1e-05
LEARN_RATE = 0.001
MOMENTUM = 0.9
DECAY = 0.0001


def gelu_soft(value):
    return jax.nn.gelu(value, approximate=True)


def gelu_back(value, grad):
    return jax.vjp(gelu_soft, value)[1](grad)[0]


def matmul(left, right):
    return jnp.dot(left, right, preferred_element_type=jnp.float32)


def matmul_left(left, right):
    return lax.dot_general(
        left, right, (((0,), (0,)), ((), ())), preferred_element_type=jnp.float32
    )


def matmul_right(left, right):
    return lax.dot_general(
        left, right, (((1,), (1,)), ((), ())), preferred_element_type=jnp.float32
    )


def widen(vector, offset, full):
    if vector.shape[0] == full:
        return vector
    return lax.dynamic_update_slice(jnp.zeros((full,), jnp.float32), vector, (offset,))


def narrow(vector, offset, width):
    if vector.shape[0] == width:
        return vector
    return lax.dynamic_slice_in_dim(vector, offset, width, 0)


def frame_mask(frame_counts, first_frame, local_frames):
    position = first_frame + jnp.arange(local_frames)
    owner = (position // FRAMES)[:, None] == jnp.arange(frame_counts.shape[0])[None, :]
    limit = jnp.sum(jnp.where(owner, frame_counts[None, :], 0), axis=1)
    alive = (position % FRAMES < limit).astype(jnp.float32)
    return jnp.broadcast_to(alive[:, None], (local_frames, HH * WW)).reshape(-1, 1)


def norm_forward(field, mask, share, offset, full, gain, shift):
    width = field.shape[1]
    totals, squares, count = lax.psum(
        (
            widen(jnp.sum(field * mask, axis=0), offset, full),
            widen(jnp.sum(field * field * mask, axis=0), offset, full),
            share,
        ),
        ("dp", "chan"),
    )
    mean = narrow(totals, offset, width) / count
    var = narrow(squares, offset, width) / count - mean * mean
    scale = lax.rsqrt(var + EPS)
    unit = (field - mean) * scale
    return (mask * (unit * gain + shift), unit, scale, count)


def norm_backward(grad, mask, unit, scale, count, gain, offset, full):
    width = grad.shape[1]
    masked = grad * mask
    shift_grad, gain_grad = lax.psum(
        (
            widen(jnp.sum(masked, axis=0), offset, full),
            widen(jnp.sum(masked * unit, axis=0), offset, full),
        ),
        ("dp", "chan"),
    )
    shift_grad = narrow(shift_grad, offset, width)
    gain_grad = narrow(gain_grad, offset, width)
    field_grad = mask * gain * scale * (masked - shift_grad / count - unit * gain_grad / count)
    return (field_grad, gain_grad, shift_grad)


def frame_inside(first_frame, local_frames, step):
    reach = (first_frame + jnp.arange(local_frames)) % FRAMES + step - 1
    return ((reach >= 0) & (reach < FRAMES)).astype(jnp.float32)[:, None, None, None]


def depthwise(field, kern, first_frame):
    width = field.shape[1]
    local_frames = field.shape[0] // (HH * WW)
    volume = field.reshape(local_frames, HH, WW, width)
    deep = jnp.pad(volume, ((1, 1), (0, 0), (0, 0), (0, 0)))
    padded = jnp.pad(deep, ((0, 0), (1, 1), (1, 1), (0, 0)))
    total = jnp.zeros_like(volume)
    for step in range(3):
        partial_sum = jnp.zeros_like(volume)
        for row in range(3):
            for column in range(3):
                tap = kern[step * 9 + row * 3 + column]
                partial_sum = (
                    partial_sum
                    + tap * padded[step : step + local_frames, row : row + HH, column : column + WW]
                )
        total = total + frame_inside(first_frame, local_frames, step) * partial_sum
    return (total.reshape(-1, width), padded)


def kernel_grad(grad, padded, first_frame):
    width = grad.shape[1]
    local_frames = grad.shape[0] // (HH * WW)
    volume = grad.reshape(local_frames, HH, WW, width)
    taps = []
    for step in range(3):
        inside = volume * frame_inside(first_frame, local_frames, step)
        for row in range(3):
            for column in range(3):
                shifted = padded[step : step + local_frames, row : row + HH, column : column + WW]
                taps.append(jnp.sum(inside * shifted, axis=(0, 1, 2)))
    return jnp.stack(taps)


def block_forward(inputs, weights, mask_rows, mask_io, share, first_frame, offset):
    w_reduce, w_mix, w_depth, w_expand, norm_mid, norm_out = weights
    wide = w_mix.shape[0]
    inputs_all = lax.all_gather(inputs, "chan", axis=0, tiled=True)
    first = matmul(inputs_all, w_reduce)
    norm_one, unit_one, scale_one, count = norm_forward(
        first, mask_rows, share, offset, wide, norm_mid[0, 0], norm_mid[0, 1]
    )
    act_one = (mask_rows * gelu_soft(norm_one)).astype(jnp.bfloat16)
    act_one_all = lax.all_gather(act_one, "chan", axis=1, tiled=True)
    second = matmul(act_one_all, w_mix)
    act_two, unit_two, scale_two, count = norm_forward(
        second, mask_rows, share, offset, wide, norm_mid[1, 0], norm_mid[1, 1]
    )
    third, padded = depthwise(act_two, w_depth, first_frame)
    norm_three, unit_three, scale_three, count = norm_forward(
        third, mask_rows, share, offset, wide, norm_mid[2, 0], norm_mid[2, 1]
    )
    act_three = (mask_rows * gelu_soft(norm_three)).astype(jnp.bfloat16)
    fourth = lax.psum_scatter(matmul(act_three, w_expand), "chan", scatter_dimension=0, tiled=True)
    full_out = fourth.shape[1]
    norm_four, unit_four, scale_four, count = norm_forward(
        fourth, mask_io, share, 0, full_out, norm_out[0], norm_out[1]
    )
    summed = norm_four + inputs.astype(jnp.float32)
    result = (mask_io * gelu_soft(summed)).astype(jnp.bfloat16)
    kept = (
        inputs_all,
        norm_one,
        unit_one,
        scale_one,
        act_one_all,
        unit_two,
        scale_two,
        padded,
        norm_three,
        unit_three,
        scale_three,
        act_three,
        unit_four,
        scale_four,
        summed,
        count,
    )
    return (result, kept)


def block_backward(grad_out, kept, weights, mask_rows, mask_io, first_frame, offset):
    w_reduce, w_mix, w_depth, w_expand, norm_mid, norm_out = weights
    (
        inputs_all,
        norm_one,
        unit_one,
        scale_one,
        act_one_all,
        unit_two,
        scale_two,
        padded,
        norm_three,
        unit_three,
        scale_three,
        act_three,
        unit_four,
        scale_four,
        summed,
        count,
    ) = kept
    wide = w_mix.shape[0]
    residual = gelu_back(summed, mask_io * grad_out)
    fourth_grad, gain_four, shift_four = norm_backward(
        residual, mask_io, unit_four, scale_four, count, norm_out[0], 0, residual.shape[1]
    )
    fourth_low = fourth_grad.astype(jnp.bfloat16)
    fourth_all = lax.all_gather(fourth_low, "chan", axis=0, tiled=True)
    grad_expand = matmul_left(act_three, fourth_all)
    act_three_grad = gelu_back(norm_three, mask_rows * matmul_right(fourth_all, w_expand))
    third_grad, gain_three, shift_three = norm_backward(
        act_three_grad, mask_rows, unit_three, scale_three, count, norm_mid[2, 0], offset, wide
    )
    act_two_grad, unused = depthwise(third_grad, w_depth[::-1], first_frame)
    grad_depth = kernel_grad(third_grad, padded, first_frame)
    second_grad, gain_two, shift_two = norm_backward(
        act_two_grad, mask_rows, unit_two, scale_two, count, norm_mid[1, 0], offset, wide
    )
    second_low = second_grad.astype(jnp.bfloat16)
    grad_mix = matmul_left(act_one_all, second_low)
    act_one_terms = matmul_right(second_low, w_mix)
    act_one_grad = lax.psum_scatter(act_one_terms, "chan", scatter_dimension=1, tiled=True)
    norm_one_grad = gelu_back(norm_one, mask_rows * act_one_grad)
    first_grad, gain_one, shift_one = norm_backward(
        norm_one_grad, mask_rows, unit_one, scale_one, count, norm_mid[0, 0], offset, wide
    )
    first_low = first_grad.astype(jnp.bfloat16)
    grad_reduce = matmul_left(inputs_all, first_low)
    input_grad = (
        lax.psum_scatter(matmul_right(first_low, w_reduce), "chan", scatter_dimension=0, tiled=True)
        + residual
    )
    grad_mid = jnp.stack(
        [
            jnp.stack([gain_one, shift_one]),
            jnp.stack([gain_two, shift_two]),
            jnp.stack([gain_three, shift_three]),
        ]
    )
    grad_out = jnp.stack([gain_four, shift_four])
    return (input_grad, (grad_reduce, grad_mix, grad_depth, grad_expand, grad_mid, grad_out))


def descend(weight, moment, grad):
    moment_new = MOMENTUM * moment + grad + DECAY * weight
    return (weight - LEARN_RATE * moment_new, moment_new)


def shards(
    tokens,
    frame_counts,
    cotangent,
    w_reduce,
    w_mix,
    w_depth,
    w_expand,
    norm_mid,
    norm_out,
    moment_reduce,
    moment_mix,
    moment_depth,
    moment_expand,
    moment_mid,
    moment_out,
):
    lane = lax.axis_index("chan")
    lanes = lax.axis_size("chan")
    io_rows = tokens.shape[0]
    io_frames = io_rows // (HH * WW)
    narrow_width = w_reduce.shape[2]
    mask_io = frame_mask(frame_counts, lane * io_frames, io_frames)
    reduce_use = w_reduce.astype(jnp.bfloat16)
    mix_use = w_mix.astype(jnp.bfloat16)
    expand_use = w_expand.astype(jnp.bfloat16)
    depth_use, mid_use = (w_depth, norm_mid)
    mask_rows = frame_mask(frame_counts, 0, io_frames * lanes)
    share = jnp.where(lane == 0, jnp.sum(mask_rows), 0.0)
    first_frame = 0
    offset = lane * narrow_width
    hidden = tokens
    stored = []
    for index in range(BLOCKS):
        weights = (
            reduce_use[index],
            mix_use[index],
            depth_use[index],
            expand_use[index],
            mid_use[index],
            norm_out[index],
        )
        hidden, kept = block_forward(
            hidden, weights, mask_rows, mask_io, share, first_frame, offset
        )
        stored.append(kept)
    gradient = cotangent.astype(jnp.float32)
    collected = [None] * BLOCKS
    for index in reversed(range(BLOCKS)):
        weights = (
            reduce_use[index],
            mix_use[index],
            depth_use[index],
            expand_use[index],
            mid_use[index],
            norm_out[index],
        )
        gradient, collected[index] = block_backward(
            gradient, stored[index], weights, mask_rows, mask_io, first_frame, offset
        )
    stacked = [jnp.stack([pieces[slot] for pieces in collected]) for slot in range(6)]
    grad_reduce, grad_mix, grad_depth, grad_expand = lax.psum(
        (stacked[0], stacked[1], stacked[2], stacked[3]), "dp"
    )
    grad_mid = stacked[4]
    grad_out = stacked[5]
    new_reduce, new_moment_reduce = descend(w_reduce, moment_reduce, grad_reduce)
    new_mix, new_moment_mix = descend(w_mix, moment_mix, grad_mix)
    new_depth, new_moment_depth = descend(w_depth, moment_depth, grad_depth)
    new_expand, new_moment_expand = descend(w_expand, moment_expand, grad_expand)
    new_mid, new_moment_mid = descend(norm_mid, moment_mid, grad_mid)
    new_out, new_moment_out = descend(norm_out, moment_out, grad_out)
    return (
        hidden,
        gradient.astype(jnp.bfloat16),
        grad_reduce,
        grad_mix,
        grad_depth,
        grad_expand,
        grad_mid,
        grad_out,
        new_reduce,
        new_mix,
        new_depth,
        new_expand,
        new_mid,
        new_out,
        new_moment_reduce,
        new_moment_mix,
        new_moment_depth,
        new_moment_expand,
        new_moment_mid,
        new_moment_out,
    )


def solution(mesh):
    placed = (
        P(("dp", "chan"), None),
        P("dp"),
        P(("dp", "chan"), None),
        P(None, None, "chan"),
        P(None, None, "chan"),
        P(None, None, "chan"),
        P(None, "chan", None),
        P(None, None, None, "chan"),
        P(),
        P(None, None, "chan"),
        P(None, None, "chan"),
        P(None, None, "chan"),
        P(None, "chan", None),
        P(None, None, None, "chan"),
        P(),
    )
    return jax.shard_map(
        shards,
        mesh=mesh,
        in_specs=placed,
        out_specs=(
            P(("dp", "chan"), None),
            P(("dp", "chan"), None),
            P(None, None, "chan"),
            P(None, None, "chan"),
            P(None, None, "chan"),
            P(None, "chan", None),
            P(None, None, None, "chan"),
            P(),
            P(None, None, "chan"),
            P(None, None, "chan"),
            P(None, None, "chan"),
            P(None, "chan", None),
            P(None, None, None, "chan"),
            P(),
            P(None, None, "chan"),
            P(None, None, "chan"),
            P(None, None, "chan"),
            P(None, "chan", None),
            P(None, None, None, "chan"),
            P(),
        ),
        check_vma=False,
    )
```

profile of v0, /device:TPU:0, one launch (start us, length us, event | category | flops | bytes accessed | tf_op | source)
XLA Modules:
  0.0 3045.8 jit_solution(11732956558992200803)
XLA Ops:
  11.8 122.7 %all-gather.7.cloned.1.call-done = bf16[9408,1024]{1,0:T(8,128)(2,1)} async-done(((bf16[2352,1024]{1,0:T(8,128)(2,1)}), bf16[9408,1024]{1,0:T(8,128)(2,1)}) %all-gather.7.cloned.1.call-update) | async-done | bytes 19267600 | tf_op jit(solution)/shard_map/all_gather | solution.py:137
  233.2 39.5 %all-reduce.22 = (f32[256]{0:T(256)S(1)}, f32[256]{0:T(256)S(1)}) all-reduce(f32[256]{0:T(256)S(1)} %dynamic_update_slice.74, f32[256]{0:T(256)S(1)} %dynamic_update_slice.75), channel_id=1, replica_groups=mesh['dp'=8,'chan'=4] {'dp','chan'}, use_global_device_ids=true, to_apply=%region_7.8 | all-reduce | flops 512 | bytes 4096 | tf_op jit(solution)/shard_map/psum | solution.py:64
  320.1 41.0 %all-reduce.21 = (f32[256]{0:T(256)S(1)}, f32[256]{0:T(256)S(1)}) all-reduce(f32[256]{0:T(256)S(1)} %dynamic_update_slice.76, f32[256]{0:T(256)S(1)} %dynamic_update_slice.77), channel_id=1, replica_groups=mesh['dp'=8,'chan'=4] {'dp','chan'}, use_global_device_ids=true, to_apply=%region_11.12 | all-reduce | flops 512 | bytes 4096 | tf_op jit(solution)/shard_map/psum | solution.py:64
  387.2 265.8 %reduce-scatter.7.cloned.1.call-done = f32[2352,1024]{1,0:T(8,128)} async-done(((f32[9408,1024]{1,0:T(8,128)}), f32[2352,1024]{1,0:T(8,128)}) %reduce-scatter.7.cloned.1.call-update) | async-done | bytes 9633808 | tf_op jit(solution)/shard_map/reduce_scatter | solution.py:153
  658.2 39.7 %all-reduce.20 = (f32[1024]{0:T(1024)S(1)}, f32[1024]{0:T(1024)S(1)}) all-reduce(f32[1024]{0:T(1024)S(1)} %get-tuple-element.155, f32[1024]{0:T(1024)S(1)} %get-tuple-element.154), channel_id=1, replica_groups=mesh['dp'=8,'chan'=4] {'dp','chan'}, use_global_device_ids=true, to_apply=%region_18.19 | all-reduce | flops 2048 | bytes 16384 | tf_op jit(solution)/shard_map/psum | solution.py:64
  709.5 123.0 %all-gather.11.cloned.1.call-done = bf16[9408,1024]{1,0:T(8,128)(2,1)} async-done(((bf16[2352,1024]{1,0:T(8,128)(2,1)}), bf16[9408,1024]{1,0:T(8,128)(2,1)}) %all-gather.11.cloned.1.call-update) | async-done | bytes 19267600 | tf_op jit(solution)/shard_map/all_gather | solution.py:137
  930.9 39.7 %all-reduce.18 = (f32[256]{0:T(256)S(1)}, f32[256]{0:T(256)S(1)}) all-reduce(f32[256]{0:T(256)S(1)} %dynamic_update_slice.80, f32[256]{0:T(256)S(1)} %dynamic_update_slice.81), channel_id=1, replica_groups=mesh['dp'=8,'chan'=4] {'dp','chan'}, use_global_device_ids=true, to_apply=%region_24.25 | all-reduce | flops 512 | bytes 4096 | tf_op jit(solution)/shard_map/psum | solution.py:64
  1017.4 41.0 %all-reduce.17 = (f32[256]{0:T(256)S(1)}, f32[256]{0:T(256)S(1)}) all-reduce(f32[256]{0:T(256)S(1)} %dynamic_update_slice.82, f32[256]{0:T(256)S(1)} %dynamic_update_slice.83), channel_id=1, replica_groups=mesh['dp'=8,'chan'=4] {'dp','chan'}, use_global_device_ids=true, to_apply=%region_28.29 | all-reduce | flops 512 | bytes 4096 | tf_op jit(solution)/shard_map/psum | solution.py:64
  1086.8 266.5 %reduce-scatter.9.cloned.1.call-done = f32[2352,1024]{1,0:T(8,128)} async-done(((f32[9408,1024]{1,0:T(8,128)}), f32[2352,1024]{1,0:T(8,128)}) %reduce-scatter.9.cloned.1.call-update) | async-done | bytes 9633808 | tf_op jit(solution)/shard_map/reduce_scatter | solution.py:153
  1358.4 39.6 %all-reduce.16 = (f32[1024]{0:T(1024)S(1)}, f32[1024]{0:T(1024)S(1)}) all-reduce(f32[1024]{0:T(1024)S(1)} %get-tuple-element.153, f32[1024]{0:T(1024)S(1)} %get-tuple-element.152), channel_id=1, replica_groups=mesh['dp'=8,'chan'=4] {'dp','chan'}, use_global_device_ids=true, to_apply=%region_35.36 | all-reduce | flops 2048 | bytes 16384 | tf_op jit(solution)/shard_map/psum | solution.py:64
  1415.9 41.0 %all-reduce.15 = (f32[1024]{0:T(1024)S(1)}, f32[1024]{0:T(1024)S(1)}) all-reduce(f32[1024]{0:T(1024)S(1)} %get-tuple-element.151, f32[1024]{0:T(1024)S(1)} %get-tuple-element.150), channel_id=1, replica_groups=mesh['dp'=8,'chan'=4] {'dp','chan'}, use_global_device_ids=true, to_apply=%region_39.40 | all-reduce | flops 2048 | bytes 16384 | tf_op jit(solution)/shard_map/psum | solution.py:82
  1481.5 109.8 %all-gather.15.cloned.1.call-done = bf16[9408,1024]{1,0:T(8,128)(2,1)} async-done(((bf16[2352,1024]{1,0:T(8,128)(2,1)}), bf16[9408,1024]{1,0:T(8,128)(2,1)}) %all-gather.15.cloned.1.call-update) | async-done | bytes 19267600 | tf_op jit(solution)/shard_map/all_gather | solution.py:207
  1606.8 39.5 %all-reduce.14 = (f32[256]{0:T(256)S(1)}, f32[256]{0:T(256)S(1)}) all-reduce(f32[256]{0:T(256)S(1)} %dynamic_update_slice.85, f32[256]{0:T(256)S(1)} %dynamic_update_slice.84), channel_id=1, replica_groups=mesh['dp'=8,'chan'=4] {'dp','chan'}, use_global_device_ids=true, to_apply=%region_43.44 | all-reduce | flops 512 | bytes 4096 | tf_op jit(solution)/shard_map/psum | solution.py:82
  1709.4 41.0 %all-reduce.13 = (f32[256]{0:T(256)S(1)}, f32[256]{0:T(256)S(1)}) all-reduce(f32[256]{0:T(256)S(1)} %dynamic_update_slice.87, f32[256]{0:T(256)S(1)} %dynamic_update_slice.86), channel_id=1, replica_groups=mesh['dp'=8,'chan'=4] {'dp','chan'}, use_global_device_ids=true, to_apply=%region_47.48 | all-reduce | flops 512 | bytes 4096 | tf_op jit(solution)/shard_map/psum | solution.py:82
  1761.3 80.0 %reduce-scatter.11.cloned.1.call-done = f32[9408,64]{0,1:T(8,128)} async-done(((f32[9408,256]{0,1:T(8,128)}), f32[9408,64]{0,1:T(8,128)}) %reduce-scatter.11.cloned.1.call-update) | async-done | bytes 2408464 | tf_op jit(solution)/shard_map/reduce_scatter | solution.py:221
  1846.8 39.7 %all-reduce.12 = (f32[256]{0:T(256)S(1)}, f32[256]{0:T(256)S(1)}) all-reduce(f32[256]{0:T(256)S(1)} %dynamic_update_slice.89, f32[256]{0:T(256)S(1)} %dynamic_update_slice.88), channel_id=1, replica_groups=mesh['dp'=8,'chan'=4] {'dp','chan'}, use_global_device_ids=true, to_apply=%region_52.53 | all-reduce | flops 512 | bytes 4096 | tf_op jit(solution)/shard_map/psum | solution.py:82
  1905.6 267.4 %reduce-scatter.13.cloned.1.call-done = f32[2352,1024]{1,0:T(8,128)} async-done(((f32[9408,1024]{1,0:T(8,128)}), f32[2352,1024]{1,0:T(8,128)}) %reduce-scatter.13.cloned.1.call-update) | async-done | bytes 9633808 | tf_op jit(solution)/shard_map/reduce_scatter | solution.py:229
  2193.2 39.4 %all-reduce.11 = (f32[1024]{0:T(1024)S(1)}, f32[1024]{0:T(1024)S(1)}) all-reduce(f32[1024]{0:T(1024)S(1)} %get-tuple-element.149, f32[1024]{0:T(1024)S(1)} %get-tuple-element.148), channel_id=1, replica_groups=mesh['dp'=8,'chan'=4] {'dp','chan'}, use_global_device_ids=true, to_apply=%region_57.58 | all-reduce | flops 2048 | bytes 16384 | tf_op jit(solution)/shard_map/psum | solution.py:82
  2257.6 110.2 %all-gather.17.cloned.1.call-done = bf16[9408,1024]{1,0:T(8,128)(2,1)} async-done(((bf16[2352,1024]{1,0:T(8,128)(2,1)}), bf16[9408,1024]{1,0:T(8,128)(2,1)}) %all-gather.17.cloned.1.call-update) | async-done | bytes 19267600 | tf_op jit(solution)/shard_map/all_gather | solution.py:207
  2383.3 39.5 %all-reduce.10 = (f32[256]{0:T(256)S(1)}, f32[256]{0:T(256)S(1)}) all-reduce(f32[256]{0:T(256)S(1)} %dynamic_update_slice.91, f32[256]{0:T(256)S(1)} %dynamic_update_slice.90), channel_id=1, replica_groups=mesh['dp'=8,'chan'=4] {'dp','chan'}, use_global_device_ids=true, to_apply=%region_61.62 | all-reduce | flops 512 | bytes 4096 | tf_op jit(solution)/shard_map/psum | solution.py:82
  2487.2 41.0 %all-reduce.9 = (f32[256]{0:T(256)S(1)}, f32[256]{0:T(256)S(1)}) all-reduce(f32[256]{0:T(256)S(1)} %dynamic_update_slice.93, f32[256]{0:T(256)S(1)} %dynamic_update_slice.92), channel_id=1, replica_groups=mesh['dp'=8,'chan'=4] {'dp','chan'}, use_global_device_ids=true, to_apply=%region_65.66 | all-reduce | flops 512 | bytes 4096 | tf_op jit(solution)/shard_map/psum | solution.py:82
  2721.8 44.9 %multiply_reduce_fusion.8 = (f32[64]{0:T(128)S(1)}, f32[64]{0:T(128)S(1)}, f32[64]{0:T(128)S(1)}, f32[64]{0:T(128)S(1)}, f32[64]{0:T(128)S(1)}, /*index=5*/f32[6...) fusion(f32[12,28,28,64]{3,2,1,0:T(8,128)} %reshape.616, ...), kind=kLoop, calls=%fused_computation.55 | loop fusion | flops 20470784 | bytes 5222496 | tf_op jit(solution)/shard_map/reduce_sum | solution.py:130
  2802.3 44.5 %multiply_reduce_fusion.34 = (f32[64]{0:T(128)S(1)}, f32[64]{0:T(128)S(1)}, f32[64]{0:T(128)S(1)}, f32[64]{0:T(128)S(1)}, f32[64]{0:T(128)S(1)}, /*index=5*/f32[...) fusion(f32[12,28,28,64]{3,2,1,0:T(8,128)} %reshape.619, ...), kind=kLoop, calls=%fused_computation.81 | loop fusion | flops 20470784 | bytes 5222496 | tf_op jit(solution)/shard_map/reduce_sum | solution.py:130
  2892.8 133.6 %reduce-scatter.17.cloned.1.call-done = f32[2352,1024]{1,0:T(8,128)} async-done(((f32[9408,1024]{1,0:T(8,128)}), f32[2352,1024]{1,0:T(8,128)}) %reduce-scatter.17.cloned.1.call-update) | async-done | bytes 9633808 | tf_op jit(solution)/shard_map/reduce_scatter | solution.py:229
  (513 shorter events, 938.5 us)
Async XLA Ops:
  7.2 127.3 %all-gather.7.cloned.1.call-start = ((), (), s32[]{:S(2)}) async-start(), calls=%async_computation.6 | async-start | bytes 24084480 | tf_op jit(solution)/shard_map/all_gather | solution.py:137
  7.9 221.2 %all-gather.9.cloned.1.call-start = ((), (), s32[]{:S(2)}) async-start(), calls=%async_computation.7 | async-start | bytes 6062080 | tf_op jit(solution)/shard_map/all_gather | solution.py:143
  11.8 178.2 %copy-start.29 = (f32[2,256,64]{1,2,0:T(8,128)S(1)}, f32[2,256,64]{1,2,0:T(8,128)}, u32[]{:S(2)}) copy-start(f32[2,256,64]{1,2,0:T(8,128)} %param.19) | copy-start | bytes 393220
  11.8 178.8 %copy-start.22 = (f32[2,64,1024]{2,1,0:T(8,128)S(1)}, f32[2,64,1024]{2,1,0:T(8,128)}, u32[]{:S(2)}) copy-start(f32[2,64,1024]{2,1,0:T(8,128)} %param.21) | copy-start | bytes 1572868
  189.9 463.1 %reduce-scatter.7.cloned.1.call-start = ((), (), s32[]{:S(2)}) async-start(), calls=%async_computation.8 | async-start | bytes 48168960 | tf_op jit(solution)/shard_map/reduce_scatter | solution.py:153
  386.5 446.0 %all-gather.11.cloned.1.call-start = ((), (), s32[]{:S(2)}) async-start(), calls=%async_computation.9 | async-start | bytes 24084480 | tf_op jit(solution)/shard_map/all_gather | solution.py:137
  387.2 322.2 %copy-start.41 = (f32[1,1,1024]{2,1,0:T(1,128)}, f32[1,1,1024]{2,1,0:T(1,128)S(1)}, u32[]{:S(2)}) copy-start(f32[1,1,1024]{2,1,0:T(1,128)S(1)} %get-tuple-element.324) | copy-start | bytes 12292
  387.2 322.1 %copy-start.43 = (f32[1,1,1024]{2,1,0:T(1,128)}, f32[1,1,1024]{2,1,0:T(1,128)S(1)}, u32[]{:S(2)}) copy-start(f32[1,1,1024]{2,1,0:T(1,128)S(1)} %get-tuple-element.323) | copy-start | bytes 12292
  709.4 217.5 %all-gather.13.cloned.1.call-start = ((), (), s32[]{:S(2)}) async-start(), calls=%async_computation.10 | async-start | bytes 6062080 | tf_op jit(solution)/shard_map/all_gather | solution.py:143
  709.5 261.9 %copy-start.124 = (f32[64]{0:T(128)}, f32[64]{0:T(128)S(1)}, u32[]{:S(2)}) copy-start(f32[64]{0:T(128)S(1)} %get-tuple-element.334) | copy-start | bytes 772
  709.5 217.5 %copy-start.26 = (bf16[2,256,64]{1,2,0:T(8,128)(2,1)S(1)}, bf16[2,256,64]{1,2,0:T(8,128)(2,1)}, u32[]{:S(2)}) copy-start(bf16[2,256,64]{1,2,0:T(8,128)(2,1)} %convert_element_type.166) | copy-start | bytes 196612
  887.8 465.4 %reduce-scatter.9.cloned.1.call-start = ((), (), s32[]{:S(2)}) async-start(), calls=%async_computation.11 | async-start | bytes 48168960 | tf_op jit(solution)/shard_map/reduce_scatter | solution.py:153
  930.4 821.4 %copy-start.8 = (f32[9408,64]{0,1:T(8,128)}, f32[9408,64]{0,1:T(8,128)S(1)}, u32[]{:S(2)}) copy-start(f32[9408,64]{0,1:T(8,128)S(1)} %get-tuple-element.359) | copy-start | bytes 7225348
  1086.7 504.5 %all-gather.15.cloned.1.call-start = ((), (), s32[]{:S(2)}) async-start(), calls=%async_computation.12 | async-start | bytes 24084480 | tf_op jit(solution)/shard_map/all_gather | solution.py:207
  1469.1 372.2 %reduce-scatter.11.cloned.1.call-start = ((), (), s32[]{:S(2)}) async-start(), calls=%async_computation.13 | async-start | bytes 12124160 | tf_op jit(solution)/shard_map/reduce_scatter | solution.py:221
  1761.3 411.8 %reduce-scatter.13.cloned.1.call-start = ((), (), s32[]{:S(2)}) async-start(), calls=%async_computation.14 | async-start | bytes 48168960 | tf_op jit(solution)/shard_map/reduce_scatter | solution.py:229
  1905.5 267.5 %copy-start.38 = (f32[1024]{0:T(1024)S(1)}, f32[1024]{0:T(1024)}, u32[]{:S(2)}) copy-start(f32[1024]{0:T(1024)} %copy-done.37) | copy-start | bytes 12292
  1905.5 267.5 %copy-start.40 = (f32[1024]{0:T(1024)S(1)}, f32[1024]{0:T(1024)}, u32[]{:S(2)}) copy-start(f32[1024]{0:T(1024)} %copy-done.39) | copy-start | bytes 12292
  1905.5 267.5 %copy-start.42 = (f32[1,1,1024]{2,1,0:T(1,128)S(1)}, f32[1,1,1024]{2,1,0:T(1,128)}, u32[]{:S(2)}) copy-start(f32[1,1,1024]{2,1,0:T(1,128)} %copy-done.41) | copy-start | bytes 12292
  1905.5 267.5 %copy-start.44 = (f32[1,1,1024]{2,1,0:T(1,128)S(1)}, f32[1,1,1024]{2,1,0:T(1,128)}, u32[]{:S(2)}) copy-start(f32[1,1,1024]{2,1,0:T(1,128)} %copy-done.43) | copy-start | bytes 12292
  1905.6 462.3 %all-gather.17.cloned.1.call-start = ((), (), s32[]{:S(2)}) async-start(), calls=%async_computation.15 | async-start | bytes 24084480 | tf_op jit(solution)/shard_map/all_gather | solution.py:207
  2244.7 373.7 %reduce-scatter.15.cloned.1.call-start = ((), (), s32[]{:S(2)}) async-start(), calls=%async_computation.16 | async-start | bytes 12124160 | tf_op jit(solution)/shard_map/reduce_scatter | solution.py:221
  2538.4 348.3 %all-reduce.27.cloned.1.call-start = ((), (), s32[]{:S(2)}) async-start(), calls=%async_computation.18 | async-start | bytes 2359296 | tf_op jit(solution)/shard_map/psum | solution.py:309
  2676.4 350.0 %reduce-scatter.17.cloned.1.call-start = ((), (), s32[]{:S(2)}) async-start(), calls=%async_computation.17 | async-start | bytes 48168960 | tf_op jit(solution)/shard_map/reduce_scatter | solution.py:229
  (132 other events, 7037.8 us)
Sparse Core Ops, SparseCore 0:
  9.6 124.8 all-gather.6
  190.0 39.1 all-gather.8
  386.6 266.3 reduce-scatter.6
  709.5 122.9 all-gather.10
  888.0 38.9 all-gather.12
  1086.8 266.3 reduce-scatter.8
  1469.2 122.0 all-gather.14
  1761.4 79.8 reduce-scatter.10
  1905.7 267.2 reduce-scatter.12
  2244.8 122.9 all-gather.16
  2538.5 79.8 reduce-scatter.14
  2676.5 81.4 all-reduce.26
  2760.6 265.6 reduce-scatter.16
where the time goes:
time: 3060 us; the launch traced here: 3050 us
  waiting for transfers between devices  1590 us (52%)
  blocking collectives  676 us (22%)
  other arithmetic  431 us (14%)
  matrix products  194 us (6%)
  local copies, waits for them, and re-layouts  134 us (4%)
    reduce_scatter x2, waiting for transfers between devices, block_forward(): lax.psum_scatter(matmul(act_three, w_expand), 'chan', scatter_dimension=0...  532 us
    reduce_scatter x2, waiting for transfers between devices, block_backward(): lax.psum_scatter(matmul_right(first_low, w_reduce), 'chan', scatter_dimen...  401 us
    psum x8, blocking collectives, norm_backward(): lax.psum((widen(jnp.sum(masked, axis=0), offset, full), widen(jnp.sum(mas...  320 us
    psum x8, blocking collectives, norm_forward(): lax.psum((widen(jnp.sum(field * mask, axis=0), offset, full), widen(jnp.s...  319 us
    all_gather x2, waiting for transfers between devices, block_forward(): inputs_all = lax.all_gather(inputs, 'chan', axis=0, tiled=True)  246 us
    all_gather x2, waiting for transfers between devices, block_backward(): fourth_all = lax.all_gather(fourth_low, 'chan', axis=0, tiled=True)  220 us
    reduce_sum x5, other arithmetic, kernel_grad(): taps.append(jnp.sum(inside * shifted, axis=(0, 1, 2)))  157 us
    reduce_scatter x2, waiting for transfers between devices, block_backward(): lax.psum_scatter(act_one_terms, 'chan', scatter_dimension=1, tiled=True)  115 us
  transfers between devices with their start and end apart: 13, of which 12 were waited for; matrix products, arithmetic and copies ran while one was open for 8% of the time, Pallas kernels for 0%

commit v1 on v0

v1 whole, which is shorter than its diff:
```python
import functools

import jax
import jax.numpy as jnp
from jax import lax
from jax.experimental import pallas as pl
from jax.experimental.pallas import tpu as pltpu
from jax.sharding import PartitionSpec as P

FRAMES = 12
HH = 28
WW = 28
BLOCKS = 2

EPS = 1e-05
LEARN_RATE = 0.001
MOMENTUM = 0.9
DECAY = 0.0001
MESH = pl.DeviceIdType.MESH


def gelu_soft(value):
    return jax.nn.gelu(value, approximate=True)


def gelu_back(value, grad):
    return jax.vjp(gelu_soft, value)[1](grad)[0]


def dot(left, right, over_left, over_right):
    return lax.dot_general(
        left, right, (((over_left,), (over_right,)), ((), ())), preferred_element_type=jnp.float32
    )


def sum_kernel(sizes, x_ref, o_ref, near, far, near_send, near_recv, far_send, far_recv):
    lanes, groups = sizes
    row = lax.axis_index("dp")
    lane = lax.axis_index("chan")
    barrier = pltpu.get_barrier_semaphore()
    near_peers = [(lax.rem(lane + o, lanes)) for o in range(1, lanes)]
    far_peers = [(lax.rem(row + o, groups)) for o in range(1, groups)]
    for peer in near_peers:
        pl.semaphore_signal(barrier, inc=1, device_id=(row, peer), device_id_type=MESH)
    for peer in far_peers:
        pl.semaphore_signal(barrier, inc=1, device_id=(peer, lane), device_id_type=MESH)
    pl.semaphore_wait(barrier, lanes + groups - 2)

    def stage(slots, send, recv, me, peers, place):
        copies = []
        for step, peer in enumerate(peers):
            copy = pltpu.make_async_remote_copy(
                src_ref=slots.at[me],
                dst_ref=slots.at[me],
                send_sem=send.at[step],
                recv_sem=recv.at[me],
                device_id=place(peer),
                device_id_type=MESH,
            )
            copy.start()
            copies.append(copy)
        for step, peer in enumerate(peers):
            pltpu.make_async_remote_copy(
                src_ref=slots.at[peer],
                dst_ref=slots.at[peer],
                send_sem=send.at[step],
                recv_sem=recv.at[peer],
                device_id=place(peer),
                device_id_type=MESH,
            ).wait_recv()
        for copy in copies:
            copy.wait_send()
        total = slots[0]
        for index in range(1, slots.shape[0]):
            total = total + slots[index]
        return total

    near[lane] = x_ref[...]
    far[row] = stage(near, near_send, near_recv, lane, near_peers, lambda p: (row, p))
    o_ref[...] = stage(far, far_send, far_recv, row, far_peers, lambda p: (p, lane))


def all_sum(sizes, rows):
    flat = jnp.concatenate([r.reshape(-1, 128) for r in rows], axis=0)
    pad = -flat.shape[0] % 8
    flat = jnp.pad(flat, ((0, pad), (0, 0)))
    lanes, groups = sizes
    shape = flat.shape
    total = pl.pallas_call(
        functools.partial(sum_kernel, sizes),
        out_shape=jax.ShapeDtypeStruct(shape, jnp.float32),
        in_specs=[pl.BlockSpec(memory_space=pltpu.VMEM)],
        out_specs=pl.BlockSpec(memory_space=pltpu.VMEM),
        scratch_shapes=[
            pltpu.VMEM((lanes,) + shape, jnp.float32),
            pltpu.VMEM((groups,) + shape, jnp.float32),
            pltpu.SemaphoreType.DMA((lanes,)),
            pltpu.SemaphoreType.DMA((lanes,)),
            pltpu.SemaphoreType.DMA((groups,)),
            pltpu.SemaphoreType.DMA((groups,)),
        ],
        compiler_params=pltpu.CompilerParams(collective_id=shape[0], has_side_effects=True),
    )(flat)
    out, at = [], 0
    for r in rows:
        n = r.size // 128
        out.append(total[at : at + n].reshape(r.shape))
        at += n
    return out


def halo(field, lanes):
    before = lax.ppermute(field[-1:], "chan", [(i, i + 1) for i in range(lanes - 1)])
    after = lax.ppermute(field[:1], "chan", [(i + 1, i) for i in range(lanes - 1)])
    return jnp.concatenate([before, field, after], axis=0)


def depthwise(deep, kern, frames):
    padded = jnp.pad(deep, ((0, 0), (1, 1), (1, 1), (0, 0)))
    total = 0.0
    for step in range(3):
        for row in range(3):
            for column in range(3):
                tap = kern[step * 9 + row * 3 + column]
                total = total + tap * padded[step : step + frames, row : row + HH, column : column + WW]
    return total


def kernel_grad(field, deep, frames):
    padded = jnp.pad(deep, ((0, 0), (1, 1), (1, 1), (0, 0)))
    taps = []
    for step in range(3):
        for row in range(3):
            for column in range(3):
                part = padded[2 - step : 2 - step + frames, 2 - row : 2 - row + HH, 2 - column : 2 - column + WW]
                taps.append(jnp.sum(field * part, axis=(0, 1, 2)))
    return jnp.stack(taps)


def descend(weight, moment, grad):
    moment_new = MOMENTUM * moment + grad + DECAY * weight
    return (weight - LEARN_RATE * moment_new, moment_new)


def column_sum(value):
    return jnp.sum(value, axis=0)


def affine_of(totals, squares, count, gain, shift):
    mean = totals / count
    var = squares / count - mean * mean
    scale = lax.rsqrt(var + EPS)
    return (mean, scale, gain * scale, shift - mean * gain * scale)


def shards(
    tokens,
    frame_counts,
    cotangent,
    w_reduce,
    w_mix,
    w_depth,
    w_expand,
    norm_mid,
    norm_out,
    moment_reduce,
    moment_mix,
    moment_depth,
    moment_expand,
    moment_mid,
    moment_out,
):
    row = lax.axis_index("dp")
    lane = lax.axis_index("chan")
    lanes = lax.axis_size("chan")
    sizes = (lanes, lax.axis_size("dp"))
    frames = tokens.shape[0] // (HH * WW)
    narrow = w_reduce.shape[2]
    gather = lambda v, axis: lax.all_gather(v, "chan", axis=axis, tiled=True)
    reduce_all = gather(w_reduce.astype(jnp.bfloat16), 2)
    mix_all = gather(w_mix.astype(jnp.bfloat16), 2)
    expand_all = gather(w_expand.astype(jnp.bfloat16), 1)
    depth_all = gather(w_depth, 2)
    mid_all = gather(norm_mid, 3)
    alive = (lane * frames - 1 + jnp.arange(frames + 2) < frame_counts[0]) & (
        lane * frames - 1 + jnp.arange(frames + 2) >= 0
    )
    alive = alive.astype(jnp.float32)
    mask = jnp.repeat(alive[1:-1], HH * WW)[:, None]
    wide = mix_all.shape[1]
    flat = lambda v: v.reshape(-1, wide)
    deepen = lambda v: v.reshape(-1, HH, WW, wide)

    hidden = tokens
    stored = []
    count = None
    for b in range(BLOCKS):
        mid = mid_all[b]
        first = dot(hidden, reduce_all[b], 1, 0)
        sums = [column_sum(first * mask), column_sum(first * first * mask)]
        if count is None:
            sums.append(jnp.full((128,), jnp.sum(mask)))
            t, q, n = all_sum(sizes, sums)
            count = n[0]
        else:
            t, q = all_sum(sizes, sums)
        mean1, scale1, a1, b1 = affine_of(t, q, count, mid[0, 0], mid[0, 1])
        act1 = (mask * gelu_soft(first * a1 + b1)).astype(jnp.bfloat16)
        second = dot(act1, mix_all[b], 1, 0)
        masked2 = second * mask
        conv = flat(depthwise(halo(deepen(masked2), lanes), depth_all[b], frames))
        ones = jnp.broadcast_to(alive[:, None, None, None], (frames + 2, HH, WW, 1))
        edge = flat(depthwise(ones, depth_all[b], frames))
        t, q, sc, scc, sce, se, see = all_sum(
            sizes,
            [
                column_sum(masked2),
                column_sum(masked2 * masked2),
                column_sum(conv * mask),
                column_sum(conv * conv * mask),
                column_sum(conv * edge * mask),
                column_sum(edge * mask),
                column_sum(edge * edge * mask),
            ],
        )
        mean2, scale2, a2, b2 = affine_of(t, q, count, mid[1, 0], mid[1, 1])
        t3 = a2 * sc + b2 * se
        q3 = a2 * a2 * scc + 2.0 * a2 * b2 * sce + b2 * b2 * see
        mean3, scale3, a3, b3 = affine_of(t3, q3, count, mid[2, 0], mid[2, 1])
        third = a2 * conv + b2 * edge
        norm3 = third * a3 + b3
        act3 = (mask * gelu_soft(norm3)).astype(jnp.bfloat16)
        fourth = dot(act3, expand_all[b], 1, 0)
        t, q = all_sum(sizes, [column_sum(fourth * mask), column_sum(fourth * fourth * mask)])
        mean4, scale4, a4, b4 = affine_of(t, q, count, norm_out[b, 0], norm_out[b, 1])
        pre = mask * (fourth * a4 + b4) + hidden.astype(jnp.float32)
        result = (mask * gelu_soft(pre)).astype(jnp.bfloat16)
        stored.append(
            (hidden, first, act1, second, conv, edge, third, norm3, act3, fourth, pre)
            + ((mean1, scale1, a1, b1), (mean2, scale2, a2, b2), (mean3, scale3, a3, b3), (mean4, scale4, a4, b4))
            + ((sc, scc, sce, se, see),)
        )
        hidden = result

    gradient = cotangent.astype(jnp.float32)
    collected = [None] * BLOCKS
    for b in reversed(range(BLOCKS)):
        (x, first, act1, second, conv, edge, third, norm3, act3, fourth, pre) = stored[b][:11]
        ((mean1, scale1, a1, b1), (mean2, scale2, a2, b2), (mean3, scale3, a3, b3), (mean4, scale4, a4, b4)) = stored[b][11:15]
        sc, scc, sce, se, see = stored[b][15]
        residual = gelu_back(pre, mask * gradient)
        unit4 = (fourth - mean4) * scale4
        shift4, gain4 = all_sum(sizes, [column_sum(residual), column_sum(residual * unit4)])
        fourth_grad = (mask * a4 * (residual - shift4 / count - unit4 * gain4 / count)).astype(jnp.bfloat16)
        grad_expand = dot(act3, fourth_grad, 0, 0)
        e3 = mask * gelu_back(norm3, dot(fourth_grad, expand_all[b], 1, 1))
        e3_sum, e3_conv, e3_edge = all_sum(sizes, [column_sum(e3), column_sum(e3 * conv), column_sum(e3 * edge)])
        shift3 = e3_sum
        gain3 = scale3 * (a2 * e3_conv + b2 * e3_edge - mean3 * e3_sum)
        r = -a3 * scale3 * gain3 / count
        q = -a3 * shift3 / count - r * mean3
        p = a3
        third_conv = a2 * scc + b2 * sce
        third_edge = a2 * sce + b2 * see
        d3_conv = p * e3_conv + q * sc + r * third_conv
        d3_edge = p * e3_edge + q * se + r * third_edge
        shift2 = d3_edge
        gain2 = scale2 * (d3_conv - mean2 * d3_edge)
        third_grad = mask * (p * e3 + q + r * third)
        deep = halo(deepen(third_grad), lanes)
        act2 = mask * (second * a2 + b2)
        grad_depth = kernel_grad(deepen(act2), deep, frames)
        act2_grad = flat(depthwise(deep, depth_all[b][::-1], frames))
        unit2 = (second - mean2) * scale2
        second_grad = (mask * a2 * (act2_grad - shift2 / count - unit2 * gain2 / count)).astype(jnp.bfloat16)
        grad_mix = dot(act1, second_grad, 0, 0)
        e1 = mask * gelu_back(first * a1 + b1, dot(second_grad, mix_all[b], 1, 1))
        unit1 = (first - mean1) * scale1
        shift1, gain1 = all_sum(sizes, [column_sum(e1), column_sum(e1 * unit1)])
        first_grad = (mask * a1 * (e1 - shift1 / count - unit1 * gain1 / count)).astype(jnp.bfloat16)
        grad_reduce = dot(x, first_grad, 0, 0)
        gradient = dot(first_grad, reduce_all[b], 1, 1) + residual
        grad_mid = jnp.stack(
            [jnp.stack([gain1, shift1]), jnp.stack([gain2, shift2]), jnp.stack([gain3, shift3])]
        )
        collected[b] = (grad_reduce, grad_mix, grad_depth, grad_expand, grad_mid, jnp.stack([gain4, shift4]))
    stacked = [jnp.stack([pieces[slot] for pieces in collected]) for slot in range(6)]
    scatter = lambda v, axis: lax.psum_scatter(v, "chan", scatter_dimension=axis, tiled=True)
    grad_reduce, grad_mix, grad_depth, grad_expand = lax.psum(
        (scatter(stacked[0], 2), scatter(stacked[1], 2), scatter(stacked[2], 2), scatter(stacked[3], 1)), "dp"
    )
    grad_mid = lax.dynamic_slice_in_dim(stacked[4], lane * narrow, narrow, 3)
    grad_out = stacked[5]
    grads = (grad_reduce, grad_mix, grad_depth, grad_expand, grad_mid, grad_out)
    params = (w_reduce, w_mix, w_depth, w_expand, norm_mid, norm_out)
    moments = (moment_reduce, moment_mix, moment_depth, moment_expand, moment_mid, moment_out)
    updated = [descend(w, m, g) for w, m, g in zip(params, moments, grads)]
    return (
        (hidden, gradient.astype(jnp.bfloat16)) + grads + tuple(u[0] for u in updated) + tuple(u[1] for u in updated)
    )


def solution(mesh):
    rows = P(("dp", "chan"), None)
    weights = (
        P(None, None, "chan"),
        P(None, None, "chan"),
        P(None, None, "chan"),
        P(None, "chan", None),
        P(None, None, None, "chan"),
        P(),
    )
    return jax.shard_map(
        shards,
        mesh=mesh,
        in_specs=(rows, P("dp"), rows) + weights + weights,
        out_specs=(rows, rows) + weights + weights + weights,
        check_vma=False,
    )
```

time: 3060 us -> 842 us (0.28)
  waiting for transfers between devices: 1590 us -> 54.8 us
  blocking collectives: 676 us -> 59.6 us
  other arithmetic: 431 us -> 262 us
  Pallas kernels: 0 us -> 139 us
  matrix products: 194 us -> 101 us
  local copies, waits for them, and re-layouts: 134 us -> 173 us
    reduce_scatter x6 -> x2, waiting for transfers between devices: 1050 us -> 0.01 us  [shards(): lax.psum_scatter(v, 'chan', scatter_dimension=axis, tiled=True)]
    psum x17 -> x1, blocking collectives: 676 us -> 37.6 us  [shards(): lax.psum((scatter(stacked[0], 2), scatter(stacked[1], 2), scatter(stacked...]
    all_gather x6 -> x2, waiting for transfers between devices: 543 us -> 0.01 us  [shards(): gather = lambda v, axis: lax.all_gather(v, 'chan', axis=axis, tiled=True)]
    reduce_sum x18 -> x10, other arithmetic: 330 us -> 127 us  [the longest x3 65.2 us: column_sum(): return jnp.sum(value, axis=0)]
    pallas_call x0 -> x12, Pallas kernels: none -> 139 us  [all_sum(): pl.pallas_call(functools.partial(sum_kernel, sizes), out_shape=jax.ShapeD...]
    slice x1 -> x25, local copies, waits for them, and re-layouts: 0.01 us -> 94.1 us  [the longest x3 56.6 us: depthwise(): tap = kern[step * 9 + row * 3 + column]]
    dot_general x18, matrix products: 194 us -> 101 us  [dot(): lax.dot_general(left, right, (((over_left,), (over_right,)), ((), ())), p...]
    psum x1, waiting for transfers between devices: 0.01 us -> 45.4 us  [shards(): lax.psum((scatter(stacked[0], 2), scatter(stacked[1], 2), scatter(stacked...]
  transfers between devices with their start and end apart: 13 -> 15, of which waited for: 12 -> 2; matrix products, arithmetic and copies ran while one was open for 8% -> 31% of each run, Pallas kernels for 0% -> 3%
where the time goes in v1:
time: 842 us; the launch traced here: 831 us
  other arithmetic  262 us (31%)
  local copies, waits for them, and re-layouts  173 us (21%)
  Pallas kernels  139 us (17%)
  matrix products  101 us (12%)
  blocking collectives  59.6 us (7%)
  waiting for transfers between devices  54.8 us (7%)
  starting transfers between devices  20.7 us (2%)
  between operations  20.5 us (2%)
    pallas_call x12, Pallas kernels, all_sum(): pl.pallas_call(functools.partial(sum_kernel, sizes), out_shape=jax.ShapeD...  139 us
    dot_general x18, matrix products, dot(): lax.dot_general(left, right, (((over_left,), (over_right,)), ((), ())), p...  101 us
    reduce_sum x3, other arithmetic, column_sum(): return jnp.sum(value, axis=0)  65.2 us
    reduce_sum x6, other arithmetic, kernel_grad(): taps.append(jnp.sum(field * part, axis=(0, 1, 2)))  61.5 us
    slice x3, local copies, waits for them, and re-layouts, depthwise(): tap = kern[step * 9 + row * 3 + column]  56.6 us
    psum x1, waiting for transfers between devices, shards(): lax.psum((scatter(stacked[0], 2), scatter(stacked[1], 2), scatter(stacked...  45.4 us
    psum x1, blocking collectives, shards(): lax.psum((scatter(stacked[0], 2), scatter(stacked[1], 2), scatter(stacked...  37.6 us
    all_gather x3, blocking collectives, shards(): gather = lambda v, axis: lax.all_gather(v, 'chan', axis=axis, tiled=True)  22 us
  transfers between devices with their start and end apart: 15, of which 2 were waited for; matrix products, arithmetic and copies ran while one was open for 31% of the time, Pallas kernels for 3%

profile of v1, /device:TPU:0, one launch (start us, length us, event | category | flops | bytes accessed | tf_op | source)
XLA Modules:
  0.0 831.0 jit_solution(4724780546760813803)
XLA Ops:
  39.4 11.0 %slice_reduce_fusion.1 = (f32[256]{0:T(256)}, f32[256]{0:T(256)}, f32[256]{0:T(256)}, f32[256]{0:T(256)}, f32[256]{0:T(256)}, /*index=5*/f32[256]{0:T(256)}, f32...) fusion(f32[3,2,256]{0,1,2:T(2,128)S(1)} %get-tuple-element.397, ...), kind=kLoop, calls=%fused_computation.382 | loop fusion | bytes 24576 | tf_op jit(solution)/shard_map/slice | solution.py:229
  50.4 16.1 %slice_reduce_fusion.61 = (f32[256]{0:T(256)S(1)}, f32[256]{0:T(256)S(1)}, f32[256]{0:T(256)S(1)}, f32[256]{0:T(256)S(1)}, f32[256]{0:T(256)S(1)}, /*index=5*/f3...) fusion(f32[2,27,256]{1,0,2:T(2,128)S(1)} %all_gather.18), kind=kLoop, calls=%fused_computation.443 | loop fusion | bytes 32768 | tf_op jit(solution)/shard_map/slice | solution.py:124
  66.7 20.3 %slice_reduce_fusion.28 = (f32[256]{0:T(256)S(1)}, f32[256]{0:T(256)S(1)}, f32[256]{0:T(256)}, f32[256]{0:T(256)}, f32[256]{0:T(256)}, /*index=5*/f32[256]{0:T(2...) fusion(f32[2,27,256]{1,0,2:T(2,128)S(1)} %all_gather.18), kind=kLoop, calls=%fused_computation.409 | loop fusion | bytes 38912 | tf_op jit(solution)/shard_map/slice | solution.py:124
  87.1 20.2 %slice_reduce_fusion.29 = (f32[256]{0:T(256)}, f32[256]{0:T(256)}, f32[256]{0:T(256)}, f32[256]{0:T(256)}, f32[256]{0:T(256)}, /*index=5*/f32[256]{0:T(256)}, f3...) fusion(f32[2,27,256]{1,0,2:T(2,128)S(1)} %all_gather.18), kind=kLoop, calls=%fused_computation.410 | loop fusion | bytes 38912 | tf_op jit(solution)/shard_map/slice | solution.py:124
  107.3 17.9 %multiply_reduce_fusion.72 = (f32[256]{0:T(256)}, f32[256]{0:T(256)}, f32[256]{0:T(256)}, f32[256]{0:T(256)}, f32[256]{0:T(256)S(1)}, /*index=5*/f32[256]{0:T(25...) fusion(f32[2352]{0:T(1024)S(1)} %mul.5234, f32[2352]{0:T(1024)S(1)} %mul.5526, ...), kind=kOutput, calls=%fused_computation.300 | convolution fusion | flops 1305979392 | bytes 12891392 | tf_op jit(solution)/shard_map/dot_general | solution.py:31
  126.2 11.3 %shard_map.302 = f32[8,128]{1,0:T(8,128)} custom-call(f32[8,128]{1,0:T(8,128)} %pad.48.x_ref), custom_call_target="tpu_custom_call" | custom-call | tf_op jit(solution)/shard_map/pallas_call | solution.py:89
  165.7 24.9 %multiply_reduce_fusion.61 = (f32[256]{0:T(256)}, f32[256]{0:T(256)}, f32[256]{0:T(256)}, f32[3,28,28,256]{3,2,1,0:T(8,128)S(1)}, f32[3,28,28,256]{3,2,1,0:T(8,128)}) fusion(f32[3]{0:T(128)S(1)} %slice.1302, f32[5,30,30,256]{3,2,1,0:T(8,128)S(1)} %select_maximum_fusion.6, f32[256]{0:T(256)S(1)} %copy-done.208, f32[256]{0:T(256)S(1)} %copy-done.211, ...), kind=kLoop, calls=%fused_computation.244 | loop fusion | flops 69844224 | bytes 66890288 | tf_op jit(solution)/shard_map/reduce_sum | solution.py:146
  192.7 13.7 %shard_map.303 = f32[16,128]{1,0:T(8,128)} custom-call(f32[16,128]{1,0:T(8,128)} %pad.51.x_ref), custom_call_target="tpu_custom_call" | custom-call | tf_op jit(solution)/shard_map/pallas_call | solution.py:89
  246.3 10.8 %shard_map.305 = f32[8,128]{1,0:T(8,128)} custom-call(f32[8,128]{1,0:T(8,128)} %select_maximum_fusion.14.x_ref), custom_call_target="tpu_custom_call" | custom-call | tf_op jit(solution)/shard_map/pallas_call | solution.py:89
  283.4 23.2 %multiply_reduce_fusion.58 = (f32[256]{0:T(256)S(1)}, f32[256]{0:T(256)S(1)}, f32[256]{0:T(256)S(1)}, f32[3,28,28,256]{3,2,1,0:T(8,128)S(1)}, f32[3,28,28,256]{3,2,1,0:T(8,128)}) fusion(f32[3]{0:T(128)S(1)} %copy-done.157, f32[5,30,30,256]{3,2,1,0:T(8,128)S(1)} %select_maximum_fusion.4, f32[256]{0:T(256)} %get-tuple-element.247, f32[256]{0:T(256)} %get-tuple-element.248, ...), kind=kLoop, calls=%fused_computation.240 | loop fusion | flops 69844224 | bytes 66890288 | tf_op jit(solution)/shard_map/reduce_sum | solution.py:146
  307.4 17.7 %shard_map.306 = f32[16,128]{1,0:T(8,128)} custom-call(f32[16,128]{1,0:T(8,128)} %pad.54.x_ref), custom_call_target="tpu_custom_call" | custom-call | tf_op jit(solution)/shard_map/pallas_call | solution.py:89
  342.0 10.9 %shard_map.307 = f32[16,128]{1,0:T(8,128)} custom-call(f32[16,128]{1,0:T(8,128)} %pad_maximum_fusion.14.x_ref), custom_call_target="tpu_custom_call" | custom-call | tf_op jit(solution)/shard_map/pallas_call | solution.py:89
  354.2 17.1 %fusion.229 = (f32[1024]{0:T(1024)S(1)}, f32[1024]{0:T(1024)S(1)}, f32[2352,1024]{1,0:T(8,128)}, bf16[2352,1024]{1,0:T(8,128)(2,1)}) fusion(f32[1024]{0:T(1024)S(1)} %get-tuple-element.353, f32[2352,1024]{1,0:T(8,128)} %get-tuple-element.491, f32[1024]{0:T(1024)S(1)} %get-tuple-element.354, bf16[2352,1024]{1,0:T(8,128)(2,1)} %copy-done.9, ...), kind=kLoop, calls=%fused_computation.677 | loop fusion | flops 81885184 | bytes 33752256 | tf_op jit(solution)/shard_map/reduce_sum | solution.py:146
  371.9 11.0 %shard_map.308 = f32[16,128]{1,0:T(8,128)} custom-call(f32[16,128]{1,0:T(8,128)} %pad_maximum_fusion.15.x_ref), custom_call_target="tpu_custom_call" | custom-call | tf_op jit(solution)/shard_map/pallas_call | solution.py:89
  402.7 10.9 %shard_map.309 = f32[8,128]{1,0:T(8,128)} custom-call(f32[8,128]{1,0:T(8,128)} %select_maximum_fusion.12.x_ref), custom_call_target="tpu_custom_call" | custom-call | tf_op jit(solution)/shard_map/pallas_call | solution.py:89
  455.1 10.4 %multiply_add_fusion.1 = f32[3,28,28,256]{3,2,1,0:T(8,128)} fusion(f32[3,28,28,256]{3,2,1,0:T(8,128)S(1)} %reshape.3638, f32[5,30,30,256]{3,2,1,0:T(8,128)S(1)} %select_maximum_fusion.2, f32[1,28,28,256]{3,2,1,0:T(8,128)S(1)} %copy.191, f32[1,28,28,256]{3,2,1,0:T(8,128)S(1)} %copy.192, f32[256]{0:T(256)} %get-tuple-element.247, f32[256]{0:T(256)} %get-tuple-element.248, ...), kind=kLoop, calls=%fused_computation.239 | loop fusion | flops 33116160 | bytes 64252928 | tf_op jit(solution)/shard_map/add | solution.py:125
  493.5 16.7 %fusion.228 = (f32[1024]{0:T(1024)S(1)}, f32[1024]{0:T(1024)S(1)}, f32[2352,1024]{1,0:T(8,128)}) fusion(f32[1024]{0:T(1024)S(1)} %copy-done.130, f32[2352,1024]{1,0:T(8,128)} %get-tuple-element.488, f32[1024]{0:T(1024)S(1)} %copy-done.132, bf16[2352,1024]{1,0:T(8,128)(2,1)} %param.15, f32[1024]{0:T(1024)S(1)} %copy-done.144, f32[1024]{0:T(1024)S(1)} %copy-done.128, ...), kind=kOutput, calls=%fused_computation.676 | convolution fusion | flops 1307785216 | bytes 35483648 | tf_op jit(solution)/shard_map/dot_general | solution.py:31
  510.8 11.0 %shard_map.311 = f32[16,128]{1,0:T(8,128)} custom-call(f32[16,128]{1,0:T(8,128)} %pad_maximum_fusion.16.x_ref), custom_call_target="tpu_custom_call" | custom-call | tf_op jit(solution)/shard_map/pallas_call | solution.py:89
  539.2 10.6 %shard_map.312 = f32[8,128]{1,0:T(8,128)} custom-call(f32[8,128]{1,0:T(8,128)} %select_maximum_fusion.9.x_ref), custom_call_target="tpu_custom_call" | custom-call | tf_op jit(solution)/shard_map/pallas_call | solution.py:89
  617.8 24.2 %multiply_reduce_fusion.6 = (f32[256]{0:T(256)S(1)}, f32[256]{0:T(256)}, f32[256]{0:T(256)}, f32[256]{0:T(256)}, f32[256]{0:T(256)}, /*index=5*/f32[256]{0:T(256...) fusion(f32[3,28,28,256]{3,2,1,0:T(8,128)S(1)} %copy-done.6, ...), kind=kLoop, calls=%fused_computation.186 | loop fusion | flops 21671424 | bytes 45778944 | tf_op jit(solution)/shard_map/reduce_sum | solution.py:136
  646.4 11.0 %shard_map.313 = f32[8,128]{1,0:T(8,128)} custom-call(f32[8,128]{1,0:T(8,128)} %select_maximum_fusion.8.x_ref), custom_call_target="tpu_custom_call" | custom-call | tf_op jit(solution)/shard_map/pallas_call | solution.py:89
  692.8 11.2 %multiply_reduce_fusion.36 = (f32[256]{0:T(256)}, f32[256]{0:T(256)}, f32[256]{0:T(256)}, f32[256]{0:T(256)}, f32[256]{0:T(256)}, /*index=5*/f32[256]{0:T(256)}, f32[256]{0:T(256)}, f32[256]{0:T(256)}) fusion(f32[3,28,28,256]{3,2,1,0:T(8,128)} %reshape.3655, f32[3,28,28,256]{3,2,1,0:T(8,128)S(1)} %copy-done.3, f32[1,28,28,256]{3,2,1,0:T(8,128)} %copy-done.17, ...), kind=kLoop, calls=%fused_computation.216 | loop fusion | flops 10835968 | bytes 20881408 | tf_op jit(solution)/shard_map/reduce_sum | solution.py:136
  731.8 37.6 %psum.30 = f32[2,27,64]{2,1,0:T(8,128)S(1)} all-reduce(f32[2,27,64]{2,1,0:T(8,128)S(1)} %copy.212), channel_id=1, replica_groups=mesh['dp'=8,'chan'=4] {'dp'}, use_global_device_ids=true, to_apply=%region_96.97 | all-reduce | flops 3456 | bytes 27648 | tf_op jit(solution)/shard_map/psum | solution.py:289
  771.3 45.4 %all-reduce.20.cloned.1.call-done = (f32[2,1024,64]{1,2,0:T(8,128)}, f32[2,256,64]{1,2,0:T(8,128)}, f32[2,64,1024]{2,1,0:T(8,128)}) async-done(((f32[2,1024,64]{1,2,0:T(8,128)}, f32[2,256,64]{1,2,0:T(8,128)}, f32[2,64,1024]{2,1,0:T(8,128)}), (f32[2,1024,64]{1,2,0:T(8,128)}, f32[2,256,64]{1,2,0:T(8,128)}, f32[2,64,1024]{2,1,0:T(8,128)})) %all-reduce.20.cloned.1.call-update) | async-done | bytes 1179664 | tf_op jit(solution)/shard_map/psum | solution.py:289
  (901 shorter events, 395.4 us)
Async XLA Ops:
  7.2 100.0 %all-gather.3.cloned.1.call-start = ((), (), s32[]{:S(2)}) async-start(), calls=%async_computation.3 | async-start | bytes 1310720 | tf_op jit(solution)/shard_map/all_gather | solution.py:179
  9.1 207.7 %all-gather.5.cloned.1.call-start = ((), (), s32[]{:S(2)}) async-start(), calls=%async_computation.4 | async-start | bytes 1310720 | tf_op jit(solution)/shard_map/all_gather | solution.py:179
  9.9 199.4 %copy-start.156 = (f32[3]{0:T(128)}, f32[3]{0:T(128)S(1)}, u32[]{:S(2)}) copy-start(f32[3]{0:T(128)S(1)} %slice.1302) | copy-start | bytes 40
  10.4 154.8 %copy-start.59 = (f32[3,28,28]{2,1,0:T(8,128)}, f32[3,28,28]{2,1,0:T(8,128)S(1)}, u32[]{:S(2)}) copy-start(f32[3,28,28]{2,1,0:T(8,128)S(1)} %get-tuple-element.418) | copy-start | bytes 28228
  10.4 154.8 %copy-start.61 = (f32[3,28,28]{2,1,0:T(8,128)}, f32[3,28,28]{2,1,0:T(8,128)S(1)}, u32[]{:S(2)}) copy-start(f32[3,28,28]{2,1,0:T(8,128)S(1)} %get-tuple-element.419) | copy-start | bytes 28228
  10.4 154.8 %copy-start.63 = (f32[3,28,28]{2,1,0:T(8,128)}, f32[3,28,28]{2,1,0:T(8,128)S(1)}, u32[]{:S(2)}) copy-start(f32[3,28,28]{2,1,0:T(8,128)S(1)} %get-tuple-element.420) | copy-start | bytes 28228
  10.4 154.8 %copy-start.65 = (f32[3,28,28]{2,1,0:T(8,128)}, f32[3,28,28]{2,1,0:T(8,128)S(1)}, u32[]{:S(2)}) copy-start(f32[3,28,28]{2,1,0:T(8,128)S(1)} %get-tuple-element.421) | copy-start | bytes 28228
  10.4 154.8 %copy-start.67 = (f32[3,28,28]{2,1,0:T(8,128)}, f32[3,28,28]{2,1,0:T(8,128)S(1)}, u32[]{:S(2)}) copy-start(f32[3,28,28]{2,1,0:T(8,128)S(1)} %get-tuple-element.422) | copy-start | bytes 28228
  27.8 232.6 %copy-start.49 = (bf16[2,256,256]{1,2,0:T(8,128)(2,1)}, bf16[2,256,256]{1,2,0:T(8,128)(2,1)S(1)}, u32[]{:S(2)}) copy-start(bf16[2,256,256]{1,2,0:T(8,128)(2,1)S(1)} %all_gather.17) | copy-start | bytes 786436
  27.9 232.5 %copy-start.37 = (f32[2352]{0:T(1024)}, f32[2352]{0:T(1024)S(1)}, u32[]{:S(2)}) copy-start(f32[2352]{0:T(1024)S(1)} %mul.5234) | copy-start | bytes 28228
  50.4 158.8 %copy-start.145 = (f32[256]{0:T(256)}, f32[256]{0:T(256)S(1)}, u32[]{:S(2)}) copy-start(f32[256]{0:T(256)S(1)} %get-tuple-element.502) | copy-start | bytes 3076
  147.3 13.3 %collective-permute-start.1 = (f32[1,28,28,256]{3,0,2,1:T(1,128)}, f32[1,28,28,256]{3,0,2,1:T(1,128)}, u32[]{:S(2)}, u32[]{:S(2)}) collective-permute-start(f32[1,28,28,256]{3,0,2,1:T(1,128)} %slice.1569), channel_id=1, source_target_pairs={{1,0},{2,1},{3,2},{5,4},{6,5},{7,6},{9,8},{10,9},{11,10},{13,12},{... | collective-permute-start | bytes 2408456 | tf_op jit(solution)/shard_map/ppermute | solution.py:114
  150.4 12.2 %collective-permute-start = (f32[1,28,28,256]{3,0,2,1:T(1,128)}, f32[1,28,28,256]{3,0,2,1:T(1,128)}, u32[]{:S(2)}, u32[]{:S(2)}) collective-permute-start(f32[1,28,28,256]{3,0,2,1:T(1,128)} %slice.1568), channel_id=1, source_target_pairs={{0,1},{1,2},{2,3},{4,5},{5,6},{6,7},{8,9},{9,10},{10,11},{12,13},{... | collective-permute-start | bytes 2408456 | tf_op jit(solution)/shard_map/ppermute | solution.py:113
  155.1 556.4 %all-reduce.18.cloned.1.call-start = ((), (), s32[]{:S(2)}) async-start(), calls=%async_computation.8 | async-start | bytes 1048576
  273.1 8.5 %collective-permute-start.3 = (f32[1,28,28,256]{3,0,2,1:T(1,128)}, f32[1,28,28,256]{3,0,2,1:T(1,128)S(1)}, u32[]{:S(2)}, u32[]{:S(2)}) collective-permute-start(f32[1,28,28,256]{3,0,2,1:T(1,128)} %slice.1571), channel_id=1, source_target_pairs={{1,0},{2,1},{3,2},{5,4},{6,5},{7,6},{9,8},{10,9},{11,10},{13,12},{... | collective-permute-start | bytes 2408456 | tf_op jit(solution)/shard_map/ppermute | solution.py:114
  274.4 7.4 collective-permute-start.2
  431.0 17.9 %collective-permute-start.5 = (f32[1,28,28,256]{3,0,2,1:T(1,128)}, f32[1,28,28,256]{3,0,2,1:T(1,128)}, u32[]{:S(2)}, u32[]{:S(2)}) collective-permute-start(f32[1,28,28,256]{3,0,2,1:T(1,128)} %slice.1573), channel_id=1, source_target_pairs={{1,0},{2,1},{3,2},{5,4},{6,5},{7,6},{9,8},{10,9},{11,10},{13,12},{... | collective-permute-start | bytes 2408456 | tf_op jit(solution)/shard_map/ppermute | solution.py:114
  432.3 17.9 %collective-permute-start.4 = (f32[1,28,28,256]{3,0,2,1:T(1,128)}, f32[1,28,28,256]{3,0,2,1:T(1,128)}, u32[]{:S(2)}, u32[]{:S(2)}) collective-permute-start(f32[1,28,28,256]{3,0,2,1:T(1,128)} %slice.1572), channel_id=1, source_target_pairs={{0,1},{1,2},{2,3},{4,5},{5,6},{6,7},{8,9},{9,10},{10,11},{12,13},{... | collective-permute-start | bytes 2408456 | tf_op jit(solution)/shard_map/ppermute | solution.py:113
  564.2 15.7 %collective-permute-start.7 = (f32[1,28,28,256]{3,0,2,1:T(1,128)}, f32[1,28,28,256]{3,0,2,1:T(1,128)}, u32[]{:S(2)}, u32[]{:S(2)}) collective-permute-start(f32[1,28,28,256]{3,0,2,1:T(1,128)} %slice.1575), channel_id=1, source_target_pairs={{1,0},{2,1},{3,2},{5,4},{6,5},{7,6},{9,8},{10,9},{11,10},{13,12},{... | collective-permute-start | bytes 2408456 | tf_op jit(solution)/shard_map/ppermute | solution.py:114
  565.5 15.7 %collective-permute-start.6 = (f32[1,28,28,256]{3,0,2,1:T(1,128)}, f32[1,28,28,256]{3,0,2,1:T(1,128)}, u32[]{:S(2)}, u32[]{:S(2)}) collective-permute-start(f32[1,28,28,256]{3,0,2,1:T(1,128)} %slice.1574), channel_id=1, source_target_pairs={{0,1},{1,2},{2,3},{4,5},{5,6},{6,7},{8,9},{9,10},{10,11},{12,13},{... | collective-permute-start | bytes 2408456 | tf_op jit(solution)/shard_map/ppermute | solution.py:113
  605.6 107.5 %reduce-scatter.8.cloned.1.call-start = ((), (), s32[]{:S(2)}) async-start(), calls=%async_computation.6 | async-start | bytes 2621440 | tf_op jit(solution)/shard_map/reduce_scatter | solution.py:288
  612.3 100.8 %reduce-scatter.6.cloned.1.call-start = ((), (), s32[]{:S(2)}) async-start(), calls=%async_computation.5 | async-start | bytes 2621440 | tf_op jit(solution)/shard_map/reduce_scatter | solution.py:288
  668.8 62.0 %reduce-scatter.10.cloned.1.call-start = ((), (), s32[]{:S(2)}) async-start(), calls=%async_computation.7 | async-start | bytes 163840
  711.4 105.3 %all-reduce.20.cloned.1.call-start = ((), (), s32[]{:S(2)}) async-start(), calls=%async_computation.9 | async-start | bytes 2359296 | tf_op jit(solution)/shard_map/psum | solution.py:289
  (321 other events, 4595.0 us)
Sparse Core Ops, SparseCore 0:
  10.2 20.8 all-gather.2
  155.2 16.8 all-gather.4
  605.7 33.2 all-reduce.17
  641.4 31.4 reduce-scatter.7
  675.3 31.4 reduce-scatter.5
  711.5 19.2 reduce-scatter.9
  735.6 80.9 all-reduce.19

commit v2 on v1

--- a/solution.py
+++ b/solution.py
@@ -10,13 +10,590 @@
 FRAMES = 12
 HH = 28
 WW = 28
+WP = 32
+KVOL = 27
 BLOCKS = 2
+GROUP = 4
+QUADS = HH // GROUP
+FLAT = GROUP * WW
+WIDE = GROUP * WP
 
 EPS = 1e-05
 LEARN_RATE = 0.001
 MOMENTUM = 0.9
 DECAY = 0.0001
 MESH = pl.DeviceIdType.MESH
+F32 = jnp.float32
+BF16 = jnp.bfloat16
+ROOT = 0.7978845608028654
+CUBE = 0.044715
+
+
+def gelu_fwd(v):
+    t = jnp.tanh(v * (ROOT + (ROOT * CUBE) * (v * v)))
+    h = 0.5 * v
+    return h * t + h
+
+
+def gelu_slope(v):
+    s = v * v
+    t = jnp.tanh(v * (ROOT + (ROOT * CUBE) * s))
+    return 0.5 * (1.0 + t) + (0.5 * v) * (1.0 - t * t) * (ROOT + (3.0 * ROOT * CUBE) * s)
+
+
+def dot(left, right):
+    return jnp.dot(left, right, preferred_element_type=F32)
+
+
+def fold(v):
+    return jnp.sum(v.reshape(v.shape[0] // 8, 8, v.shape[1]), axis=0)
+
+
+def spread(v):
+    gap = jnp.zeros((WP - WW, v.shape[1]), v.dtype)
+    parts = []
+    for h in range(GROUP):
+        parts += [v[WW * h : WW * (h + 1)], gap]
+    return jnp.concatenate(parts, axis=0)
+
+
+def squeeze(v):
+    return jnp.concatenate([v[WP * h : WP * h + WW] for h in range(GROUP)], axis=0)
+
+
+def rows_of(*vectors):
+    parts = []
+    for v in vectors:
+        parts += [v[:, 256 * i : 256 * (i + 1)] for i in range(v.shape[1] // 256)]
+    if len(parts) < 8:
+        parts.append(jnp.zeros((8 - len(parts), 256), F32))
+    return jnp.concatenate(parts, axis=0)
+
+
+def flat_sum(v):
+    return jnp.sum(v, axis=0, keepdims=True)
+
+
+def wide_row(v, first):
+    return jnp.concatenate([v[first + i : first + i + 1] for i in range(4)], axis=1)
+
+
+class Net:
+    def __init__(self, groups, lanes):
+        self.groups, self.lanes = groups, lanes
+        self.row = lax.axis_index("dp")
+        self.lane = lax.axis_index("chan")
+        self.core = lax.rem(self.lane, 2)
+        self.side = lax.div(self.lane, 2)
+        self.half = lanes // 2
+
+    def near(self):
+        return [(1 - self.core, (self.row, self.side * 2 + 1 - self.core))]
+
+    def far(self):
+        out = []
+        for o in range(self.groups):
+            for p in range(self.half):
+                if o or p:
+                    row = lax.rem(self.row + o, self.groups)
+                    side = lax.rem(self.side + p, self.half)
+                    out.append((row * self.half + side, (row, side * 2 + self.core)))
+        return out
+
+    def far_slot(self):
+        return self.row * self.half + self.side
+
+    def chan_peers(self):
+        return [
+            (lax.rem(self.lane + o, self.lanes), (self.row, lax.rem(self.lane + o, self.lanes)))
+            for o in range(1, self.lanes)
+        ]
+
+
+def push(src, dst, send, recv, device):
+    copy = pltpu.make_async_remote_copy(
+        src_ref=src, dst_ref=dst, send_sem=send, recv_sem=recv, device_id=device, device_id_type=MESH
+    )
+    return copy
+
+
+def forward_kernel(
+    groups,
+    lanes,
+    counts,
+    tokens,
+    reduce_loc,
+    mix_loc,
+    expand_loc,
+    small_loc,
+    norm_out,
+    out_hbm,
+    x1_hbm,
+    z1_out,
+    z2_out,
+    c_out,
+    sums_out,
+    x0,
+    x1,
+    red_t,
+    red,
+    mix_t,
+    mix,
+    exp,
+    small,
+    z1,
+    a1s,
+    z2,
+    conv,
+    a3s,
+    edge,
+    halo_send,
+    halo_recv,
+    near,
+    far,
+    near_send,
+    near_recv,
+    far_send,
+    far_recv,
+    gather_send,
+    gather_recv,
+    halo_ssem,
+    halo_rsem,
+    load_sem,
+    store_sem,
+):
+    net = Net(groups, lanes)
+    lane = net.lane
+    frames = tokens.shape[0] // (HH * WW)
+    frame_rows = HH * WW
+    count_here = counts[0]
+
+    def live(frame):
+        position = lane * frames + frame
+        return jnp.where((position >= 0) & (position < count_here), 1.0, 0.0)
+
+    loads = []
+    for f in range(frames):
+        rows = pl.ds(f * frame_rows, frame_rows)
+        copy = pltpu.make_async_copy(tokens.at[rows], x0.at[rows], load_sem.at[f])
+        copy.start()
+        loads.append(copy)
+
+    barrier = pltpu.get_barrier_semaphore()
+    friends = [d for _, d in net.near()] + [d for _, d in net.far()] + [d for _, d in net.chan_peers()]
+    for device in friends:
+        pl.semaphore_signal(barrier, inc=1, device_id=device, device_id_type=MESH)
+    pl.semaphore_wait(barrier, len(friends))
+
+    own = net.lane
+    share = red_t.shape[1] // lanes
+    late = []
+
+    def gather(slot, src, dst_of):
+        for step, (_, device) in enumerate(net.chan_peers()):
+            copy = push(src, dst_of(own), gather_send.at[slot, step], gather_recv.at[slot, own], device)
+            copy.start()
+            late.append(copy)
+        dst_of(own)[...] = src[...]
+
+    def gather_wait(slot, src, dst_of):
+        for step, (peer, device) in enumerate(net.chan_peers()):
+            push(src, dst_of(peer), gather_send.at[slot, step], gather_recv.at[slot, peer], device).wait_recv()
+
+    def block_rows(ref, b):
+        return lambda who: ref.at[b, pl.ds(pl.multiple_of(who * share, share), share)]
+
+    plan = {
+        ("red", 0): (0, reduce_loc.at[0], block_rows(red_t, 0)),
+        ("mix", 0): (1, mix_loc.at[0], block_rows(mix_t, 0)),
+        ("small", 0): (2, small_loc, lambda who: small.at[who]),
+        ("exp", 0): (3, expand_loc.at[0], block_rows(exp, 0)),
+        ("red", 1): (4, reduce_loc.at[1], block_rows(red_t, 1)),
+        ("mix", 1): (5, mix_loc.at[1], block_rows(mix_t, 1)),
+        ("exp", 1): (6, expand_loc.at[1], block_rows(exp, 1)),
+    }
+    for slot, src, dst_of in plan.values():
+        gather(slot, src, dst_of)
+
+    def total_start(i, value):
+        near[i, net.core] = value
+        for who, device in net.near():
+            copy = push(
+                near.at[i, net.core], near.at[i, net.core], near_send.at[i], near_recv.at[i], device
+            )
+            copy.start()
+            late.append(copy)
+            copy.wait_recv()
+        far[i, net.far_slot()] = near[i, 0] + near[i, 1]
+        for step, (who, device) in enumerate(net.far()):
+            copy = push(
+                far.at[i, net.far_slot()],
+                far.at[i, net.far_slot()],
+                far_send.at[i, step],
+                far_recv.at[i, net.far_slot()],
+                device,
+            )
+            copy.start()
+            late.append(copy)
+
+    def total_finish(i):
+        for step, (who, device) in enumerate(net.far()):
+            push(
+                far.at[i, who], far.at[i, who], far_send.at[i, step], far_recv.at[i, who], device
+            ).wait_recv()
+        total = far[i, 0]
+        for j in range(1, groups * net.half):
+            total = total + far[i, j]
+        return total
+
+    column = lax.broadcasted_iota(jnp.int32, (WIDE, 256), 0) % WP
+    pad_mask = (column < WW).astype(F32)
+
+    def affine(total, square, count, gain, shift):
+        mean = total / count
+        var = square / count - mean * mean
+        scale = lax.rsqrt(var + EPS)
+        return mean, scale, gain * scale, shift - mean * (gain * scale)
+
+    def zero8(n=256):
+        return jnp.zeros((8, n), F32)
+
+    for ref in (z2,):
+        for b in range(BLOCKS):
+            for f in range(frames + 2):
+                ref[b, f, 0] = jnp.zeros((WP, 256), F32)
+                ref[b, f, HH + 1] = jnp.zeros((WP, 256), F32)
+
+    gather_wait(*plan["red", 0])
+    red[0] = red_t[0].T
+
+    carry = (zero8(), zero8())
+    for f in range(frames):
+        loads[f].wait()
+        alive = live(f)
+
+        def project(j, carry):
+            q = f * QUADS + j
+            x = x0[pl.ds(pl.multiple_of(q * FLAT, FLAT), FLAT)]
+            z = dot(x, red[0])
+            z1[0, pl.ds(q * GROUP, GROUP)] = spread(z).reshape(GROUP, WP, 256)
+            z = z * alive
+            return (carry[0] + fold(z), carry[1] + fold(z * z))
+
+        carry = lax.fori_loop(0, QUADS, project, carry)
+
+    gather_wait(*plan["small", 0])
+    taps = small[0]
+    for who in range(1, lanes):
+        taps = taps + small[who]
+    small[0] = taps
+
+    def mid(b, norm, which):
+        r = BLOCKS * KVOL + (b * 3 + norm) * 2 + which
+        return small[0, r : r + 1]
+
+    edge_sums = []
+    pattern_col = lax.broadcasted_iota(jnp.int32, (WP, 256), 0)
+    for b in range(BLOCKS):
+        taps_b = [[small[0, b * KVOL + dt * 9 + k : b * KVOL + dt * 9 + k + 1] for k in range(9)] for dt in range(3)]
+        se = jnp.zeros((1, 256), F32)
+        see = jnp.zeros((1, 256), F32)
+        for f in range(-1, frames + 1):
+            here = live(f)
+            t = [
+                here * (live(f - 1) * taps_b[0][k] + here * taps_b[1][k] + live(f + 1) * taps_b[2][k])
+                for k in range(9)
+            ]
+            for cls in range(3):
+                use = [dh for dh in range(3) if not (cls == 0 and dh == 0) and not (cls == 2 and dh == 2)]
+                col = []
+                for dw in range(3):
+                    v = t[use[0] * 3 + dw]
+                    for dh in use[1:]:
+                        v = v + t[dh * 3 + dw]
+                    col.append(v)
+                middle = col[0] + col[1] + col[2]
+                first, last = col[1] + col[2], col[0] + col[1]
+                edge[b, f + 1, cls] = jnp.where(
+                    pattern_col == 0,
+                    first,
+                    jnp.where(pattern_col == WW - 1, last, jnp.where(pattern_col < WW - 1, middle, 0.0)),
+                )
+                if 0 <= f < frames:
+                    times = 1.0 if cls != 1 else HH - 2.0
+                    se = se + times * (first + last + (WW - 2.0) * middle)
+                    see = see + times * (first * first + last * last + (WW - 2.0) * (middle * middle))
+        edge_sums += [se, see]
+
+    alive_all = sum(live(f) for f in range(frames)) * (HH * WW)
+    here_count = jnp.full((1, 256), 1.0, F32) * alive_all
+    total_start(0, rows_of(flat_sum(carry[0]), flat_sum(carry[1]), here_count, *edge_sums))
+
+    for slot in (("mix", 0), ("exp", 0), ("red", 1), ("mix", 1), ("exp", 1)):
+        gather_wait(*plan[slot])
+    for b in range(BLOCKS):
+        mix[b] = mix_t[b].T
+    red[1] = red_t[1].T
+
+    got = total_finish(0)
+    sums_out[0] = got
+    count = got[2:3]
+    global_edge = [(got[3:4], got[4:5]), (got[5:6], got[6:7])]
+    first_sums = (got[0:1], got[1:2])
+
+    def edge_rows(b, f, j):
+        top = jnp.where(j == 0, 0, 1)
+        bottom = jnp.where(j == QUADS - 1, 2, 1)
+        middle = edge[b, f + 1, 1]
+        return jnp.concatenate([edge[b, f + 1, top], middle, middle, edge[b, f + 1, bottom]], axis=0)
+
+    for b in range(BLOCKS):
+        mean1, scale1, a1, b1 = affine(first_sums[0], first_sums[1], count, mid(b, 0, 0), mid(b, 0, 1))
+        carry = (zero8(), zero8())
+        for f in (0, frames - 1) + tuple(range(1, frames - 1)):
+            alive = live(f)
+
+            def mixing(j, carry):
+                q = f * QUADS + j
+                z = z1[b, pl.ds(q * GROUP, GROUP)].reshape(WIDE, 256)
+                act = (gelu_fwd(z * a1 + b1) * (pad_mask * alive)).astype(BF16)
+                a1s[b, pl.ds(q * GROUP, GROUP)] = act.reshape(GROUP, WP, 256)
+                m = dot(act, mix[b])
+                z2[b, f + 1, pl.ds(1 + j * GROUP, GROUP)] = m.reshape(GROUP, WP, 256)
+                if f in (0, frames - 1):
+                    halo_send[b, 0 if f == 0 else 1, pl.ds(j * GROUP, GROUP)] = m.astype(BF16).reshape(GROUP, WP, 256)
+                return (carry[0] + fold(m), carry[1] + fold(m * m))
+
+            carry = lax.fori_loop(0, QUADS, mixing, carry)
+
+            if f == 0:
+
+                @pl.when(lane > 0)
+                def _():
+                    push(
+                        halo_send.at[b, 0], halo_recv.at[b, 1], halo_ssem.at[b, 0], halo_rsem.at[b, 1], (net.row, lane - 1)
+                    ).start()
+
+            if f == frames - 1:
+
+                @pl.when(lane < lanes - 1)
+                def _():
+                    push(
+                        halo_send.at[b, 1], halo_recv.at[b, 0], halo_ssem.at[b, 1], halo_rsem.at[b, 0], (net.row, lane + 1)
+                    ).start()
+
+        def taps_of(b, half):
+            cols = slice(128 * half, 128 * (half + 1))
+            return [small[0, b * KVOL + k : b * KVOL + k + 1, cols] for k in range(KVOL)]
+
+        def convolve(b, f, acc):
+            alive = live(f)
+            parts = []
+            for half in range(2):
+                lanes_here = slice(128 * half, 128 * (half + 1))
+                kern = taps_of(b, half)
+                pad = pad_mask[:WP, :128] * alive
+
+                def two_rows(i, carry):
+                    s0, s1, s2 = carry
+                    h = 2 * i
+                    part = [[None] * 3 for _ in range(2)]
+                    for dt in range(3):
+                        for rr in range(4):
+                            v = z2[b, f + dt, h + rr, :, lanes_here]
+                            for o in range(2):
+                                dh = rr - o
+                                if 0 <= dh < 3:
+                                    for dw in range(3):
+                                        term = kern[dt * 9 + dh * 3 + dw] * v
+                                        part[o][dw] = term if part[o][dw] is None else part[o][dw] + term
+                    for o in range(2):
+                        p = part[o]
+                        c = p[1] + pltpu.roll(p[0], 1, 0) + pltpu.roll(p[2], WP - 1, 0)
+                        c = c * pad
+                        conv[b, f * HH + h + o, :, lanes_here] = c
+                        cls = jnp.where(h + o == 0, 0, jnp.where(h + o == HH - 1, 2, 1))
+                        e = edge[b, f + 1, cls, :, lanes_here]
+                        s0 = s0 + fold(c)
+                        s1 = s1 + fold(c * c)
+                        s2 = s2 + fold(c * e)
+                    return (s0, s1, s2)
+
+                parts.append(lax.fori_loop(0, HH // 2, two_rows, tuple(a[half] for a in acc)))
+            return [[parts[0][k], parts[1][k]] for k in range(3)]
+
+        acc = [[zero8(128), zero8(128)] for _ in range(3)]
+        for f in range(1, frames - 1):
+            acc = convolve(b, f, acc)
+
+        def fill(side, frame, present):
+            @pl.when(present)
+            def _():
+                push(
+                    halo_send.at[b, 1 - side],
+                    halo_recv.at[b, side],
+                    halo_ssem.at[b, 1 - side],
+                    halo_rsem.at[b, side],
+                    (net.row, jnp.where(side == 0, jnp.maximum(lane - 1, 0), jnp.minimum(lane + 1, lanes - 1))),
+                ).wait_recv()
+
+                def widen(j, _):
+                    z2[b, frame, pl.ds(1 + j * GROUP, GROUP)] = halo_recv[b, side, pl.ds(j * GROUP, GROUP)].astype(F32)
+                    return 0
+
+                lax.fori_loop(0, QUADS, widen, 0)
+
+            @pl.when(jnp.logical_not(present))
+            def _():
+                def clear(j, _):
+                    z2[b, frame, pl.ds(1 + j * GROUP, GROUP)] = jnp.zeros((GROUP, WP, 256), F32)
+                    return 0
+
+                lax.fori_loop(0, QUADS, clear, 0)
+
+        fill(0, 0, lane > 0)
+        acc = convolve(b, 0, acc)
+        fill(1, frames + 1, lane < lanes - 1)
+        acc = convolve(b, frames - 1, acc)
+        joined = [jnp.concatenate([flat_sum(a[0]), flat_sum(a[1])], axis=1) for a in acc]
+        total_start(3 * b + 1, rows_of(flat_sum(carry[0]), flat_sum(carry[1]), *joined))
+        got = total_finish(3 * b + 1)
+        sums_out[3 * b + 1] = got
+        mean2, scale2, a2, b2 = affine(got[0:1], got[1:2], count, mid(b, 1, 0), mid(b, 1, 1))
+        sc, scc, sce = got[2:3], got[3:4], got[4:5]
+        se, see = global_edge[b]
+        total3 = a2 * sc + b2 * se
+        square3 = a2 * a2 * scc + 2.0 * a2 * b2 * sce + b2 * b2 * see
+        mean3, scale3, a3, b3 = affine(total3, square3, count, mid(b, 2, 0), mid(b, 2, 1))
+
+        pc, pe = a3 * a2, a3 * b2
+
+        def expanding(q, carry):
+            f = lax.div(q, QUADS)
+            j = lax.rem(q, QUADS)
+            alive = live(f)
+            c = conv[b, pl.ds(q * GROUP, GROUP)].reshape(WIDE, 256)
+            n3 = c * pc + (edge_rows(b, f, j) * pe + b3)
+            act = squeeze(gelu_fwd(n3) * alive).astype(BF16)
+            a3s[b, pl.ds(pl.multiple_of(q * FLAT, FLAT), FLAT)] = act
+            z = dot(act, exp[b])
+            return (carry[0] + fold(z), carry[1] + fold(z * z))
+
+        carry = lax.fori_loop(0, frames * QUADS, expanding, (zero8(1024), zero8(1024)))
+        total_start(3 * b + 2, rows_of(flat_sum(carry[0]), flat_sum(carry[1])))
+        got = total_finish(3 * b + 2)
+        sums_out[3 * b + 2] = got
+        gain4, shift4 = norm_out[b, 0:1], norm_out[b, 1:2]
+        mean4, scale4, a4, b4 = affine(
+            wide_row(got, 0), wide_row(got, 4), jnp.concatenate([count] * 4, axis=1), gain4, shift4
+        )
+
+        source = x0 if b == 0 else x1
+
+        def closing(q, carry):
+            f = lax.div(q, QUADS)
+            alive = live(f)
+            rows = pl.ds(pl.multiple_of(q * FLAT, FLAT), FLAT)
+            z = dot(a3s[b, rows], exp[b])
+            pre = (z * a4 + b4) * alive + source[rows].astype(F32)
+            result = (gelu_fwd(pre) * alive).astype(BF16)
+            if b == 0:
+                x1[rows] = result
+                z = dot(result, red[1])
+                z1[1, pl.ds(q * GROUP, GROUP)] = spread(z).reshape(GROUP, WP, 256)
+                return (carry[0] + fold(z), carry[1] + fold(z * z))
+            x0[rows] = result
+            return carry
+
+        carry = lax.fori_loop(0, frames * QUADS, closing, (zero8(), zero8()))
+        if b == 0:
+            total_start(3, rows_of(flat_sum(carry[0]), flat_sum(carry[1])))
+            got = total_finish(3)
+            sums_out[3] = got
+            first_sums = (got[0:1], got[1:2])
+
+    stores = []
+    for k, (src, dst) in enumerate(((x0, out_hbm), (x1, x1_hbm), (z1, z1_out), (conv, c_out))):
+        copy = pltpu.make_async_copy(src, dst, store_sem.at[k])
+        copy.start()
+        stores.append(copy)
+    for b in range(BLOCKS):
+        copy = pltpu.make_async_copy(z2.at[b, pl.ds(1, frames), pl.ds(1, HH)], z2_out.at[b], store_sem.at[4 + b])
+        copy.start()
+        stores.append(copy)
+    for copy in stores:
+        copy.wait()
+    for copy in late:
+        copy.wait_send()
+    for b in range(BLOCKS):
+
+        @pl.when(lane > 0)
+        def _():
+            push(
+                halo_send.at[b, 0], halo_recv.at[b, 1], halo_ssem.at[b, 0], halo_rsem.at[b, 1], (net.row, jnp.maximum(lane - 1, 0))
+            ).wait_send()
+
+        @pl.when(lane < lanes - 1)
+        def _():
+            push(
+                halo_send.at[b, 1], halo_recv.at[b, 0], halo_ssem.at[b, 1], halo_rsem.at[b, 0], (net.row, jnp.minimum(lane + 1, lanes - 1))
+            ).wait_send()
+
+
+def forward_call(groups, lanes, counts, tokens, reduce_loc, mix_loc, expand_loc, small_loc, norm_out):
+    rows = tokens.shape[0]
+    frames = rows // (HH * WW)
+    whole = pl.BlockSpec(memory_space=pltpu.VMEM)
+    hbm = pl.BlockSpec(memory_space=pl.ANY)
+    dma = pltpu.SemaphoreType.DMA
+    far = groups * (lanes // 2)
+    lines = frames * HH
+    return pl.pallas_call(
+        functools.partial(forward_kernel, groups, lanes),
+        out_shape=(
+            jax.ShapeDtypeStruct((rows, 1024), BF16),
+            jax.ShapeDtypeStruct((rows, 1024), BF16),
+            jax.ShapeDtypeStruct((BLOCKS, lines, WP, 256), F32),
+            jax.ShapeDtypeStruct((BLOCKS, frames, HH, WP, 256), F32),
+            jax.ShapeDtypeStruct((BLOCKS, lines, WP, 256), F32),
+            jax.ShapeDtypeStruct((6, 8, 256), F32),
+        ),
+        in_specs=[pl.BlockSpec(memory_space=pltpu.SMEM), hbm] + [whole] * 5,
+        out_specs=[hbm] * 5 + [whole],
+        scratch_shapes=[
+            pltpu.VMEM((rows, 1024), BF16),
+            pltpu.VMEM((rows, 1024), BF16),
+            pltpu.VMEM((BLOCKS, 256, 1024), BF16),
+            pltpu.VMEM((BLOCKS, 1024, 256), BF16),
+            pltpu.VMEM((BLOCKS, 256, 256), BF16),
+            pltpu.VMEM((BLOCKS, 256, 256), BF16),
+            pltpu.VMEM((BLOCKS, 256, 1024), BF16),
+            pltpu.VMEM((lanes,) + small_loc.shape, F32),
+            pltpu.VMEM((BLOCKS, lines, WP, 256), F32),
+            pltpu.VMEM((BLOCKS, lines, WP, 256), BF16),
+            pltpu.VMEM((BLOCKS, frames + 2, HH + 2, WP, 256), F32),
+            pltpu.VMEM((BLOCKS, lines, WP, 256), F32),
+            pltpu.VMEM((BLOCKS, rows, 256), BF16),
+            pltpu.VMEM((BLOCKS, frames + 2, 3, WP, 256), F32),
+            pltpu.VMEM((BLOCKS, 2, HH, WP, 256), BF16),
+            pltpu.VMEM((BLOCKS, 2, HH, WP, 256), BF16),
+            pltpu.VMEM((6, 2, 8, 256), F32),
+            pltpu.VMEM((6, far, 8, 256), F32),
+            dma((6,)),
+            dma((6,)),
+            dma((6, far)),
+            dma((6, far)),
+            dma((7, lanes)),
+            dma((7, lanes)),
+            dma((BLOCKS, 2)),
+            dma((BLOCKS, 2)),
+            dma((frames,)),
+            dma((6,)),
+        ],
+        compiler_params=pltpu.CompilerParams(
+            collective_id=1, has_side_effects=True, vmem_limit_bytes=60 * 2**20
+        ),
+    )(counts, tokens, reduce_loc, mix_loc, expand_loc, small_loc, norm_out)
 
 
 def gelu_soft(value):
@@ -27,7 +604,7 @@
     return jax.vjp(gelu_soft, value)[1](grad)[0]
 
 
-def dot(left, right, over_left, over_right):
+def dot_over(left, right, over_left, over_right):
     return lax.dot_general(
         left, right, (((over_left,), (over_right,)), ((), ())), preferred_element_type=jnp.float32
     )
@@ -191,38 +768,34 @@
     flat = lambda v: v.reshape(-1, wide)
     deepen = lambda v: v.reshape(-1, HH, WW, wide)
 
-    hidden = tokens
+    small = jnp.concatenate([w_depth.reshape(-1, narrow), norm_mid.reshape(-1, narrow)], axis=0)
+    small = jnp.pad(small, ((0, -small.shape[0] % 8), (0, 0)))
+    small = lax.dynamic_update_slice(jnp.zeros((small.shape[0], mix_all.shape[1]), F32), small, (0, lane * narrow))
+    hidden, x1, z1, z2, c, sums = forward_call(
+        sizes[1],
+        lanes,
+        frame_counts,
+        tokens,
+        jnp.swapaxes(w_reduce, 1, 2).astype(BF16),
+        jnp.swapaxes(w_mix, 1, 2).astype(BF16),
+        w_expand.astype(BF16),
+        small,
+        norm_out,
+    )
+    unpad = lambda v: v.reshape(-1, HH, WP, wide)[:, :, :WW].reshape(-1, wide)
+    count = sums[0, 2, 0]
     stored = []
-    count = None
     for b in range(BLOCKS):
         mid = mid_all[b]
-        first = dot(hidden, reduce_all[b], 1, 0)
-        sums = [column_sum(first * mask), column_sum(first * first * mask)]
-        if count is None:
-            sums.append(jnp.full((128,), jnp.sum(mask)))
-            t, q, n = all_sum(sizes, sums)
-            count = n[0]
-        else:
-            t, q = all_sum(sizes, sums)
-        mean1, scale1, a1, b1 = affine_of(t, q, count, mid[0, 0], mid[0, 1])
+        x = tokens if b == 0 else x1
+        first, second, conv = unpad(z1[b]), unpad(z2[b]), unpad(c[b])
+        got = sums[0] if b == 0 else sums[3]
+        mean1, scale1, a1, b1 = affine_of(got[0], got[1], count, mid[0, 0], mid[0, 1])
         act1 = (mask * gelu_soft(first * a1 + b1)).astype(jnp.bfloat16)
-        second = dot(act1, mix_all[b], 1, 0)
-        masked2 = second * mask
-        conv = flat(depthwise(halo(deepen(masked2), lanes), depth_all[b], frames))
         ones = jnp.broadcast_to(alive[:, None, None, None], (frames + 2, HH, WW, 1))
         edge = flat(depthwise(ones, depth_all[b], frames))
-        t, q, sc, scc, sce, se, see = all_sum(
-            sizes,
-            [
-                column_sum(masked2),
-                column_sum(masked2 * masked2),
-                column_sum(conv * mask),
-                column_sum(conv * conv * mask),
-                column_sum(conv * edge * mask),
-                column_sum(edge * mask),
-                column_sum(edge * edge * mask),
-            ],
-        )
+        t, q, sc, scc, sce = [sums[3 * b + 1, i] for i in range(5)]
+        se, see = sums[0, 3 + 2 * b], sums[0, 4 + 2 * b]
         mean2, scale2, a2, b2 = affine_of(t, q, count, mid[1, 0], mid[1, 1])
         t3 = a2 * sc + b2 * se
         q3 = a2 * a2 * scc + 2.0 * a2 * b2 * sce + b2 * b2 * see
@@ -230,17 +803,15 @@
         third = a2 * conv + b2 * edge
         norm3 = third * a3 + b3
         act3 = (mask * gelu_soft(norm3)).astype(jnp.bfloat16)
-        fourth = dot(act3, expand_all[b], 1, 0)
-        t, q = all_sum(sizes, [column_sum(fourth * mask), column_sum(fourth * fourth * mask)])
+        fourth = dot_over(act3, expand_all[b], 1, 0)
+        t, q = sums[3 * b + 2, :4].reshape(-1), sums[3 * b + 2, 4:].reshape(-1)
         mean4, scale4, a4, b4 = affine_of(t, q, count, norm_out[b, 0], norm_out[b, 1])
-        pre = mask * (fourth * a4 + b4) + hidden.astype(jnp.float32)
-        result = (mask * gelu_soft(pre)).astype(jnp.bfloat16)
+        pre = mask * (fourth * a4 + b4) + x.astype(jnp.float32)
         stored.append(
-            (hidden, first, act1, second, conv, edge, third, norm3, act3, fourth, pre)
+            (x, first, act1, second, conv, edge, third, norm3, act3, fourth, pre)
             + ((mean1, scale1, a1, b1), (mean2, scale2, a2, b2), (mean3, scale3, a3, b3), (mean4, scale4, a4, b4))
             + ((sc, scc, sce, se, see),)
         )
-        hidden = result
 
     gradient = cotangent.astype(jnp.float32)
     collected = [None] * BLOCKS
@@ -252,8 +823,8 @@
         unit4 = (fourth - mean4) * scale4
         shift4, gain4 = all_sum(sizes, [column_sum(residual), column_sum(residual * unit4)])
         fourth_grad = (mask * a4 * (residual - shift4 / count - unit4 * gain4 / count)).astype(jnp.bfloat16)
-        grad_expand = dot(act3, fourth_grad, 0, 0)
-        e3 = mask * gelu_back(norm3, dot(fourth_grad, expand_all[b], 1, 1))
+        grad_expand = dot_over(act3, fourth_grad, 0, 0)
+        e3 = mask * gelu_back(norm3, dot_over(fourth_grad, expand_all[b], 1, 1))
         e3_sum, e3_conv, e3_edge = all_sum(sizes, [column_sum(e3), column_sum(e3 * conv), column_sum(e3 * edge)])
         shift3 = e3_sum
         gain3 = scale3 * (a2 * e3_conv + b2 * e3_edge - mean3 * e3_sum)
@@ -273,13 +844,13 @@
         act2_grad = flat(depthwise(deep, depth_all[b][::-1], frames))
         unit2 = (second - mean2) * scale2
         second_grad = (mask * a2 * (act2_grad - shift2 / count - unit2 * gain2 / count)).astype(jnp.bfloat16)
-        grad_mix = dot(act1, second_grad, 0, 0)
-        e1 = mask * gelu_back(first * a1 + b1, dot(second_grad, mix_all[b], 1, 1))
+        grad_mix = dot_over(act1, second_grad, 0, 0)
+        e1 = mask * gelu_back(first * a1 + b1, dot_over(second_grad, mix_all[b], 1, 1))
         unit1 = (first - mean1) * scale1
         shift1, gain1 = all_sum(sizes, [column_sum(e1), column_sum(e1 * unit1)])
         first_grad = (mask * a1 * (e1 - shift1 / count - unit1 * gain1 / count)).astype(jnp.bfloat16)
-        grad_reduce = dot(x, first_grad, 0, 0)
-        gradient = dot(first_grad, reduce_all[b], 1, 1) + residual
+        grad_reduce = dot_over(x, first_grad, 0, 0)
+        gradient = dot_over(first_grad, reduce_all[b], 1, 1) + residual
         grad_mid = jnp.stack(
             [jnp.stack([gain1, shift1]), jnp.stack([gain2, shift2]), jnp.stack([gain3, shift3])]
         )

time: 842 us -> 897 us (1.065)
  Pallas kernels: 139 us -> 203 us
  other arithmetic: 262 us -> 232 us
  local copies, waits for them, and re-layouts: 173 us -> 186 us
  waiting for transfers between devices: 54.8 us -> 67.1 us
  starting transfers between devices: 20.7 us -> 9.59 us
  matrix products: 101 us -> 112 us
    pallas_call x0 -> x1, Pallas kernels: none -> 138 us  [forward_call(): pl.pallas_call(functools.partial(forward_kernel, groups, lanes), out_shap...]
    pallas_call x12 -> x6, Pallas kernels: 139 us -> 64.7 us  [all_sum(): pl.pallas_call(functools.partial(sum_kernel, sizes), out_shape=jax.ShapeD...]
    reduce_sum x3 -> x2, other arithmetic: 65.2 us -> 1.2 us  [column_sum(): return jnp.sum(value, axis=0)]
    mul x0 -> x2, other arithmetic: none -> 23.3 us  [shards(): third_grad = mask * (p * e3 + q + r * third)]
    add x2 -> x0, other arithmetic: 19.8 us -> none  [depthwise(): total + tap * padded[step:step + frames, row:row + HH, column:column + WW]]
    convert_element_type x2, other arithmetic: 7.61 us -> 26.5 us  [shards(): (mask * a2 * (act2_grad - shift2 / count - unit2 * gain2 / count)).astype...]
    convert_element_type x2, other arithmetic: 8.5 us -> 26.9 us  [shards(): act3 = (mask * gelu_soft(norm3)).astype(jnp.bfloat16)]
    add x2, other arithmetic: 6.15 us -> 22.7 us  [shards(): third = a2 * conv + b2 * edge]
  transfers between devices with their start and end apart: 15 -> 11, of which waited for: 2 -> 3; matrix products, arithmetic and copies ran while one was open for 31% -> 47% of each run, Pallas kernels for 3% -> 20%
where the time goes in v2:
time: 897 us; the launch traced here: 889 us
  other arithmetic  232 us (26%)
  Pallas kernels  203 us (23%)
  local copies, waits for them, and re-layouts  186 us (21%)
  matrix products  112 us (12%)
  waiting for transfers between devices  67.1 us (7%)
  blocking collectives  58.6 us (7%)
  between operations  20.8 us (2%)
  starting transfers between devices  9.59 us (1%)
    pallas_call x1, Pallas kernels, forward_call(): pl.pallas_call(functools.partial(forward_kernel, groups, lanes), out_shap...  138 us
    dot_general x14, matrix products, dot_over(): lax.dot_general(left, right, (((over_left,), (over_right,)), ((), ())), p...  112 us
    pallas_call x6, Pallas kernels, all_sum(): pl.pallas_call(functools.partial(sum_kernel, sizes), out_shape=jax.ShapeD...  64.7 us
    slice x3, local copies, waits for them, and re-layouts, depthwise(): tap = kern[step * 9 + row * 3 + column]  56.8 us
    reduce_sum x6, other arithmetic, kernel_grad(): taps.append(jnp.sum(field * part, axis=(0, 1, 2)))  47.5 us
    psum x1, waiting for transfers between devices, shards(): lax.psum((scatter(stacked[0], 2), scatter(stacked[1], 2), scatter(stacked...  45.4 us
    psum x1, blocking collectives, shards(): lax.psum((scatter(stacked[0], 2), scatter(stacked[1], 2), scatter(stacked...  37.6 us
    convert_element_type x2, other arithmetic, shards(): act3 = (mask * gelu_soft(norm3)).astype(jnp.bfloat16)  26.9 us
  transfers between devices with their start and end apart: 11, of which 3 were waited for; matrix products, arithmetic and copies ran while one was open for 47% of the time, Pallas kernels for 20%

profile of v2, /device:TPU:0, one launch (start us, length us, event | category | flops | bytes accessed | tf_op | source)
XLA Modules:
  0.0 888.7 jit_solution(13561569606629448561)
XLA Ops:
  21.0 16.9 %slice_reduce_fusion.54 = (f32[256]{0:T(256)}, f32[256]{0:T(256)}, f32[256]{0:T(256)}, f32[256]{0:T(256)}, f32[256]{0:T(256)}, /*index=5*/f32[256]{0:T(256)}, f3...) fusion(f32[2,27,256]{1,0,2:T(2,128)S(1)} %all_gather.16), kind=kLoop, calls=%fused_computation.315 | loop fusion | bytes 32768 | tf_op jit(solution)/shard_map/slice | solution.py:701
  37.8 19.4 %slice_reduce_fusion.55 = (f32[256]{0:T(256)}, f32[256]{0:T(256)}, f32[256]{0:T(256)}, f32[256]{0:T(256)}, f32[256]{0:T(256)}, /*index=5*/f32[256]{0:T(256)}, f3...) fusion(f32[2,27,256]{1,0,2:T(2,128)S(1)} %all_gather.16), kind=kLoop, calls=%fused_computation.316 | loop fusion | bytes 38912 | tf_op jit(solution)/shard_map/slice | solution.py:701
  57.2 20.5 %slice_reduce_fusion.58 = (f32[256]{0:T(256)}, f32[256]{0:T(256)}, f32[256]{0:T(256)}, f32[256]{0:T(256)}, f32[256]{0:T(256)}, /*index=5*/f32[256]{0:T(256)}, f3...) fusion(f32[2,27,256]{1,0,2:T(2,128)S(1)} %all_gather.16), kind=kLoop, calls=%fused_computation.319 | loop fusion | bytes 38912 | tf_op jit(solution)/shard_map/slice | solution.py:701
  83.2 138.0 %shard_map.302 = (bf16[2352,1024]{1,0:T(8,128)(2,1)}, bf16[2352,1024]{1,0:T(8,128)(2,1)}, f32[2,84,32,256]{3,2,1,0:T(8,128)}, f32[2,3,28,32,256]{4,3,2,1,0:T(8,1...) custom-call(s32[1]{0:T(128)} %copy.163.counts, bf16[2352,1024]{1,0:T(8,128)(2,1)} %tokens.1, ...), custom_call_target="tpu_custom_call" | custom-call | tf_op jit(solution)/shard_map/pallas_call | solution.py:551
  266.4 11.7 %slice_reduce_fusion.60 = (f32[256]{0:T(256)}, f32[256]{0:T(256)}, f32[256]{0:T(256)}, f32[256]{0:T(256)}, f32[256]{0:T(256)}, /*index=5*/f32[256]{0:T(256)}, f3...) fusion(f32[3,2,256]{0,1,2:T(2,128)S(1)} %get-tuple-element.334, ...), kind=kLoop, calls=%fused_computation.321 | loop fusion | bytes 24576 | tf_op jit(solution)/shard_map/slice | solution.py:793
  288.7 13.1 %fusion.32 = bf16[3,28,28,256]{3,2,1,0:T(8,128)(2,1)} fusion(f32[256]{0:T(256)S(1)} %multiply_subtract_fusion.9, f32[256]{0:T(256)S(1)} %get-tuple-element.312, f32[256]{0:T(256)S(1)} %copy-done.196, f32[256]{0:T(256)S(1)} %copy-done.200, f32[256]{0:T(256)S(1)} %copy-done.204, f32[256]{0:T(256)S(1)} %copy-done.208, f32[256]{0:T(256)S(1)} %copy-done.212, ...), kind=kLoop, calls=%fused_computation.63 | loop fusion | flops 40943616 | bytes 3870256 | tf_op jit(solution)/shard_map/convert_element_type | solution.py:805
  308.5 13.8 %fusion.23 = bf16[3,28,28,256]{3,2,1,0:T(8,128)(2,1)} fusion(f32[256]{0:T(256)S(1)} %multiply_subtract_fusion.11, f32[256]{0:T(256)S(1)} %get-tuple-element.306, f32[3,28,28]{2,1,0:T(8,128)S(1)} %copy-done.48, f32[3,28,28]{2,1,0:T(8,128)S(1)} %copy-done.49, f32[256]{0:T(256)} %get-tuple-element.238, f32[3,28,28]{2,1,0:T(8,128)S(1)} %copy-done.50, ...), kind=kLoop, calls=%fused_computation.54 | loop fusion | flops 40943616 | bytes 3870256 | tf_op jit(solution)/shard_map/convert_element_type | solution.py:805
  333.0 11.5 %multiply_add_fusion.4 = f32[2352,256]{1,0:T(8,128)} fusion(f32[2352,256]{1,0:T(8,128)} %reshape.3084, f32[256]{0:T(256)S(1)} %get-tuple-element.310, f32[256]{0:T(256)S(1)} %get-tuple-element.309, f32[2352]{0:T(1024)S(1)} %copy-done.90, f32[256]{0:T(256)} %get-tuple-element.210, f32[2352]{0:T(1024)S(1)} %copy-done.88, f32[256]{0:T(256)} %get-tuple-element.238, ...), kind=kLoop, calls=%fused_computation.192 | loop fusion | flops 33718272 | bytes 5100608 | tf_op jit(solution)/shard_map/add | solution.py:803
  344.7 11.1 %multiply_add_fusion.1 = f32[2352,256]{1,0:T(8,128)} fusion(f32[2352,256]{1,0:T(8,128)S(1)} %copy-done.9, f32[256]{0:T(256)S(1)} %get-tuple-element.316, f32[256]{0:T(256)S(1)} %get-tuple-element.315, f32[2352]{0:T(1024)S(1)} %copy-done.90, f32[256]{0:T(256)S(1)} %copy-done.162, f32[2352]{0:T(1024)S(1)} %copy-done.88, f32[256]{0:T(256)S(1)} %copy-done.197, ...), kind=kLoop, calls=%fused_computation.183 | loop fusion | flops 33718272 | bytes 5100608 | tf_op jit(solution)/shard_map/add | solution.py:803
  367.3 18.0 %fusion.219 = (f32[1024]{0:T(1024)S(1)}, f32[1024]{0:T(1024)S(1)}, f32[2352,1024]{1,0:T(8,128)}, f32[2352,1024]{1,0:T(8,128)}) fusion(f32[1024]{0:T(1024)S(1)} %get-tuple-element.423, f32[1024]{0:T(1024)S(1)} %bitcast.711, bf16[2352,1024]{1,0:T(8,128)(2,1)} %get-tuple-element.29, f32[1024]{0:T(1024)S(1)} %get-tuple-element.413, ...), kind=kOutput, calls=%fused_computation.571 | convolution fusion | flops 1307785216 | bytes 30663872 | tf_op jit(solution)/shard_map/dot_general | solution.py:608
  436.0 11.7 %add_multiply_fusion.3 = f32[2352,256]{1,0:T(8,128)S(1)} fusion(f32[2352,256]{1,0:T(8,128)} %copy-done.25, f32[256]{0:T(256)S(1)} %get-tuple-element.302, f32[256]{0:T(256)S(1)} %get-tuple-element.301, f32[256]{0:T(256)S(1)} %get-tuple-element.306, f32[2352]{0:T(1024)S(1)} %mul.4718, f32[2352]{0:T(1024)S(1)} %copy-done.90, f32[256]{0:T(256)S(1)} %copy-done.299, ...), kind=kLoop, calls=%fused_computation.188 | loop fusion | flops 36728832 | bytes 7521536 | tf_op jit(solution)/shard_map/mul | solution.py:840
  485.9 13.2 %multiply_convert_fusion.3 = bf16[3,28,28,256]{3,2,1,0:T(8,128)(2,1)} fusion(f32[3,28,28,256]{3,2,1,0:T(8,128)} %reshape.3091, f32[3,28,32,256]{3,2,1,0:T(8,128)S(1)} %get-tuple-element.319, f32[5,30,30,256]{3,2,1,0:T(8,128)S(1)} %select_maximum_fusion.2, f32[1,28,28,256]{3,2,1,0:T(8,128)} %copy-done.17, f32[1,28,28,256]{3,2,1,0:T(8,128)} %copy-done.15, ...), kind=kLoop, calls=%fused_computation.144 | loop fusion | flops 38535168 | bytes 65462288 | tf_op jit(solution)/shard_map/convert_element_type | solution.py:846
  508.7 11.8 %shard_map.305 = f32[8,128]{1,0:T(8,128)} custom-call(f32[8,128]{1,0:T(8,128)} %select_maximum_fusion.8.x_ref), custom_call_target="tpu_custom_call" | custom-call | tf_op jit(solution)/shard_map/pallas_call | solution.py:666
  529.2 19.2 %fusion.218 = (f32[1024]{0:T(1024)S(1)}, f32[1024]{0:T(1024)S(1)}, f32[2352,1024]{1,0:T(8,128)}) fusion(f32[1024]{0:T(1024)S(1)} %copy-done.318, f32[2352,1024]{1,0:T(8,128)} %fusion.106, f32[1024]{0:T(1024)S(1)} %bitcast.708, bf16[2352,1024]{1,0:T(8,128)(2,1)} %tokens.1, f32[1024]{0:T(1024)S(1)} %copy-done.360, f32[1024]{0:T(1024)S(1)} %copy-done.317, ...), kind=kOutput, calls=%fused_computation.570 | convolution fusion | flops 1307785216 | bytes 35480768 | tf_op jit(solution)/shard_map/dot_general | solution.py:608
  571.2 11.1 %multiply_reduce_fusion.57 = (f32[256]{0:T(256)S(1)}, f32[2352,256]{1,0:T(8,128)S(1)}) fusion(f32[2352]{0:T(1024)S(1)} %copy-done.91, f32[256]{0:T(256)S(1)} %copy-done.163, f32[2352]{0:T(1024)S(1)} %copy-done.89, f32[256]{0:T(256)} %get-tuple-element.211, f32[2352]{0:T(1024)S(1)} %copy-done.87, f32[256]{0:T(256)} %get-tuple-element.212, ...), kind=kOutput, calls=%fused_computation.180 | convolution fusion | flops 1279487744 | bytes 10532864 | tf_op jit(solution)/shard_map/dot_general | solution.py:608
  584.3 11.0 %shard_map.307 = f32[8,128]{1,0:T(8,128)} custom-call(f32[8,128]{1,0:T(8,128)} %select_maximum_fusion.6.x_ref), custom_call_target="tpu_custom_call" | custom-call | tf_op jit(solution)/shard_map/pallas_call | solution.py:666
  597.6 11.6 %add_multiply_fusion.2 = f32[2352,256]{1,0:T(8,128)S(1)} fusion(f32[2352,256]{1,0:T(8,128)} %copy-done.24, f32[256]{0:T(256)S(1)} %get-tuple-element.296, f32[256]{0:T(256)S(1)} %get-tuple-element.295, f32[256]{0:T(256)S(1)} %copy-done.155, f32[2352]{0:T(1024)S(1)} %copy-done.42, f32[2352]{0:T(1024)S(1)} %copy-done.91, f32[256]{0:T(256)S(1)} %copy-done.163, ...), kind=kLoop, calls=%fused_computation.179 | loop fusion | flops 36728832 | bytes 7521536 | tf_op jit(solution)/shard_map/mul | solution.py:840
  625.0 11.4 %multiply_reduce_fusion.2 = (f32[256]{0:T(256)}, f32[256]{0:T(256)}, f32[256]{0:T(256)}, f32[256]{0:T(256)}, f32[256]{0:T(256)}, /*index=5*/f32[256]{0:T(256)}, f32[256]{0:T(256)}, f32[256]{0:T(256)}) fusion(f32[5,30,30,256]{3,2,1,0:T(8,128)} %copy-done, f32[256]{0:T(256)} %copy-done.140, f32[256]{0:T(256)} %copy-done.134, ...), kind=kLoop, calls=%fused_computation.86 | loop fusion | flops 11438080 | bytes 21686284 | tf_op jit(solution)/shard_map/reduce_sum | solution.py:713
  640.9 13.3 %multiply_convert_fusion.2 = bf16[3,28,28,256]{3,2,1,0:T(8,128)(2,1)} fusion(f32[3,28,28,256]{3,2,1,0:T(8,128)} %reshape.3104, f32[3,28,32,256]{3,2,1,0:T(8,128)S(1)} %copy-done.2, f32[5,30,30,256]{3,2,1,0:T(8,128)S(1)} %select_maximum_fusion, f32[1,28,28,256]{3,2,1,0:T(8,128)} %copy-done.21, f32[1,28,28,256]{3,2,1,0:T(8,128)} %copy-done.19, ...), kind=kLoop, calls=%fused_computation.142 | loop fusion | flops 38535168 | bytes 65462288 | tf_op jit(solution)/shard_map/convert_element_type | solution.py:846
  671.5 12.0 %multiply_reduce_fusion.4 = (f32[256]{0:T(256)}, f32[256]{0:T(256)}, f32[256]{0:T(256)}, f32[256]{0:T(256)}, f32[256]{0:T(256)}, /*index=5*/f32[256]{0:T(256)}, ...) fusion(f32[5,30,30,256]{3,2,1,0:T(8,128)} %copy-done, f32[256]{0:T(256)S(1)} %copy-done.142, ...), kind=kLoop, calls=%fused_computation.88 | loop fusion | flops 16254208 | bytes 25703436 | tf_op jit(solution)/shard_map/reduce_sum | solution.py:713
  726.5 11.2 %multiply_reduce_fusion.30 = (f32[256]{0:T(256)}, f32[256]{0:T(256)}, f32[256]{0:T(256)}, f32[256]{0:T(256)}, f32[256]{0:T(256)}, /*index=5*/f32[256]{0:T(256)}, f32[256]{0:T(256)}, f32[256]{0:T(256)}) fusion(f32[5,30,30,256]{3,2,1,0:T(8,128)} %copy-done.1, f32[256]{0:T(256)S(1)} %copy-done.139, f32[256]{0:T(256)S(1)} %copy-done.133, ...), kind=kLoop, calls=%fused_computation.115 | loop fusion | flops 11438080 | bytes 21686284 | tf_op jit(solution)/shard_map/reduce_sum | solution.py:713
  769.3 14.0 %reduce-scatter.10.cloned.1.call-done = f32[64,54]{1,0:T(8,128)} async-done(((f32[256,54]{1,0:T(8,128)}), f32[64,54]{1,0:T(8,128)}) %reduce-scatter.10.cloned.1.call-update) | async-done | bytes 13840
  784.3 37.6 %psum.30 = f32[2,27,64]{2,1,0:T(8,128)S(1)} all-reduce(f32[2,27,64]{2,1,0:T(8,128)S(1)} %copy.143), channel_id=1, replica_groups=mesh['dp'=8,'chan'=4] {'dp'}, use_global_device_ids=true, to_apply=%region_73.74 | all-reduce | flops 3456 | bytes 27648 | tf_op jit(solution)/shard_map/psum | solution.py:860
  823.8 45.4 %all-reduce.15.cloned.1.call-done = (f32[2,1024,64]{1,2,0:T(8,128)}, f32[2,256,64]{1,2,0:T(8,128)}, f32[2,64,1024]{2,1,0:T(8,128)}) async-done(((f32[2,1024,64]{1,2,0:T(8,128)}, f32[2,256,64]{1,2,0:T(8,128)}, f32[2,64,1024]{2,1,0:T(8,128)}), (f32[2,1024,64]{1,2,0:T(8,128)}, f32[2,256,64]{1,2,0:T(8,128)}, f32[2,64,1024]{2,1,0:T(8,128)})) %all-reduce.15.cloned.1.call-update) | async-done | bytes 1179664 | tf_op jit(solution)/shard_map/psum | solution.py:860
  (963 shorter events, 359.2 us)
Async XLA Ops:
  7.2 360.1 %all-gather.3.cloned.1.call-start = ((), (), s32[]{:S(2)}) async-start(), calls=%async_computation.3 | async-start | bytes 1310720 | tf_op jit(solution)/shard_map/all_gather | solution.py:756
  9.1 520.2 %all-gather.5.cloned.1.call-start = ((), (), s32[]{:S(2)}) async-start(), calls=%async_computation.4 | async-start | bytes 1310720 | tf_op jit(solution)/shard_map/all_gather | solution.py:756
  10.9 740.8 %all-reduce.13.cloned.1.call-start = ((), (), s32[]{:S(2)}) async-start(), calls=%async_computation.8 | async-start | bytes 1048576
  79.2 228.7 %copy-start.143 = (f32[3]{0:T(128)}, f32[3]{0:T(128)S(1)}, u32[]{:S(2)}) copy-start(f32[3]{0:T(128)S(1)} %slice.1093) | copy-start | bytes 40
  226.4 209.5 %copy-start.41 = (f32[2352]{0:T(1024)}, f32[2352]{0:T(1024)S(1)}, u32[]{:S(2)}) copy-start(f32[2352]{0:T(1024)S(1)} %mul.4718) | copy-start | bytes 28228
  227.0 208.9 %copy-start.66 = (f32[2352]{0:T(1024)}, f32[2352]{0:T(1024)S(1)}, u32[]{:S(2)}) copy-start(f32[2352]{0:T(1024)S(1)} %mul.4966) | copy-start | bytes 28228
  261.1 105.6 %copy-start.148 = (f32[1,2,4,128]{3,1,2,0:T(2,128)}, f32[1,2,4,128]{3,1,2,0:T(2,128)S(1)}, u32[]{:S(2)}) copy-start(f32[1,2,4,128]{3,1,2,0:T(2,128)S(1)} %copy.145) | copy-start | bytes 12292
  266.4 358.6 %copy-start.3 = (f32[3,28,32,256]{3,2,1,0:T(8,128)}, f32[3,28,32,256]{3,2,1,0:T(8,128)S(1)}, u32[]{:S(2)}) copy-start(f32[3,28,32,256]{3,2,1,0:T(8,128)S(1)} %get-tuple-element.319) | copy-start | bytes 8257540
  306.7 129.3 %copy-start.134 = (f32[256]{0:T(256)}, f32[256]{0:T(256)S(1)}, u32[]{:S(2)}) copy-start(f32[256]{0:T(256)S(1)} %get-tuple-element.309) | copy-start | bytes 3076
  306.7 129.3 %copy-start.140 = (f32[256]{0:T(256)}, f32[256]{0:T(256)S(1)}, u32[]{:S(2)}) copy-start(f32[256]{0:T(256)S(1)} %get-tuple-element.310) | copy-start | bytes 3076
  306.7 129.3 %copy-start.157 = (f32[256]{0:T(256)}, f32[256]{0:T(256)S(1)}, u32[]{:S(2)}) copy-start(f32[256]{0:T(256)S(1)} %get-tuple-element.306) | copy-start | bytes 3076
  454.6 23.3 %collective-permute-start.1 = (f32[1,28,28,256]{3,0,2,1:T(1,128)}, f32[1,28,28,256]{3,0,2,1:T(1,128)}, u32[]{:S(2)}, u32[]{:S(2)}) collective-permute-start(f32[1,28,28,256]{3,0,2,1:T(1,128)} %slice.1312), channel_id=1, source_target_pairs={{1,0},{2,1},{3,2},{5,4},{6,5},{7,6},{9,8},{10,9},{11,10},{13,12},{... | collective-permute-start | bytes 2408456 | tf_op jit(solution)/shard_map/ppermute | solution.py:691
  455.9 23.4 %collective-permute-start = (f32[1,28,28,256]{3,0,2,1:T(1,128)}, f32[1,28,28,256]{3,0,2,1:T(1,128)S(1)}, u32[]{:S(2)}, u32[]{:S(2)}) collective-permute-start(f32[1,28,28,256]{3,0,2,1:T(1,128)} %slice.1311), channel_id=1, source_target_pairs={{0,1},{1,2},{2,3},{4,5},{5,6},{6,7},{8,9},{9,10},{10,11},{12,13},{... | collective-permute-start | bytes 2408456 | tf_op jit(solution)/shard_map/ppermute | solution.py:690
  619.8 16.6 %collective-permute-start.3 = (f32[1,28,28,256]{3,0,2,1:T(1,128)}, f32[1,28,28,256]{3,0,2,1:T(1,128)S(1)}, u32[]{:S(2)}, u32[]{:S(2)}) collective-permute-start(f32[1,28,28,256]{3,0,2,1:T(1,128)} %slice.1314), channel_id=1, source_target_pairs={{1,0},{2,1},{3,2},{5,4},{6,5},{7,6},{9,8},{10,9},{11,10},{13,12},{... | collective-permute-start | bytes 2408456 | tf_op jit(solution)/shard_map/ppermute | solution.py:691
  621.1 15.4 %collective-permute-start.2 = (f32[1,28,28,256]{3,0,2,1:T(1,128)}, f32[1,28,28,256]{3,0,2,1:T(1,128)S(1)}, u32[]{:S(2)}, u32[]{:S(2)}) collective-permute-start(f32[1,28,28,256]{3,0,2,1:T(1,128)} %slice.1313), channel_id=1, source_target_pairs={{0,1},{1,2},{2,3},{4,5},{5,6},{6,7},{8,9},{9,10},{10,11},{12,13},{... | collective-permute-start | bytes 2408456 | tf_op jit(solution)/shard_map/ppermute | solution.py:690
  658.9 94.4 %reduce-scatter.8.cloned.1.call-start = ((), (), s32[]{:S(2)}) async-start(), calls=%async_computation.6 | async-start | bytes 2621440 | tf_op jit(solution)/shard_map/reduce_scatter | solution.py:859
  665.5 95.4 %reduce-scatter.6.cloned.1.call-start = ((), (), s32[]{:S(2)}) async-start(), calls=%async_computation.5 | async-start | bytes 2621440 | tf_op jit(solution)/shard_map/reduce_scatter | solution.py:859
  715.2 68.1 %reduce-scatter.10.cloned.1.call-start = ((), (), s32[]{:S(2)}) async-start(), calls=%async_computation.7 | async-start | bytes 163840
  751.0 118.2 %all-reduce.15.cloned.1.call-start = ((), (), s32[]{:S(2)}) async-start(), calls=%async_computation.9 | async-start | bytes 2359296 | tf_op jit(solution)/shard_map/psum | solution.py:860
  761.6 107.6 %copy-start.38 = (f32[2,256,64]{1,2,0:T(8,128)S(1)}, f32[2,256,64]{1,2,0:T(8,128)}, u32[]{:S(2)}) copy-start(f32[2,256,64]{1,2,0:T(8,128)} %param.19) | copy-start | bytes 393220
  761.6 107.6 %copy-start.130 = (f32[2,256,64]{1,2,0:T(8,128)S(1)}, f32[2,256,64]{1,2,0:T(8,128)}, u32[]{:S(2)}) copy-start(f32[2,256,64]{1,2,0:T(8,128)} %param.25) | copy-start | bytes 393220
  761.6 109.3 %copy-start.31 = (f32[2,1024,64]{1,2,0:T(8,128)S(1)}, f32[2,1024,64]{1,2,0:T(8,128)}, u32[]{:S(2)}) copy-start(f32[2,1024,64]{1,2,0:T(8,128)} %param.18) | copy-start | bytes 1572868
  761.6 109.2 %copy-start.44 = (f32[2,1024,64]{1,2,0:T(8,128)S(1)}, f32[2,1024,64]{1,2,0:T(8,128)}, u32[]{:S(2)}) copy-start(f32[2,1024,64]{1,2,0:T(8,128)} %param.24) | copy-start | bytes 1572868
  769.3 103.8 %copy-start.45 = (f32[2,64,1024]{2,1,0:T(8,128)S(1)}, f32[2,64,1024]{2,1,0:T(8,128)}, u32[]{:S(2)}) copy-start(f32[2,64,1024]{2,1,0:T(8,128)} %param.27) | copy-start | bytes 1572868
  (364 other events, 3085.8 us)
Sparse Core Ops, SparseCore 0:
  10.2 19.4 all-gather.2
  31.8 16.7 all-gather.4
  659.0 32.7 all-reduce.12
  694.8 31.4 reduce-scatter.7
  729.3 31.4 reduce-scatter.5
  763.7 19.5 reduce-scatter.9
  788.2 80.9 all-reduce.14

commit v3 on v2

v3 whole, which is shorter than its diff:
```python
import functools

import jax
import jax.numpy as jnp
from jax import lax
from jax.experimental import pallas as pl
from jax.experimental.pallas import tpu as pltpu
from jax.sharding import PartitionSpec as P

FRAMES = 12
HH = 28
WW = 28
WP = 32
KVOL = 27
BLOCKS = 2
GROUP = 4
QUADS = HH // GROUP
FLAT = GROUP * WW
WIDE = GROUP * WP

EPS = 1e-05
LEARN_RATE = 0.001
MOMENTUM = 0.9
DECAY = 0.0001
MESH = pl.DeviceIdType.MESH
F32 = jnp.float32
BF16 = jnp.bfloat16
ROOT = 0.7978845608028654
CUBE = 0.044715


def gelu_fwd(v):
    t = jnp.tanh(v * (ROOT + (ROOT * CUBE) * (v * v)))
    h = 0.5 * v
    return h * t + h


def gelu_slope(v):
    s = v * v
    t = jnp.tanh(v * (ROOT + (ROOT * CUBE) * s))
    return 0.5 * (1.0 + t) + (0.5 * v) * (1.0 - t * t) * (ROOT + (3.0 * ROOT * CUBE) * s)


def dot_rows(left, right):
    return lax.dot_general(left, right, (((0,), (0,)), ((), ())), preferred_element_type=F32)


def dot(left, right):
    return jnp.dot(left, right, preferred_element_type=F32)


def fold(v):
    return jnp.sum(v.reshape(v.shape[0] // 8, 8, v.shape[1]), axis=0)


def spread(v):
    gap = jnp.zeros((WP - WW, v.shape[1]), v.dtype)
    parts = []
    for h in range(GROUP):
        parts += [v[WW * h : WW * (h + 1)], gap]
    return jnp.concatenate(parts, axis=0)


def squeeze(v):
    return jnp.concatenate([v[WP * h : WP * h + WW] for h in range(GROUP)], axis=0)


def rows_of(*vectors):
    parts = []
    for v in vectors:
        parts += [v[:, 256 * i : 256 * (i + 1)] for i in range(v.shape[1] // 256)]
    if len(parts) < 8:
        parts.append(jnp.zeros((8 - len(parts), 256), F32))
    return jnp.concatenate(parts, axis=0)


def flat_sum(v):
    return jnp.sum(v, axis=0, keepdims=True)


def wide_row(v, first):
    return jnp.concatenate([v[first + i : first + i + 1] for i in range(4)], axis=1)


class Net:
    def __init__(self, groups, lanes):
        self.lanes = lanes
        self.low, self.high = stages(groups)
        self.row = lax.axis_index("dp")
        self.lane = lax.axis_index("chan")
        self.core = lax.rem(self.lane, 2)
        self.side = lax.div(self.lane, 2)
        self.half = lanes // 2
        self.row_low = lax.rem(self.row, self.low)
        self.row_high = lax.div(self.row, self.low)

    def near(self):
        return [(1 - self.core, (self.row, self.side * 2 + 1 - self.core))]

    def far(self):
        out = []
        for o in range(self.low):
            for p in range(self.half):
                if o or p:
                    row = lax.rem(self.row_low + o, self.low)
                    side = lax.rem(self.side + p, self.half)
                    out.append((row * self.half + side, (self.row_high * self.low + row, side * 2 + self.core)))
        return out

    def far_slot(self):
        return self.row_low * self.half + self.side

    def top(self):
        rows = [lax.rem(self.row_high + o, self.high) for o in range(1, self.high)]
        return [(row, (row * self.low + self.row_low, self.lane)) for row in rows]

    def chan_peers(self):
        lanes = [lax.rem(self.lane + o, self.lanes) for o in range(1, self.lanes)]
        return [(lane, (self.row, lane)) for lane in lanes]


def stages(groups):
    low = min(groups, 8)
    return low, groups // low


def push(src, dst, send, recv, device):
    copy = pltpu.make_async_remote_copy(
        src_ref=src, dst_ref=dst, send_sem=send, recv_sem=recv, device_id=device, device_id_type=MESH
    )
    return copy


def whole_kernel(
    groups,
    lanes,
    counts,
    tokens,
    cotangent,
    reduce_loc,
    mix_loc,
    expand_loc,
    small_loc,
    norm_out,
    out_hbm,
    gtok_hbm,
    gred_hbm,
    gexp_hbm,
    gmix_hbm,
    gdep_out,
    gmid_out,
    gout_out,
    x0,
    x1,
    yb,
    sb,
    red_t,
    exp,
    tbuf,
    mix_t,
    mix,
    small,
    z1,
    a1s,
    z2,
    dz,
    hz,
    conv,
    a3s,
    edge,
    pat,
    d2s,
    halo_send,
    halo_recv,
    gbig,
    gmix,
    near,
    far,
    top,
    near_send,
    near_recv,
    far_send,
    far_recv,
    top_send,
    top_recv,
    gather_send,
    gather_recv,
    halo_ssem,
    halo_rsem,
    load_sem,
    store_sem,
):
    net = Net(groups, lanes)
    lane = net.lane
    frames = tokens.shape[0] // (HH * WW)
    frame_rows = HH * WW
    last = frames - 1
    count_here = counts[0]
    xs = (x0, x1)

    def live(frame):
        position = lane * frames + frame
        return jnp.where((position >= 0) & (position < count_here), 1.0, 0.0)

    def frame_copy(src, dst, f, sem):
        rows = pl.ds(f * frame_rows, frame_rows)
        return pltpu.make_async_copy(src.at[rows], dst.at[rows], sem)

    loads = [frame_copy(tokens, x0, f, load_sem.at[f]) for f in range(frames)]
    cot_load = pltpu.make_async_copy(cotangent, sb, load_sem.at[frames])
    for copy in loads:
        copy.start()
    cot_load.start()

    barrier = pltpu.get_barrier_semaphore()
    friends = [d for peers in (net.near(), net.far(), net.top(), net.chan_peers()) for _, d in peers]
    for device in friends:
        pl.semaphore_signal(barrier, inc=1, device_id=device, device_id_type=MESH)
    pl.semaphore_wait(barrier, len(friends))

    own = net.lane
    share = red_t.shape[1] // lanes
    late = []

    def gather(slot, src, dst_of):
        for step, (_, device) in enumerate(net.chan_peers()):
            copy = push(src, dst_of(own), gather_send.at[slot, step], gather_recv.at[slot, own], device)
            copy.start()
            late.append(copy)
        dst_of(own)[...] = src[...]

    def gather_wait(slot, src, dst_of):
        for step, (peer, device) in enumerate(net.chan_peers()):
            push(src, dst_of(peer), gather_send.at[slot, step], gather_recv.at[slot, peer], device).wait_recv()

    def block_rows(ref, b):
        return lambda who: ref.at[b, pl.ds(pl.multiple_of(who * share, share), share)]

    plan = {
        ("red", 0): (0, reduce_loc.at[0], block_rows(red_t, 0)),
        ("mix", 0): (1, mix_loc.at[0], block_rows(mix_t, 0)),
        ("small", 0): (2, small_loc, lambda who: small.at[who]),
        ("exp", 0): (3, expand_loc.at[0], block_rows(exp, 0)),
        ("red", 1): (4, reduce_loc.at[1], block_rows(red_t, 1)),
        ("mix", 1): (5, mix_loc.at[1], block_rows(mix_t, 1)),
        ("exp", 1): (6, expand_loc.at[1], block_rows(exp, 1)),
    }
    for slot, src, dst_of in plan.values():
        gather(slot, src, dst_of)

    def total_start(i, value):
        near[i, net.core] = value
        for who, device in net.near():
            copy = push(near.at[i, net.core], near.at[i, net.core], near_send.at[i], near_recv.at[i], device)
            copy.start()
            late.append(copy)
            copy.wait_recv()
        far[i, net.far_slot()] = near[i, 0] + near[i, 1]
        for step, (who, device) in enumerate(net.far()):
            mine = far.at[i, net.far_slot()]
            copy = push(mine, mine, far_send.at[i, step], far_recv.at[i, net.far_slot()], device)
            copy.start()
            late.append(copy)

    def total_finish(i):
        for step, (who, device) in enumerate(net.far()):
            push(far.at[i, who], far.at[i, who], far_send.at[i, step], far_recv.at[i, who], device).wait_recv()
        total = far[i, 0]
        for j in range(1, net.low * net.half):
            total = total + far[i, j]
        if net.high > 1:
            mine = top.at[i, net.row_high]
            top[i, net.row_high] = total
            for step, (who, device) in enumerate(net.top()):
                copy = push(mine, mine, top_send.at[i, step], top_recv.at[i, net.row_high], device)
                copy.start()
                late.append(copy)
            for step, (who, device) in enumerate(net.top()):
                push(top.at[i, who], top.at[i, who], top_send.at[i, step], top_recv.at[i, who], device).wait_recv()
            total = top[i, 0]
            for j in range(1, net.high):
                total = total + top[i, j]
        return total

    def halo_copy(kind, slot, side):
        step = -1 if side == 0 else 1
        return push(
            halo_send.at[side],
            halo_recv.at[slot, 1 - side],
            halo_ssem.at[kind, side],
            halo_rsem.at[kind, 1 - side],
            (net.row, lane + step),
        )

    def sends_to(side):
        return lane > 0 if side == 0 else lane < lanes - 1

    def halo_start(kind, slot, side):
        @pl.when(sends_to(side))
        def _():
            halo_copy(kind, slot, side).start()

    def halo_sent(kind, slot, side):
        @pl.when(sends_to(side))
        def _():
            halo_copy(kind, slot, side).wait_send()

    def halo_wait(kind, slot, side):
        step = -1 if side == 0 else 1
        push(
            halo_send.at[1 - side],
            halo_recv.at[slot, side],
            halo_ssem.at[kind, 1 - side],
            halo_rsem.at[kind, side],
            (net.row, lane + step),
        ).wait_recv()

    column = lax.broadcasted_iota(jnp.int32, (WIDE, 256), 0) % WP
    pad_mask = (column < WW).astype(F32)

    def affine(total, square, count, gain, shift):
        mean = total / count
        var = square / count - mean * mean
        scale = lax.rsqrt(var + EPS)
        return mean, scale, gain * scale, shift - mean * (gain * scale)

    def back_affine(e_sum, ez_sum, count, norm):
        mean, scale, a, _ = norm
        gain_grad = scale * (ez_sum - mean * e_sum)
        slope = -a * scale * gain_grad / count
        bias = -a * e_sum / count - slope * mean
        return slope, bias, gain_grad, e_sum

    def zero8(n=256):
        return jnp.zeros((8, n), F32)

    blank = jnp.zeros((WP, 256), F32)
    for f in range(frames):
        for b in range(BLOCKS):
            z2[b, f, 0] = blank
            z2[b, f, HH + 1] = blank
        dz[f, 0] = blank
        dz[f, HH + 1] = blank
    for side in range(2):
        hz[side, 0] = blank
        hz[side, HH + 1] = blank

    gather_wait(*plan["red", 0])
    tbuf[...] = red_t[0].T

    carry = (zero8(), zero8())
    for f in range(frames):
        loads[f].wait()
        alive = live(f)

        def project(j, carry):
            q = f * QUADS + j
            x = x0[pl.ds(pl.multiple_of(q * FLAT, FLAT), FLAT)]
            z = dot(x, tbuf[...])
            z1[0, pl.ds(q * GROUP, GROUP)] = spread(z).reshape(GROUP, WP, 256)
            z = z * alive
            return (carry[0] + fold(z), carry[1] + fold(z * z))

        carry = lax.fori_loop(0, QUADS, project, carry)

    alive_all = sum(live(f) for f in range(frames)) * (HH * WW)
    here_count = jnp.full((1, 256), 1.0, F32) * alive_all
    total_start(0, rows_of(flat_sum(carry[0]), flat_sum(carry[1]), here_count))

    gather_wait(*plan["small", 0])
    taps = small[0]
    for who in range(1, lanes):
        taps = taps + small[who]
    small[0] = taps

    def mid(b, norm, which):
        r = BLOCKS * KVOL + (b * 3 + norm) * 2 + which
        return small[0, r : r + 1]

    edge_sums = []
    pattern_col = lax.broadcasted_iota(jnp.int32, (WP, 256), 0)
    for b in range(BLOCKS):
        taps_b = [[small[0, b * KVOL + dt * 9 + k : b * KVOL + dt * 9 + k + 1] for k in range(9)] for dt in range(3)]
        se = jnp.zeros((1, 256), F32)
        see = jnp.zeros((1, 256), F32)
        for f in range(-1, frames + 1):
            here = live(f)
            t = [
                here * (live(f - 1) * taps_b[0][k] + here * taps_b[1][k] + live(f + 1) * taps_b[2][k])
                for k in range(9)
            ]
            for cls in range(3):
                use = [dh for dh in range(3) if not (cls == 0 and dh == 0) and not (cls == 2 and dh == 2)]
                col = []
                for dw in range(3):
                    v = t[use[0] * 3 + dw]
                    for dh in use[1:]:
                        v = v + t[dh * 3 + dw]
                    col.append(v)
                inner = col[0] + col[1] + col[2]
                left, right = col[1] + col[2], col[0] + col[1]
                edge[b, f + 1, cls] = jnp.where(
                    pattern_col == 0,
                    left,
                    jnp.where(pattern_col == WW - 1, right, jnp.where(pattern_col < WW - 1, inner, 0.0)),
                )
                if 0 <= f < frames:
                    times = 1.0 if cls != 1 else HH - 2.0
                    se = se + times * (left + right + (WW - 2.0) * inner)
                    see = see + times * (left * left + right * right + (WW - 2.0) * (inner * inner))
        edge_sums.append((se, see))

    for slot in (("mix", 0), ("exp", 0), ("red", 1), ("mix", 1), ("exp", 1)):
        gather_wait(*plan[slot])
    for b in range(BLOCKS):
        mix[b] = mix_t[b].T
    tbuf[...] = red_t[1].T

    got = total_finish(0)
    count = got[2:3]
    count4 = jnp.concatenate([count] * 4, axis=1)
    first_sums = (got[0:1], got[1:2])

    def edge_rows(ref, j):
        top = jnp.where(j == 0, 0, 1)
        bottom = jnp.where(j == QUADS - 1, 2, 1)
        middle = ref[1]
        return jnp.concatenate([ref[top], middle, middle, ref[bottom]], axis=0)

    def row_class(h):
        return jnp.where(h == 0, 0, jnp.where(h == HH - 1, 2, 1))

    def convolve(local, f, b, flip, emit, acc):
        done = []
        for half in range(2):
            cols = slice(128 * half, 128 * (half + 1))
            kern = [small[0, b * KVOL + k : b * KVOL + k + 1, cols] for k in range(KVOL)]
            if flip:
                kern = kern[::-1]
            planes = []
            for dt in range(3):
                g = f + dt - 1
                planes.append(hz.at[0] if g < 0 else hz.at[1] if g > last else local.at[g])

            def two_rows(i, carry):
                h = 2 * i
                part = [[None] * 3 for _ in range(2)]
                for dt in range(3):
                    for rr in range(4):
                        v = planes[dt][h + rr, :, cols]
                        for o in range(2):
                            dh = rr - o
                            if 0 <= dh < 3:
                                for dw in range(3):
                                    term = kern[dt * 9 + dh * 3 + dw] * v
                                    part[o][dw] = term if part[o][dw] is None else part[o][dw] + term
                for o in range(2):
                    p = part[o]
                    c = p[1] + pltpu.roll(p[0], 1, 0) + pltpu.roll(p[2], WP - 1, 0)
                    carry = emit(h + o, half, cols, c, carry)
                return carry

            done.append(lax.fori_loop(0, HH // 2, two_rows, tuple(a[half] for a in acc)))
        return [[done[0][k], done[1][k]] for k in range(len(acc))]

    order = (0, last) + tuple(range(1, last))
    norms = []
    mid_grads = {}
    out_grads = {}

    def open_block(b, q, f, rows):
        z = dot(a3s[b, rows], exp[b])
        a4, b4 = norms[b][3][2], norms[b][3][3]
        return z, (z * a4 + b4) * live(f) + xs[b][rows].astype(F32)

    out_store = [frame_copy(yb, out_hbm, f, store_sem.at[f]) for f in range(frames)]

    for b in range(BLOCKS):
        norm1 = affine(first_sums[0], first_sums[1], count, mid(b, 0, 0), mid(b, 0, 1))
        _, _, a1, b1 = norm1
        carry = (zero8(), zero8())
        if b > 0:
            for side in range(2):
                halo_sent(2 * (b - 1) + 1, 2 + b - 1, side)
        for f in order:
            alive = live(f)

            def mixing(j, carry):
                q = f * QUADS + j
                z = z1[b, pl.ds(q * GROUP, GROUP)].reshape(WIDE, 256)
                act = (gelu_fwd(z * a1 + b1) * (pad_mask * alive)).astype(BF16)
                m = dot(act, mix[b])
                z2[b, f, pl.ds(1 + j * GROUP, GROUP)] = m.reshape(GROUP, WP, 256)
                if f in (0, last):
                    halo_send[0 if f == 0 else 1, pl.ds(j * GROUP, GROUP)] = m.astype(BF16).reshape(GROUP, WP, 256)
                return (carry[0] + fold(m), carry[1] + fold(m * m))

            carry = lax.fori_loop(0, QUADS, mixing, carry)
            if f in (0, last):
                halo_start(2 * b, b, 0 if f == 0 else 1)

        def emit_conv(f):
            pad = pad_mask[:WP, :128] * live(f)

            def emit(row, half, cols, c, carry):
                c = c * pad
                conv[b, f * HH + row, :, cols] = c
                if f in (0, last):
                    halo_send[0 if f == 0 else 1, row, :, cols] = c.astype(BF16)
                e = edge[b, f + 1, row_class(row), :, cols]
                s0, s1, s2 = carry
                return (s0 + fold(c), s1 + fold(c * c), s2 + fold(c * e))

            return emit

        def fill(side):
            present = lane > 0 if side == 0 else lane < lanes - 1

            @pl.when(present)
            def _():
                halo_wait(2 * b, b, side)

                def widen(j, _):
                    hz[side, pl.ds(1 + j * GROUP, GROUP)] = halo_recv[b, side, pl.ds(j * GROUP, GROUP)].astype(F32)
                    return 0

                lax.fori_loop(0, QUADS, widen, 0)

            @pl.when(jnp.logical_not(present))
            def _():
                def clear(j, _):
                    hz[side, pl.ds(1 + j * GROUP, GROUP)] = jnp.zeros((GROUP, WP, 256), F32)
                    return 0

                lax.fori_loop(0, QUADS, clear, 0)

        acc = [[zero8(128), zero8(128)] for _ in range(3)]
        for f in range(1, last):
            acc = convolve(z2.at[b], f, b, False, emit_conv(f), acc)
        for side in range(2):
            fill(side)
            halo_sent(2 * b, b, side)
            f = 0 if side == 0 else last
            acc = convolve(z2.at[b], f, b, False, emit_conv(f), acc)
            halo_start(2 * b + 1, 2 + b, side)
        joined = [jnp.concatenate([flat_sum(a[0]), flat_sum(a[1])], axis=1) for a in acc]
        total_start(3 * b + 1, rows_of(flat_sum(carry[0]), flat_sum(carry[1]), *joined, *edge_sums[b]))
        got = total_finish(3 * b + 1)
        norm2 = affine(got[0:1], got[1:2], count, mid(b, 1, 0), mid(b, 1, 1))
        _, _, a2, b2 = norm2
        sc, scc, sce, se, see = [got[i : i + 1] for i in range(2, 7)]
        total3 = a2 * sc + b2 * se
        square3 = a2 * a2 * scc + 2.0 * a2 * b2 * sce + b2 * b2 * see
        norm3 = affine(total3, square3, count, mid(b, 2, 0), mid(b, 2, 1))
        _, _, a3, b3 = norm3

        def expanding(q, carry):
            f = lax.div(q, QUADS)
            j = lax.rem(q, QUADS)
            c = conv[b, pl.ds(q * GROUP, GROUP)].reshape(WIDE, 256)
            n3 = c * (a3 * a2) + (edge_rows(edge.at[b, f + 1], j) * (a3 * b2) + b3)
            act = squeeze(gelu_fwd(n3) * live(f)).astype(BF16)
            a3s[b, pl.ds(pl.multiple_of(q * FLAT, FLAT), FLAT)] = act
            z = dot(act, exp[b])
            return (carry[0] + fold(z), carry[1] + fold(z * z))

        carry = lax.fori_loop(0, frames * QUADS, expanding, (zero8(1024), zero8(1024)))
        total_start(3 * b + 2, rows_of(flat_sum(carry[0]), flat_sum(carry[1])))
        got = total_finish(3 * b + 2)
        norm4 = affine(wide_row(got, 0), wide_row(got, 4), count4, norm_out[b, 0:1], norm_out[b, 1:2])
        norms.append((norm1, norm2, norm3, norm4, (sc, scc, sce, se, see)))

        if b == 0:
            def closing(q, carry):
                f = lax.div(q, QUADS)
                rows = pl.ds(pl.multiple_of(q * FLAT, FLAT), FLAT)
                _, pre = open_block(0, q, f, rows)
                result = (gelu_fwd(pre) * live(f)).astype(BF16)
                x1[rows] = result
                z = dot(result, tbuf[...])
                z1[1, pl.ds(q * GROUP, GROUP)] = spread(z).reshape(GROUP, WP, 256)
                return (carry[0] + fold(z), carry[1] + fold(z * z))

            carry = lax.fori_loop(0, frames * QUADS, closing, (zero8(), zero8()))
            total_start(3, rows_of(flat_sum(carry[0]), flat_sum(carry[1])))
            tbuf[...] = exp[1].T
            got = total_finish(3)
            first_sums = (got[0:1], got[1:2])

    cot_load.wait()

    def ending(q, carry):
        f = lax.div(q, QUADS)
        alive = live(f)
        rows = pl.ds(pl.multiple_of(q * FLAT, FLAT), FLAT)
        z, pre = open_block(1, q, f, rows)
        yb[rows] = (gelu_fwd(pre) * alive).astype(BF16)
        s = gelu_slope(pre) * (sb[rows].astype(F32) * alive)
        sb[rows] = s.astype(BF16)
        return (carry[0] + fold(s), carry[1] + fold(s * z))

    carry = lax.fori_loop(0, frames * QUADS, ending, (zero8(1024), zero8(1024)))
    total_start(6, rows_of(flat_sum(carry[0]), flat_sum(carry[1])))
    for copy in out_store:
        copy.start()

    grad_stores = []
    for b in reversed(range(BLOCKS)):
        turn = BLOCKS - 1 - b
        base = 6 + 3 * turn
        norm1, norm2, norm3, norm4, (sc, scc, sce, se, see) = norms[b]
        _, _, a1, b1 = norm1
        mean2, scale2, a2, b2 = norm2
        mean3, scale3, a3, b3 = norm3
        a4 = norm4[2]

        got = total_finish(base)
        slope4, bias4, gain_grad, shift_grad = back_affine(wide_row(got, 0), wide_row(got, 4), count4, norm4)
        out_grads[b] = (gain_grad, shift_grad)
        if turn == 0:
            for copy in out_store:
                copy.wait()
        for side in range(2):
            if turn == 0:
                halo_sent(2 * (BLOCKS - 1) + 1, 2 + BLOCKS - 1, side)
            else:
                halo_sent(2 * BLOCKS + turn - 1, b + 1, side)

        kind = 2 * BLOCKS + turn
        acc = (zero8(), zero8(), zero8())
        for f in order:
            alive = live(f)

            def shrinking(j, acc):
                q = f * QUADS + j
                rows = pl.ds(pl.multiple_of(q * FLAT, FLAT), FLAT)
                z = dot(a3s[b, rows], exp[b])
                d4 = (sb[rows].astype(F32) * a4 + (z * slope4 + bias4) * alive).astype(BF16)
                yb[rows] = d4
                c = conv[b, pl.ds(q * GROUP, GROUP)].reshape(WIDE, 256)
                e = edge_rows(edge.at[b, f + 1], j)
                n3 = c * (a3 * a2) + (e * (a3 * b2) + b3)
                e3 = spread(dot(d4, tbuf[...])) * gelu_slope(n3)
                dz[f, pl.ds(1 + j * GROUP, GROUP)] = e3.reshape(GROUP, WP, 256)
                if f in (0, last):
                    halo_send[0 if f == 0 else 1, pl.ds(j * GROUP, GROUP)] = e3.astype(BF16).reshape(GROUP, WP, 256)
                return (acc[0] + fold(e3), acc[1] + fold(e3 * c), acc[2] + fold(e3 * e))

            acc = lax.fori_loop(0, QUADS, shrinking, acc)
            if f in (0, last):
                halo_start(kind, b, 0 if f == 0 else 1)
        total_start(base + 1, rows_of(*[flat_sum(a) for a in acc]))

        if turn > 0:
            for copy in grad_stores:
                copy.wait()

        def expand_grad(i, _):
            cols = pl.ds(pl.multiple_of(i * 256, 256), 256)
            gbig[0, :, cols] = dot_rows(a3s[b], yb[:, cols])
            return 0

        lax.fori_loop(0, 4, expand_grad, 0)
        if b > 0:
            tbuf[...] = exp[b - 1].T

        got = total_finish(base + 1)
        e3_sum, e3_conv, e3_edge = got[0:1], got[1:2], got[2:3]
        e3_third = a2 * e3_conv + b2 * e3_edge
        slope3, bias3, gain3, shift3 = back_affine(e3_sum, e3_third, count, norm3)
        third_conv = a2 * scc + b2 * sce
        third_edge = a2 * sce + b2 * see
        d3_conv = a3 * e3_conv + bias3 * sc + slope3 * third_conv
        d3_edge = a3 * e3_edge + bias3 * se + slope3 * third_edge
        slope2, bias2, gain2, shift2 = back_affine(d3_edge, d3_conv, count, norm2)

        for f in range(-1, frames + 1):
            live_pad = pad_mask[:WP] * live(f)
            for cls in range(3):
                pat[f + 1, cls] = bias3 * live_pad + (slope3 * b2) * edge[b, f + 1, cls]
        slope_c = slope3 * a2

        def to_d3(q, _):
            f = lax.div(q, QUADS)
            j = lax.rem(q, QUADS)
            rows = pl.ds(1 + j * GROUP, GROUP)
            c = conv[b, pl.ds(q * GROUP, GROUP)].reshape(WIDE, 256)
            e3 = dz[f, rows].reshape(WIDE, 256)
            d3 = e3 * a3 + c * slope_c + edge_rows(pat.at[f + 1], j)
            dz[f, rows] = d3.reshape(GROUP, WP, 256)
            return 0

        lax.fori_loop(0, frames * QUADS, to_d3, 0)

        def fill_back(side):
            present = lane > 0 if side == 0 else lane < lanes - 1
            f = -1 if side == 0 else frames

            @pl.when(present)
            def _():
                halo_wait(2 * b + 1, 2 + b, side)
                halo_wait(kind, b, side)

                def widen(j, _):
                    rows = pl.ds(j * GROUP, GROUP)
                    c = halo_recv[2 + b, side, rows].astype(F32).reshape(WIDE, 256)
                    e3 = halo_recv[b, side, rows].astype(F32).reshape(WIDE, 256)
                    d3 = e3 * a3 + c * slope_c + edge_rows(pat.at[f + 1], j)
                    hz[side, pl.ds(1 + j * GROUP, GROUP)] = d3.reshape(GROUP, WP, 256)
                    return 0

                lax.fori_loop(0, QUADS, widen, 0)

            @pl.when(jnp.logical_not(present))
            def _():
                def clear(j, _):
                    hz[side, pl.ds(1 + j * GROUP, GROUP)] = jnp.zeros((GROUP, WP, 256), F32)
                    return 0

                lax.fori_loop(0, QUADS, clear, 0)

        for side in range(2):
            fill_back(side)

        def emit_back(f):
            pad = pad_mask[:WP, :128] * live(f)

            def emit(row, half, cols, e2, carry):
                z = z2[b, f, row + 1, :, cols]
                d2 = (e2 * a2[:, cols] + (z * slope2[:, cols] + bias2[:, cols])) * pad
                d2s[f * HH + row, :, cols] = d2.astype(BF16)
                return carry

            return emit

        for f in range(frames):
            convolve(dz, f, b, True, emit_back(f), [])

        def unmixing(q, acc):
            rows = pl.ds(q * GROUP, GROUP)
            e = dot(d2s[rows].reshape(WIDE, 256), mix_t[b])
            z = z1[b, rows].reshape(WIDE, 256)
            n1 = z * a1 + b1
            a1s[rows] = (gelu_fwd(n1) * (pad_mask * live(lax.div(q, QUADS)))).astype(BF16).reshape(GROUP, WP, 256)
            e1 = e * gelu_slope(n1)
            conv[b, rows] = e1.reshape(GROUP, WP, 256)
            return (acc[0] + fold(e1), acc[1] + fold(e1 * z))

        acc = lax.fori_loop(0, frames * QUADS, unmixing, (zero8(), zero8()))
        total_start(base + 2, rows_of(*[flat_sum(a) for a in acc]))

        for half in range(2):
            cols = slice(128 * half, 128 * (half + 1))
            taps_grad = tuple(zero8(128) for _ in range(KVOL))
            for f in range(frames):
                planes = []
                for dt in range(3):
                    g = f - (dt - 1)
                    planes.append(hz.at[0] if g < 0 else hz.at[1] if g > last else dz.at[g])
                shift_rows = b2[:, cols] * (pad_mask[:WP, :128] * live(f))

                def tap_rows(h, taps_grad):
                    a = z2[b, f, h + 1, :, cols] * a2[:, cols] + shift_rows
                    moved = [pltpu.roll(a, 1, 0), a, pltpu.roll(a, WP - 1, 0)]
                    new = list(taps_grad)
                    for dt in range(3):
                        for dh in range(3):
                            d = planes[dt][h + 1 - (dh - 1), :, cols]
                            for dw in range(3):
                                k = dt * 9 + dh * 3 + dw
                                new[k] = new[k] + fold(d * moved[dw])
                    return tuple(new)

                taps_grad = lax.fori_loop(0, HH, tap_rows, taps_grad)
            for k in range(KVOL):
                gdep_out[b, k : k + 1, cols] = flat_sum(taps_grad[k])
        gmix[b] = dot_rows(d2s[...].reshape(frames * HH * WP, 256), a1s[...].reshape(frames * HH * WP, 256))

        got = total_finish(base + 2)
        slope1, bias1, gain1, shift1 = back_affine(got[0:1], got[1:2], count, norm1)
        mid_grads[b] = ((gain1, shift1), (gain2, shift2), (gain3, shift3))

        def input_grad(q):
            f = lax.div(q, QUADS)
            rows = pl.ds(pl.multiple_of(q * FLAT, FLAT), FLAT)
            wide = pl.ds(q * GROUP, GROUP)
            e1 = conv[b, wide].reshape(WIDE, 256)
            z = z1[b, wide].reshape(WIDE, 256)
            d1 = squeeze((e1 * a1 + (z * slope1 + bias1)) * live(f)).astype(BF16)
            a3s[b, rows] = d1
            return f, rows, dot(d1, red_t[b]) + sb[rows].astype(F32)

        if b > 0:

            def passing(q, carry):
                f, rows, g = input_grad(q)
                z, pre = open_block(b - 1, q, f, rows)
                s = gelu_slope(pre) * (g * live(f))
                sb[rows] = s.astype(BF16)
                return (carry[0] + fold(s), carry[1] + fold(s * z))

            carry = lax.fori_loop(0, frames * QUADS, passing, (zero8(1024), zero8(1024)))
            total_start(base + 3, rows_of(flat_sum(carry[0]), flat_sum(carry[1])))
        else:

            def final(q, _):
                f, rows, g = input_grad(q)
                yb[rows] = g.astype(BF16)
                return 0

            lax.fori_loop(0, frames * QUADS, final, 0)
            gtok_store = [frame_copy(yb, gtok_hbm, f, store_sem.at[f]) for f in range(frames)]
            for copy in gtok_store:
                copy.start()

        def reduce_grad(i, _):
            cols = pl.ds(pl.multiple_of(i * 256, 256), 256)
            gbig[1, :, cols] = dot_rows(a3s[b], xs[b][:, cols])
            return 0

        lax.fori_loop(0, 4, reduce_grad, 0)
        grad_stores = [
            pltpu.make_async_copy(gbig.at[0], gexp_hbm.at[b], store_sem.at[frames]),
            pltpu.make_async_copy(gbig.at[1], gred_hbm.at[b], store_sem.at[frames + 1]),
            pltpu.make_async_copy(gmix.at[b], gmix_hbm.at[b], store_sem.at[frames + 2]),
        ]
        for copy in grad_stores:
            copy.start()

    for b in range(BLOCKS):
        for k in range(3):
            for w in range(2):
                r = (b * 3 + k) * 2 + w
                gmid_out[r : r + 1] = mid_grads[b][k][w]
        for w in range(2):
            gout_out[2 * b + w : 2 * b + w + 1] = out_grads[b][w]

    for copy in grad_stores + gtok_store:
        copy.wait()
    for copy in late:
        copy.wait_send()
    for side in range(2):
        halo_sent(2 * BLOCKS + BLOCKS - 1, 0, side)


def whole_call(groups, lanes, counts, tokens, cotangent, reduce_loc, mix_loc, expand_loc, small_loc, norm_out):
    rows = tokens.shape[0]
    frames = rows // (HH * WW)
    whole = pl.BlockSpec(memory_space=pltpu.VMEM)
    hbm = pl.BlockSpec(memory_space=pl.ANY)
    dma = pltpu.SemaphoreType.DMA
    low, high = stages(groups)
    far = low * (lanes // 2)
    lines = frames * HH
    sums = 6 * BLOCKS
    kinds = 3 * BLOCKS
    shape = jax.ShapeDtypeStruct
    return pl.pallas_call(
        functools.partial(whole_kernel, groups, lanes),
        out_shape=(
            shape((rows, 1024), BF16),
            shape((rows, 1024), BF16),
            shape((BLOCKS, 256, 1024), F32),
            shape((BLOCKS, 256, 1024), F32),
            shape((BLOCKS, 256, 256), F32),
            shape((BLOCKS, KVOL, 256), F32),
            shape((BLOCKS * 6, 256), F32),
            shape((BLOCKS * 2, 1024), F32),
        ),
        in_specs=[pl.BlockSpec(memory_space=pltpu.SMEM), hbm, hbm] + [whole] * 5,
        out_specs=[hbm] * 5 + [whole] * 3,
        scratch_shapes=[
            pltpu.VMEM((rows, 1024), BF16),
            pltpu.VMEM((rows, 1024), BF16),
            pltpu.VMEM((rows, 1024), BF16),
            pltpu.VMEM((rows, 1024), BF16),
            pltpu.VMEM((BLOCKS, 256, 1024), BF16),
            pltpu.VMEM((BLOCKS, 256, 1024), BF16),
            pltpu.VMEM((1024, 256), BF16),
            pltpu.VMEM((BLOCKS, 256, 256), BF16),
            pltpu.VMEM((BLOCKS, 256, 256), BF16),
            pltpu.VMEM((lanes,) + small_loc.shape, F32),
            pltpu.VMEM((BLOCKS, lines, WP, 256), F32),
            pltpu.VMEM((lines, WP, 256), BF16),
            pltpu.VMEM((BLOCKS, frames, HH + 2, WP, 256), F32),
            pltpu.VMEM((frames, HH + 2, WP, 256), F32),
            pltpu.VMEM((2, HH + 2, WP, 256), F32),
            pltpu.VMEM((BLOCKS, lines, WP, 256), F32),
            pltpu.VMEM((BLOCKS, rows, 256), BF16),
            pltpu.VMEM((BLOCKS, frames + 2, 3, WP, 256), F32),
            pltpu.VMEM((frames + 2, 3, WP, 256), F32),
            pltpu.VMEM((lines, WP, 256), BF16),
            pltpu.VMEM((2, HH, WP, 256), BF16),
            pltpu.VMEM((2 * BLOCKS, 2, HH, WP, 256), BF16),
            pltpu.VMEM((2, 256, 1024), F32),
            pltpu.VMEM((BLOCKS, 256, 256), F32),
            pltpu.VMEM((sums, 2, 8, 256), F32),
            pltpu.VMEM((sums, far, 8, 256), F32),
            pltpu.VMEM((sums, high, 8, 256), F32),
            dma((sums,)),
            dma((sums,)),
            dma((sums, far)),
            dma((sums, far)),
            dma((sums, high)),
            dma((sums, high)),
            dma((7, lanes)),
            dma((7, lanes)),
            dma((kinds, 2)),
            dma((kinds, 2)),
            dma((frames + 1,)),
            dma((frames + 3,)),
        ],
        compiler_params=pltpu.CompilerParams(
            collective_id=1, has_side_effects=True, vmem_limit_bytes=63 * 2**20
        ),
    )(counts, tokens, cotangent, reduce_loc, mix_loc, expand_loc, small_loc, norm_out)


def descend(weight, moment, grad):
    moment_new = MOMENTUM * moment + grad + DECAY * weight
    return (weight - LEARN_RATE * moment_new, moment_new)


def shards(
    tokens,
    frame_counts,
    cotangent,
    w_reduce,
    w_mix,
    w_depth,
    w_expand,
    norm_mid,
    norm_out,
    moment_reduce,
    moment_mix,
    moment_depth,
    moment_expand,
    moment_mid,
    moment_out,
):
    lane = lax.axis_index("chan")
    lanes = lax.axis_size("chan")
    narrow = w_reduce.shape[2]
    small = jnp.concatenate([w_depth.reshape(-1, narrow), norm_mid.reshape(-1, narrow)], axis=0)
    small = jnp.pad(small, ((0, -small.shape[0] % 8), (0, 0)))
    small = lax.dynamic_update_slice(jnp.zeros((small.shape[0], narrow * lanes), F32), small, (0, lane * narrow))
    output, grad_tokens, gred, gexp, gmix, gdep, gmid, gout = whole_call(
        lax.axis_size("dp"),
        lanes,
        frame_counts,
        tokens,
        cotangent,
        jnp.swapaxes(w_reduce, 1, 2).astype(BF16),
        jnp.swapaxes(w_mix, 1, 2).astype(BF16),
        w_expand.astype(BF16),
        small,
        norm_out,
    )
    scatter = lambda v, axis: lax.psum_scatter(v, "chan", scatter_dimension=axis, tiled=True)
    gred, gmix, gdep, gexp = lax.psum((scatter(gred, 1), scatter(gmix, 1), scatter(gdep, 2), scatter(gexp, 1)), "dp")
    grads = (
        jnp.swapaxes(gred, 1, 2),
        jnp.swapaxes(gmix, 1, 2),
        gdep,
        gexp,
        lax.dynamic_slice_in_dim(gmid.reshape(BLOCKS, 3, 2, -1), lane * narrow, narrow, 3),
        gout.reshape(BLOCKS, 2, -1),
    )
    params = (w_reduce, w_mix, w_depth, w_expand, norm_mid, norm_out)
    moments = (moment_reduce, moment_mix, moment_depth, moment_expand, moment_mid, moment_out)
    updated = [descend(w, m, g) for w, m, g in zip(params, moments, grads)]
    return (output, grad_tokens) + grads + tuple(u[0] for u in updated) + tuple(u[1] for u in updated)


def solution(mesh):
    rows = P(("dp", "chan"), None)
    weights = (
        P(None, None, "chan"),
        P(None, None, "chan"),
        P(None, None, "chan"),
        P(None, "chan", None),
        P(None, None, None, "chan"),
        P(),
    )
    return jax.shard_map(
        shards,
        mesh=mesh,
        in_specs=(rows, P("dp"), rows) + weights + weights,
        out_specs=(rows, rows) + weights + weights + weights,
        check_vma=False,
    )
```

time: 897 us -> 479 us (0.53)
  other arithmetic: 232 us -> 11.5 us
  local copies, waits for them, and re-layouts: 186 us -> 17.4 us
  matrix products: 112 us -> 0 us
  waiting for transfers between devices: 67.1 us -> 153 us
  Pallas kernels: 203 us -> 244 us
  blocking collectives: 58.6 us -> 37.6 us
  starting transfers between devices: 9.59 us -> 0.2 us
    dot_general x14 -> x0, matrix products: 112 us -> none  [dot_over(): lax.dot_general(left, right, (((over_left,), (over_right,)), ((), ())), p...]
    slice x20 -> x0, local copies, waits for them, and re-layouts: 92.3 us -> none  [the longest x3 56.8 us: depthwise(): tap = kern[step * 9 + row * 3 + column]]
    reduce_scatter x2 -> x3, waiting for transfers between devices: 7.53 us -> 85.8 us  [shards(): lax.psum_scatter(v, 'chan', scatter_dimension=axis, tiled=True)]
    convert_element_type x10 -> x0, other arithmetic: 77.7 us -> none  [the longest x2 26.9 us: shards(): act3 = (mask * gelu_soft(norm3)).astype(jnp.bfloat16)]
    reduce_sum x8 -> x0, other arithmetic: 48.7 us -> none  [the longest x6 47.5 us: kernel_grad(): taps.append(jnp.sum(field * part, axis=(0, 1, 2)))]
    pallas_call x7 -> x1, Pallas kernels: 203 us -> 244 us  [whole_call(): pl.pallas_call(functools.partial(whole_kernel, groups, lanes), out_shape=...]
    mul x14 -> x0, other arithmetic: 35.4 us -> none  [the longest x2 23.3 us: shards(): third_grad = mask * (p * e3 + q + r * third)]
    add x2 -> x0, other arithmetic: 22.7 us -> none  [shards(): third = a2 * conv + b2 * edge]
  transfers between devices with their start and end apart: 11 -> 5, of which waited for: 3 -> 5; matrix products, arithmetic and copies ran while one was open for 47% -> 1% of each run, Pallas kernels for 20% -> 0%
where the time goes in v3:
time: 479 us; the launch traced here: 478 us
  Pallas kernels  244 us (51%)
  waiting for transfers between devices  153 us (32%)
  blocking collectives  37.6 us (8%)
  local copies, waits for them, and re-layouts  17.4 us (4%)
  between operations  14.7 us (3%)
  other arithmetic  11.5 us (2%)
    pallas_call x1, Pallas kernels, whole_call(): pl.pallas_call(functools.partial(whole_kernel, groups, lanes), out_shape=...  244 us
    reduce_scatter x3, waiting for transfers between devices, shards(): lax.psum_scatter(v, 'chan', scatter_dimension=axis, tiled=True)  85.8 us
    psum x1, waiting for transfers between devices, shards(): lax.psum((scatter(gred, 1), scatter(gmix, 1), scatter(gdep, 2), scatter(g...  44.2 us
    psum x1, blocking collectives, shards(): lax.psum((scatter(gred, 1), scatter(gmix, 1), scatter(gdep, 2), scatter(g...  37.6 us
    unnamed x6, waiting for transfers between devices  22.5 us
    unnamed x55, local copies, waits for them, and re-layouts  16.2 us
  transfers between devices with their start and end apart: 5, of which 5 were waited for; matrix products, arithmetic and copies ran while one was open for 1% of the time, Pallas kernels for 0%

profile of v3, /device:TPU:0, one launch (start us, length us, event | category | flops | bytes accessed | tf_op | source)
XLA Modules:
  0.0 478.3 jit_solution(18299975942524689013)
XLA Ops:
  7.2 0.8 copy.49
  8.0 0.7 reshape.53
  8.7 1.8 convert_bitcast_fusion.reduce_loc
  10.5 1.8 convert_element_type.19.expand_loc
  12.3 1.5 convert_bitcast_fusion.1.mix_loc
  15.6 244.2 %shard_map.302 = (bf16[2352,1024]{1,0:T(8,128)(2,1)}, bf16[2352,1024]{1,0:T(8,128)(2,1)}, f32[2,256,1024]{2,1,0:T(8,128)}, f32[2,256,1024]{2,1,0:T(8,128)}, f32[...) custom-call(s32[1]{0:T(128)S(6)} %copy.73.counts, ...), custom_call_target="tpu_custom_call" | custom-call | tf_op jit(solution)/shard_map/pallas_call | solution.py:858
  260.1 0.7 reduce-scatter.7.cloned.1.call-update
  261.5 1.0 copy.56
  262.5 0.8 reshape.56
  263.4 17.7 %reduce-scatter.9.cloned.1.call-done = f32[2,64,256]{2,1,0:T(8,128)} async-done(((f32[2,256,256]{2,1,0:T(8,128)}), f32[2,64,256]{2,1,0:T(8,128)}) %reduce-scatter.9.cloned.1.call-update) | async-done | bytes 131088 | tf_op jit(solution)/shard_map/reduce_scatter | solution.py:959
  281.2 34.1 %reduce-scatter.7.cloned.1.call-done = f32[2,64,1024]{2,1,0:T(8,128)} async-done(((f32[2,256,1024]{2,1,0:T(8,128)}), f32[2,64,1024]{2,1,0:T(8,128)}) %reduce-scatter.7.cloned.1.call-update) | async-done | bytes 524304 | tf_op jit(solution)/shard_map/reduce_scatter | solution.py:959
  315.3 34.0 %reduce-scatter.11.cloned.1.call-done = f32[2,64,1024]{2,1,0:T(8,128)} async-done(((f32[2,256,1024]{2,1,0:T(8,128)}), f32[2,64,1024]{2,1,0:T(8,128)}) %reduce-scatter.11.cloned.1.call-update) | async-done | bytes 524304 | tf_op jit(solution)/shard_map/reduce_scatter | solution.py:959
  349.4 0.7 multiply_subtract_fusion.5
  350.7 21.2 %reduce-scatter.13.cloned.1.call-done = f32[64,54]{1,0:T(8,128)} async-done(((f32[256,54]{1,0:T(8,128)}), f32[64,54]{1,0:T(8,128)}) %reduce-scatter.13.cloned.1.call-update) | async-done | bytes 13840
  371.9 0.9 reshape.57
  372.8 37.6 %psum.30 = f32[2,27,64]{2,1,0:T(8,128)S(1)} all-reduce(f32[2,27,64]{2,1,0:T(8,128)S(1)} %copy.57), channel_id=1, replica_groups=mesh['dp'=8,'chan'=4] {'dp'}, use_global_device_ids=true, to_apply=%region_5.6 | all-reduce | flops 3456 | bytes 27648 | tf_op jit(solution)/shard_map/psum | solution.py:960
  412.4 44.2 %all-reduce.4.cloned.1.call-done = (f32[2,1024,64]{1,2,0:T(8,128)}, f32[2,256,64]{1,2,0:T(8,128)}, f32[2,64,1024]{2,1,0:T(8,128)}) async-done(((f32[2,1024,64]{1,2,0:T(8,128)}, f32[2,256,64]{1,2,0:T(8,128)}, f32[2,64,1024]{2,1,0:T(8,128)}), (f32[2,1024,64]{1,2,0:T(8,128)}, f32[2,256,64]{1,2,0:T(8,128)}, f32[2,64,1024]{2,1,0:T(8,128)})) %all-reduce.4.cloned.1.call-update) | async-done | bytes 1179664 | tf_op jit(solution)/shard_map/psum | solution.py:960
  456.6 2.2 multiply_subtract_fusion.1
  458.8 2.2 multiply_subtract_fusion
  461.0 0.7 multiply_subtract_fusion.2
  461.7 5.6 %copy.74 = bf16[2352,1024]{1,0:T(8,128)(2,1)} copy(bf16[2352,1024]{1,0:T(8,128)(2,1)} %get-tuple-element.132) | data formatting | bytes 9633792
  467.3 2.2 copy.75
  469.5 0.8 copy.76
  471.0 0.8 copy.78
  (65 shorter events, 5.5 us)
Async XLA Ops:
  7.2 274.0 %reduce-scatter.9.cloned.1.call-start = ((), (), s32[]{:S(2)}) async-start(), calls=%async_computation.5 | async-start | bytes 655360 | tf_op jit(solution)/shard_map/reduce_scatter | solution.py:959
  259.8 89.5 %copy-start.16 = (f32[12,256]{1,0:T(8,128)S(1)}, f32[12,256]{1,0:T(8,128)}, u32[]{:S(2)}) copy-start(f32[12,256]{1,0:T(8,128)} %get-tuple-element.34) | copy-start | bytes 36868
  259.8 89.5 %copy-start.17 = (f32[4,1024]{1,0:T(4,128)S(1)}, f32[4,1024]{1,0:T(4,128)}, u32[]{:S(2)}) copy-start(f32[4,1024]{1,0:T(4,128)} %get-tuple-element.35) | copy-start | bytes 49156
  259.9 89.5 %copy-start.14 = (f32[2,3,2,64]{3,2,1,0:T(2,128)S(1)}, f32[2,3,2,64]{3,2,1,0:T(2,128)}, u32[]{:S(2)}) copy-start(f32[2,3,2,64]{3,2,1,0:T(2,128)} %param.22) | copy-start | bytes 9220
  259.9 89.5 %copy-start.18 = (f32[2,3,2,64]{3,2,1,0:T(2,128)S(1)}, f32[2,3,2,64]{3,2,1,0:T(2,128)}, u32[]{:S(2)}) copy-start(f32[2,3,2,64]{3,2,1,0:T(2,128)} %param.28) | copy-start | bytes 9220
  259.9 90.2 %copy-start.11 = (f32[2,2,1024]{2,1,0:T(2,128)S(1)}, f32[2,2,1024]{2,1,0:T(2,128)}, u32[]{:S(2)}) copy-start(f32[2,2,1024]{2,1,0:T(2,128)} %norm_out.1) | copy-start | bytes 49156
  259.9 90.2 %copy-start.15 = (f32[2,2,1024]{2,1,0:T(2,128)S(1)}, f32[2,2,1024]{2,1,0:T(2,128)}, u32[]{:S(2)}) copy-start(f32[2,2,1024]{2,1,0:T(2,128)} %param.29) | copy-start | bytes 49156
  259.9 151.2 %copy-start.10 = (f32[2,27,64]{2,0,1:T(2,128)S(1)}, f32[2,27,64]{2,0,1:T(2,128)}, u32[]{:S(2)}) copy-start(f32[2,27,64]{2,0,1:T(2,128)} %param.20) | copy-start | bytes 41476
  259.9 151.2 %copy-start.13 = (f32[2,27,64]{2,0,1:T(2,128)S(1)}, f32[2,27,64]{2,0,1:T(2,128)}, u32[]{:S(2)}) copy-start(f32[2,27,64]{2,0,1:T(2,128)} %param.26) | copy-start | bytes 41476
  259.9 196.7 %copy-start = (f32[2,1024,64]{1,2,0:T(8,128)S(1)}, f32[2,1024,64]{1,2,0:T(8,128)}, u32[]{:S(2)}) copy-start(f32[2,1024,64]{1,2,0:T(8,128)} %param.18) | copy-start | bytes 1572868
  259.9 196.6 %copy-start.4 = (f32[2,1024,64]{1,2,0:T(8,128)S(1)}, f32[2,1024,64]{1,2,0:T(8,128)}, u32[]{:S(2)}) copy-start(f32[2,1024,64]{1,2,0:T(8,128)} %param.24) | copy-start | bytes 1572868
  260.0 55.3 %reduce-scatter.7.cloned.1.call-start = ((), (), s32[]{:S(2)}) async-start(), calls=%async_computation.4 | async-start | bytes 2621440 | tf_op jit(solution)/shard_map/reduce_scatter | solution.py:959
  260.0 198.8 %copy-start.1 = (f32[2,64,1024]{2,1,0:T(8,128)S(1)}, f32[2,64,1024]{2,1,0:T(8,128)}, u32[]{:S(2)}) copy-start(f32[2,64,1024]{2,1,0:T(8,128)} %param.21) | copy-start | bytes 1572868
  260.0 198.8 %copy-start.5 = (f32[2,64,1024]{2,1,0:T(8,128)S(1)}, f32[2,64,1024]{2,1,0:T(8,128)}, u32[]{:S(2)}) copy-start(f32[2,64,1024]{2,1,0:T(8,128)} %param.27) | copy-start | bytes 1572868
  260.7 88.5 %reduce-scatter.11.cloned.1.call-start = ((), (), s32[]{:S(2)}) async-start(), calls=%async_computation.6 | async-start | bytes 2621440 | tf_op jit(solution)/shard_map/reduce_scatter | solution.py:959
  260.8 200.2 %copy-start.6 = (f32[2,256,64]{1,2,0:T(8,128)S(1)}, f32[2,256,64]{1,2,0:T(8,128)}, u32[]{:S(2)}) copy-start(f32[2,256,64]{1,2,0:T(8,128)} %param.19) | copy-start | bytes 393220
  260.8 200.2 %copy-start.9 = (f32[2,256,64]{1,2,0:T(8,128)S(1)}, f32[2,256,64]{1,2,0:T(8,128)}, u32[]{:S(2)}) copy-start(f32[2,256,64]{1,2,0:T(8,128)} %param.25) | copy-start | bytes 393220
  261.5 110.4 %reduce-scatter.13.cloned.1.call-start = ((), (), s32[]{:S(2)}) async-start(), calls=%async_computation.7 | async-start | bytes 163840
  263.4 193.2 %all-reduce.4.cloned.1.call-start = ((), (), s32[]{:S(2)}) async-start(), calls=%async_computation.8 | async-start | bytes 2359296 | tf_op jit(solution)/shard_map/psum | solution.py:960
  349.4 117.9 %copy-start.12 = (f32[2,2,1024]{2,1,0:T(2,128)}, f32[2,2,1024]{2,1,0:T(2,128)S(1)}, u32[]{:S(2)}) copy-start(f32[2,2,1024]{2,1,0:T(2,128)S(1)} %reshape.55) | copy-start | bytes 49156
  456.6 4.4 copy-start.7
  461.0 6.3 %slice-start = ((s8[4816896]{0:T(1024)(128)(4,1)}), s8[4194304]{0:T(1024)(128)(4,1)S(1)}, s32[]{:S(2)}) async-start(s8[4816896]{0:T(1024)(128)(4,1)} %bitcast.8), calls=%async_computation.9 | async-start | bytes 8388608
  461.7 5.6 %slice-start.1 = ((s8[4816896]{0:T(1024)(128)(4,1)}), s8[622592]{0:T(1024)(128)(4,1)S(1)}, s32[]{:S(2)}) async-start(s8[4816896]{0:T(1024)(128)(4,1)} %bitcast.8), calls=%async_computation.10 | async-start | bytes 1245184
  467.3 3.7 copy-start.2
  (2 other events, 2.9 us)
Sparse Core Ops, SparseCore 0:
  260.1 21.0 reduce-scatter.8
  283.8 31.3 reduce-scatter.6
  317.8 31.4 reduce-scatter.10
  352.3 19.5 reduce-scatter.12
  375.5 81.0 all-reduce.3

commit v4 on v3

--- a/solution.py
+++ b/solution.py
@@ -17,6 +17,7 @@
 QUADS = HH // GROUP
 FLAT = GROUP * WW
 WIDE = GROUP * WP
+PIECES = 8
 
 EPS = 1e-05
 LEARN_RATE = 0.001
@@ -144,10 +145,7 @@
     norm_out,
     out_hbm,
     gtok_hbm,
-    gred_hbm,
-    gexp_hbm,
-    gmix_hbm,
-    gdep_out,
+    grads_out,
     gmid_out,
     gout_out,
     x0,
@@ -172,8 +170,12 @@
     d2s,
     halo_send,
     halo_recv,
-    gbig,
-    gmix,
+    grad_a,
+    grad_ra,
+    grad_b,
+    grad_rb,
+    grad_all,
+    grad_top,
     near,
     far,
     top,
@@ -189,6 +191,14 @@
     halo_rsem,
     load_sem,
     store_sem,
+    grad_sa,
+    grad_qa,
+    grad_sb,
+    grad_qb,
+    grad_sc,
+    grad_qc,
+    grad_st,
+    grad_qt,
 ):
     net = Net(groups, lanes)
     lane = net.lane
@@ -463,6 +473,94 @@
             done.append(lax.fori_loop(0, HH // 2, two_rows, tuple(a[half] for a in acc)))
         return [[done[0][k], done[1][k]] for k in range(len(acc))]
 
+    class Reduction:
+        def __init__(self, first, size, out_row):
+            self.lines = pl.ds(first, size)
+            self.size, self.out_row = size, out_row
+            self.which = 0 if first == 0 else 1
+            self.open = []
+
+        def put(self, who, piece, first, value):
+            grad_a[who, piece, pl.ds(self.lines.start + first, value.shape[0])] = value.astype(BF16)
+
+        def clear(self):
+            for copy in self.open:
+                copy.wait_send()
+            self.open = []
+
+        def move(self, copy):
+            copy.start()
+            self.open.append(copy)
+
+        def to_chan(self, b):
+            i = 2 * b + self.which
+            for step, (who, device) in enumerate(net.chan_peers()):
+                src, dst = grad_a.at[who, :, self.lines], grad_ra.at[own, :, self.lines]
+                self.move(push(src, dst, grad_sa.at[i, step], grad_qa.at[i, own], device))
+
+        def low_peers(self):
+            rows = [lax.rem(net.row_low + o, net.low) for o in range(1, net.low)]
+            return [(row, (net.row_high * net.low + row, lane)) for row in rows]
+
+        def to_rows(self, b):
+            i = 2 * b + self.which
+            for step, (who, device) in enumerate(net.chan_peers()):
+                src, dst = grad_a.at[who, :, self.lines], grad_ra.at[who, :, self.lines]
+                push(src, dst, grad_sa.at[i, step], grad_qa.at[i, who], device).wait_recv()
+
+            def add(piece, _):
+                total = grad_a[own, piece, self.lines].astype(F32)
+                for who, _device in net.chan_peers():
+                    total = total + grad_ra[who, piece, self.lines].astype(F32)
+                grad_b[piece, self.lines] = total.astype(BF16)
+                return 0
+
+            lax.fori_loop(0, PIECES, add, 0)
+            each = PIECES // net.low
+            for step, (who, device) in enumerate(self.low_peers()):
+                src = grad_b.at[pl.ds(who * each, each), self.lines]
+                dst = grad_rb.at[net.row_low, :, self.lines]
+                self.move(push(src, dst, grad_sb.at[i, step], grad_qb.at[i, net.row_low], device))
+
+        def to_all(self, b):
+            i = 2 * b + self.which
+            each = PIECES // net.low
+            mine = pl.ds(net.row_low * each, each)
+            for step, (who, device) in enumerate(self.low_peers()):
+                src, dst = grad_b.at[mine, self.lines], grad_rb.at[who, :, self.lines]
+                push(src, dst, grad_sb.at[i, step], grad_qb.at[i, who], device).wait_recv()
+            total = grad_b[mine, self.lines].astype(F32)
+            for who, _device in self.low_peers():
+                total = total + grad_rb[who, :, self.lines].astype(F32)
+            if net.high > 1:
+                grad_top[b, net.row_high, :, self.lines] = total.astype(BF16)
+                for step, (who, device) in enumerate(net.top()):
+                    here = grad_top.at[b, net.row_high, :, self.lines]
+                    self.move(push(here, here, grad_st.at[i, step], grad_qt.at[i, net.row_high], device))
+                for step, (who, device) in enumerate(net.top()):
+                    there = grad_top.at[b, who, :, self.lines]
+                    push(there, there, grad_st.at[i, step], grad_qt.at[i, who], device).wait_recv()
+                total = grad_top[b, 0, :, self.lines].astype(F32)
+                for j in range(1, net.high):
+                    total = total + grad_top[b, j, :, self.lines].astype(F32)
+            grad_all[mine, self.lines] = total.astype(BF16)
+            for step, (who, device) in enumerate(self.low_peers()):
+                here = grad_all.at[mine, self.lines]
+                self.move(push(here, here, grad_sc.at[i, step], grad_qc.at[i, net.row_low], device))
+
+        def finish(self, b):
+            i = 2 * b + self.which
+            each = PIECES // net.low
+            for step, (who, device) in enumerate(self.low_peers()):
+                there = grad_all.at[pl.ds(who * each, each), self.lines]
+                push(there, there, grad_sc.at[i, step], grad_qc.at[i, who], device).wait_recv()
+            for piece in range(PIECES):
+                cols = slice(128 * piece, 128 * (piece + 1))
+                grads_out[b, self.out_row : self.out_row + self.size, cols] = grad_all[piece, self.lines].astype(F32)
+
+    early = Reduction(0, 96, 0)
+    final = Reduction(96, 64, 96)
+
     order = (0, last) + tuple(range(1, last))
     norms = []
     mid_grads = {}
@@ -604,7 +702,6 @@
     for copy in out_store:
         copy.start()
 
-    grad_stores = []
     for b in reversed(range(BLOCKS)):
         turn = BLOCKS - 1 - b
         base = 6 + 3 * turn
@@ -652,12 +749,16 @@
         total_start(base + 1, rows_of(*[flat_sum(a) for a in acc]))
 
         if turn > 0:
-            for copy in grad_stores:
-                copy.wait()
+            early.to_all(b + 1)
+            final.to_rows(b + 1)
+            early.clear()
 
         def expand_grad(i, _):
             cols = pl.ds(pl.multiple_of(i * 256, 256), 256)
-            gbig[0, :, cols] = dot_rows(a3s[b], yb[:, cols])
+            g = dot_rows(a3s[b], yb[:, cols])
+            for who in range(lanes):
+                for h in range(2):
+                    early.put(who, 2 * i + h, 0, g[share * who : share * (who + 1), 128 * h : 128 * (h + 1)])
             return 0
 
         lax.fori_loop(0, 4, expand_grad, 0)
@@ -772,15 +873,29 @@
                     return tuple(new)
 
                 taps_grad = lax.fori_loop(0, HH, tap_rows, taps_grad)
-            for k in range(KVOL):
-                gdep_out[b, k : k + 1, cols] = flat_sum(taps_grad[k])
-        gmix[b] = dot_rows(d2s[...].reshape(frames * HH * WP, 256), a1s[...].reshape(frames * HH * WP, 256))
+            lines = jnp.concatenate(
+                [flat_sum(t) for t in taps_grad] + [jnp.zeros((WP - KVOL, 128), F32)], axis=0
+            )
+            for r in range(4):
+                part = jnp.concatenate([lines[8 * r : 8 * r + 8], zero8(128)], axis=0)
+                for who in range(lanes):
+                    early.put(who, 2 * r + half, 80, part)
+        g = dot_rows(d2s[...].reshape(frames * HH * WP, 256), a1s[...].reshape(frames * HH * WP, 256))
+        for who in range(lanes):
+            for r in range(4):
+                for h in range(2):
+                    first = share * who + 16 * r
+                    early.put(who, 2 * r + h, 64, g[first : first + 16, 128 * h : 128 * (h + 1)])
+        if turn > 0:
+            early.finish(b + 1)
+            final.to_all(b + 1)
+        early.to_chan(b)
 
         got = total_finish(base + 2)
         slope1, bias1, gain1, shift1 = back_affine(got[0:1], got[1:2], count, norm1)
         mid_grads[b] = ((gain1, shift1), (gain2, shift2), (gain3, shift3))
 
-        def input_grad(q):
+        def first_grad(q):
             f = lax.div(q, QUADS)
             rows = pl.ds(pl.multiple_of(q * FLAT, FLAT), FLAT)
             wide = pl.ds(q * GROUP, GROUP)
@@ -788,12 +903,21 @@
             z = z1[b, wide].reshape(WIDE, 256)
             d1 = squeeze((e1 * a1 + (z * slope1 + bias1)) * live(f)).astype(BF16)
             a3s[b, rows] = d1
-            return f, rows, dot(d1, red_t[b]) + sb[rows].astype(F32)
+            return f, rows, d1
+
+        def reduce_grad(i, _):
+            cols = pl.ds(pl.multiple_of(i * 256, 256), 256)
+            g = dot_rows(a3s[b], xs[b][:, cols])
+            for who in range(lanes):
+                for h in range(2):
+                    final.put(who, 2 * i + h, 0, g[share * who : share * (who + 1), 128 * h : 128 * (h + 1)])
+            return 0
 
         if b > 0:
 
             def passing(q, carry):
-                f, rows, g = input_grad(q)
+                f, rows, d1 = first_grad(q)
+                g = dot(d1, red_t[b]) + sb[rows].astype(F32)
                 z, pre = open_block(b - 1, q, f, rows)
                 s = gelu_slope(pre) * (g * live(f))
                 sb[rows] = s.astype(BF16)
@@ -801,31 +925,36 @@
 
             carry = lax.fori_loop(0, frames * QUADS, passing, (zero8(1024), zero8(1024)))
             total_start(base + 3, rows_of(flat_sum(carry[0]), flat_sum(carry[1])))
+            lax.fori_loop(0, 4, reduce_grad, 0)
+            final.to_chan(b)
+            early.to_rows(b)
         else:
 
-            def final(q, _):
-                f, rows, g = input_grad(q)
-                yb[rows] = g.astype(BF16)
+            def only_d1(q, _):
+                first_grad(q)
                 return 0
 
-            lax.fori_loop(0, frames * QUADS, final, 0)
+            lax.fori_loop(0, frames * QUADS, only_d1, 0)
+            final.clear()
+            lax.fori_loop(0, 4, reduce_grad, 0)
+            final.to_chan(b)
+            final.finish(b + 1)
+            early.to_rows(b)
+
+            def closing_grad(q, _):
+                rows = pl.ds(pl.multiple_of(q * FLAT, FLAT), FLAT)
+                yb[rows] = (dot(a3s[b, rows], red_t[b]) + sb[rows].astype(F32)).astype(BF16)
+                return 0
+
             gtok_store = [frame_copy(yb, gtok_hbm, f, store_sem.at[f]) for f in range(frames)]
-            for copy in gtok_store:
-                copy.start()
-
-        def reduce_grad(i, _):
-            cols = pl.ds(pl.multiple_of(i * 256, 256), 256)
-            gbig[1, :, cols] = dot_rows(a3s[b], xs[b][:, cols])
-            return 0
-
-        lax.fori_loop(0, 4, reduce_grad, 0)
-        grad_stores = [
-            pltpu.make_async_copy(gbig.at[0], gexp_hbm.at[b], store_sem.at[frames]),
-            pltpu.make_async_copy(gbig.at[1], gred_hbm.at[b], store_sem.at[frames + 1]),
-            pltpu.make_async_copy(gmix.at[b], gmix_hbm.at[b], store_sem.at[frames + 2]),
-        ]
-        for copy in grad_stores:
-            copy.start()
+            for f in range(frames):
+                lax.fori_loop(f * QUADS, (f + 1) * QUADS, closing_grad, 0)
+                gtok_store[f].start()
+            final.to_rows(b)
+            early.to_all(b)
+            final.to_all(b)
+            early.finish(b)
+            final.finish(b)
 
     for b in range(BLOCKS):
         for k in range(3):
@@ -835,8 +964,10 @@
         for w in range(2):
             gout_out[2 * b + w : 2 * b + w + 1] = out_grads[b][w]
 
-    for copy in grad_stores + gtok_store:
+    for copy in gtok_store:
         copy.wait()
+    early.clear()
+    final.clear()
     for copy in late:
         copy.wait_send()
     for side in range(2):
@@ -860,15 +991,12 @@
         out_shape=(
             shape((rows, 1024), BF16),
             shape((rows, 1024), BF16),
-            shape((BLOCKS, 256, 1024), F32),
-            shape((BLOCKS, 256, 1024), F32),
-            shape((BLOCKS, 256, 256), F32),
-            shape((BLOCKS, KVOL, 256), F32),
+            shape((BLOCKS, 160, 1024), F32),
             shape((BLOCKS * 6, 256), F32),
             shape((BLOCKS * 2, 1024), F32),
         ),
         in_specs=[pl.BlockSpec(memory_space=pltpu.SMEM), hbm, hbm] + [whole] * 5,
-        out_specs=[hbm] * 5 + [whole] * 3,
+        out_specs=[hbm] * 2 + [whole] * 3,
         scratch_shapes=[
             pltpu.VMEM((rows, 1024), BF16),
             pltpu.VMEM((rows, 1024), BF16),
@@ -892,8 +1020,12 @@
             pltpu.VMEM((lines, WP, 256), BF16),
             pltpu.VMEM((2, HH, WP, 256), BF16),
             pltpu.VMEM((2 * BLOCKS, 2, HH, WP, 256), BF16),
-            pltpu.VMEM((2, 256, 1024), F32),
-            pltpu.VMEM((BLOCKS, 256, 256), F32),
+            pltpu.VMEM((lanes, PIECES, 160, 128), BF16),
+            pltpu.VMEM((lanes, PIECES, 160, 128), BF16),
+            pltpu.VMEM((PIECES, 160, 128), BF16),
+            pltpu.VMEM((low, PIECES // low, 160, 128), BF16),
+            pltpu.VMEM((PIECES, 160, 128), BF16),
+            pltpu.VMEM((BLOCKS, high, PIECES // low, 160 if high > 1 else 16, 128), BF16),
             pltpu.VMEM((sums, 2, 8, 256), F32),
             pltpu.VMEM((sums, far, 8, 256), F32),
             pltpu.VMEM((sums, high, 8, 256), F32),
@@ -908,7 +1040,15 @@
             dma((kinds, 2)),
             dma((kinds, 2)),
             dma((frames + 1,)),
-            dma((frames + 3,)),
+            dma((frames,)),
+            dma((2 * BLOCKS, lanes)),
+            dma((2 * BLOCKS, lanes)),
+            dma((2 * BLOCKS, low)),
+            dma((2 * BLOCKS, low)),
+            dma((2 * BLOCKS, low)),
+            dma((2 * BLOCKS, low)),
+            dma((2 * BLOCKS, high)),
+            dma((2 * BLOCKS, high)),
         ],
         compiler_params=pltpu.CompilerParams(
             collective_id=1, has_side_effects=True, vmem_limit_bytes=63 * 2**20
@@ -944,7 +1084,7 @@
     small = jnp.concatenate([w_depth.reshape(-1, narrow), norm_mid.reshape(-1, narrow)], axis=0)
     small = jnp.pad(small, ((0, -small.shape[0] % 8), (0, 0)))
     small = lax.dynamic_update_slice(jnp.zeros((small.shape[0], narrow * lanes), F32), small, (0, lane * narrow))
-    output, grad_tokens, gred, gexp, gmix, gdep, gmid, gout = whole_call(
+    output, grad_tokens, reduced, gmid, gout = whole_call(
         lax.axis_size("dp"),
         lanes,
         frame_counts,
@@ -956,13 +1096,13 @@
         small,
         norm_out,
     )
-    scatter = lambda v, axis: lax.psum_scatter(v, "chan", scatter_dimension=axis, tiled=True)
-    gred, gmix, gdep, gexp = lax.psum((scatter(gred, 1), scatter(gmix, 1), scatter(gdep, 2), scatter(gexp, 1)), "dp")
+    gmix = reduced[:, 64:80].reshape(BLOCKS, 16, 4, 256).swapaxes(1, 2).reshape(BLOCKS, narrow, 256)
+    gdep = reduced[:, 80:88].reshape(BLOCKS, 8, 4, 256).swapaxes(1, 2).reshape(BLOCKS, WP, 256)[:, :KVOL]
     grads = (
-        jnp.swapaxes(gred, 1, 2),
+        jnp.swapaxes(reduced[:, 96:], 1, 2),
         jnp.swapaxes(gmix, 1, 2),
-        gdep,
-        gexp,
+        lax.dynamic_slice_in_dim(gdep, lane * narrow, narrow, 2),
+        reduced[:, :64],
         lax.dynamic_slice_in_dim(gmid.reshape(BLOCKS, 3, 2, -1), lane * narrow, narrow, 3),
         gout.reshape(BLOCKS, 2, -1),
     )

time: 479 us -> 296 us (0.62)
  waiting for transfers between devices: 153 us -> 0 us
  blocking collectives: 37.6 us -> 0 us
  Pallas kernels: 244 us -> 268 us
  between operations: 14.7 us -> 1.56 us
  local copies, waits for them, and re-layouts: 17.4 us -> 12 us
    reduce_scatter x3 -> x0, waiting for transfers between devices: 85.8 us -> none  [shards(): lax.psum_scatter(v, 'chan', scatter_dimension=axis, tiled=True)]
    psum x1 -> x0, waiting for transfers between devices: 44.2 us -> none  [shards(): lax.psum((scatter(gred, 1), scatter(gmix, 1), scatter(gdep, 2), scatter(g...]
    psum x1 -> x0, blocking collectives: 37.6 us -> none  [shards(): lax.psum((scatter(gred, 1), scatter(gmix, 1), scatter(gdep, 2), scatter(g...]
    pallas_call x1, Pallas kernels: 244 us -> 268 us  [whole_call(): pl.pallas_call(functools.partial(whole_kernel, groups, lanes), out_shape=...]
    unnamed x6 -> x0, waiting for transfers between devices: 22.5 us -> none
    unnamed x55 -> x39, local copies, waits for them, and re-layouts: 16.2 us -> 8.85 us
  transfers between devices with their start and end apart: 5 -> 0, of which waited for: 5 -> 0; matrix products, arithmetic and copies ran while one was open for 1% -> 0% of each run, Pallas kernels for 0% -> 0%
where the time goes in v4:
time: 296 us; the launch traced here: 295 us
  Pallas kernels  268 us (91%)
  other arithmetic  12.9 us (4%)
  local copies, waits for them, and re-layouts  12 us (4%)
    pallas_call x1, Pallas kernels, whole_call(): pl.pallas_call(functools.partial(whole_kernel, groups, lanes), out_shape=...  268 us
    unnamed x39, local copies, waits for them, and re-layouts  8.85 us
    sub x6, other arithmetic, descend(): return (weight - LEARN_RATE * moment_new, moment_new)  7.8 us

profile of v4, /device:TPU:0, one launch (start us, length us, event | category | flops | bytes accessed | tf_op | source)
XLA Modules:
  0.0 294.9 jit_solution(10777653109268001029)
XLA Ops:
  1.3 1.8 convert_bitcast_fusion.reduce_loc
  3.1 1.5 convert_bitcast_fusion.1.mix_loc
  4.6 1.8 convert_element_type.19.expand_loc
  6.4 0.7 reshape.65
  7.1 0.7 copy.38
  7.9 0.5 dynamic_update_slice.3.small_loc
  8.4 0.0 copy-start.5
  8.4 0.6 copy-done.5
  9.0 268.3 %shard_map.302 = (bf16[2352,1024]{1,0:T(8,128)(2,1)}, bf16[2352,1024]{1,0:T(8,128)(2,1)}, f32[2,160,1024]{2,1,0:T(8,128)}, f32[12,256]{1,0:T(8,128)}, f32[4,1024]{1,0:T(4,128)}) custom-call(s32[1]{0:T(128)S(6)} %copy.44.counts, bf16[2352,1024]{1,0:T(8,128)(2,1)} %tokens.1, bf16[2352,1024]{1,0:T(8,128)(2,1)} %cotangent.1, ...), custom_call_target="tpu_custom_call" | custom-call | tf_op jit(solution)/shard_map/pallas_call | solution.py:989
  277.4 0.0 copy-start.4
  277.5 2.7 multiply_subtract_fusion.1
  280.2 0.9 slice.16
  281.1 0.1 reshape.66
  281.2 0.0 copy-start.3
  281.2 0.9 slice.17
  282.1 0.1 copy.40
  282.2 0.7 multiply_subtract_fusion.3
  282.9 2.3 multiply_subtract_fusion
  285.3 0.7 multiply_subtract_fusion.5
  286.0 0.0 copy-start.9
  286.1 0.7 multiply_subtract_fusion.2
  286.8 0.6 multiply_subtract_fusion.4
  287.4 5.2 %copy.45 = bf16[2352,1024]{1,0:T(8,128)(2,1)} copy(bf16[2352,1024]{1,0:T(8,128)(2,1)} %get-tuple-element.66) | data formatting | bytes 9633792
  292.6 2.2 copy.46
  (39 shorter events, 0.2 us)
Async XLA Ops:
  8.4 0.6 copy-start.5
  9.0 268.5 %copy-start = (f32[2,1024,64]{1,2,0:T(8,128)S(1)}, f32[2,1024,64]{1,2,0:T(8,128)}, u32[]{:S(2)}) copy-start(f32[2,1024,64]{1,2,0:T(8,128)} %param.18) | copy-start | bytes 1572868
  9.0 273.1 %copy-start.7 = (f32[2,27,64]{2,0,1:T(2,128)S(1)}, f32[2,27,64]{2,0,1:T(2,128)}, u32[]{:S(2)}) copy-start(f32[2,27,64]{2,0,1:T(2,128)} %param.20) | copy-start | bytes 41476
  9.0 273.2 %copy-start.10 = (f32[2,27,64]{2,0,1:T(2,128)S(1)}, f32[2,27,64]{2,0,1:T(2,128)}, u32[]{:S(2)}) copy-start(f32[2,27,64]{2,0,1:T(2,128)} %param.26) | copy-start | bytes 41476
  277.4 5.5 %copy-start.1 = (f32[2,64,1024]{2,1,0:T(8,128)S(1)}, f32[2,64,1024]{2,1,0:T(8,128)}, u32[]{:S(2)}) copy-start(f32[2,64,1024]{2,1,0:T(8,128)} %param.21) | copy-start | bytes 1572868
  277.4 5.5 %copy-start.4 = (f32[2,64,1024]{2,1,0:T(8,128)S(1)}, f32[2,64,1024]{2,1,0:T(8,128)}, u32[]{:S(2)}) copy-start(f32[2,64,1024]{2,1,0:T(8,128)} %param.27) | copy-start | bytes 1572868
  277.4 7.9 %copy-start.13 = (f32[12,256]{1,0:T(8,128)S(1)}, f32[12,256]{1,0:T(8,128)}, u32[]{:S(2)}) copy-start(f32[12,256]{1,0:T(8,128)} %get-tuple-element.28) | copy-start | bytes 36868
  277.4 7.9 %copy-start.11 = (f32[2,3,2,64]{3,2,1,0:T(2,128)S(1)}, f32[2,3,2,64]{3,2,1,0:T(2,128)}, u32[]{:S(2)}) copy-start(f32[2,3,2,64]{3,2,1,0:T(2,128)} %param.22) | copy-start | bytes 9220
  277.4 7.9 %copy-start.15 = (f32[2,3,2,64]{3,2,1,0:T(2,128)S(1)}, f32[2,3,2,64]{3,2,1,0:T(2,128)}, u32[]{:S(2)}) copy-start(f32[2,3,2,64]{3,2,1,0:T(2,128)} %param.28) | copy-start | bytes 9220
  277.4 8.6 %copy-start.14 = (f32[4,1024]{1,0:T(4,128)S(1)}, f32[4,1024]{1,0:T(4,128)}, u32[]{:S(2)}) copy-start(f32[4,1024]{1,0:T(4,128)} %get-tuple-element.29) | copy-start | bytes 49156
  277.4 8.6 %copy-start.2 = (f32[2,256,64]{1,2,0:T(8,128)S(1)}, f32[2,256,64]{1,2,0:T(8,128)}, u32[]{:S(2)}) copy-start(f32[2,256,64]{1,2,0:T(8,128)} %param.19) | copy-start | bytes 393220
  277.5 8.6 %copy-start.6 = (f32[2,256,64]{1,2,0:T(8,128)S(1)}, f32[2,256,64]{1,2,0:T(8,128)}, u32[]{:S(2)}) copy-start(f32[2,256,64]{1,2,0:T(8,128)} %param.25) | copy-start | bytes 393220
  277.5 9.3 %copy-start.8 = (f32[2,2,1024]{2,1,0:T(2,128)S(1)}, f32[2,2,1024]{2,1,0:T(2,128)}, u32[]{:S(2)}) copy-start(f32[2,2,1024]{2,1,0:T(2,128)} %norm_out.1) | copy-start | bytes 49156
  277.5 9.3 %copy-start.12 = (f32[2,2,1024]{2,1,0:T(2,128)S(1)}, f32[2,2,1024]{2,1,0:T(2,128)}, u32[]{:S(2)}) copy-start(f32[2,2,1024]{2,1,0:T(2,128)} %param.29) | copy-start | bytes 49156
  281.2 11.4 %copy-start.3 = (f32[2,4,16,256]{3,2,1,0:T(8,128)}, f32[2,4,16,256]{3,2,1,0:T(8,128)S(1)}, u32[]{:S(2)}) copy-start(f32[2,4,16,256]{3,2,1,0:T(8,128)S(1)} %copy.39) | copy-start | bytes 393220
  286.0 6.6 %copy-start.9 = (f32[2,2,1024]{2,1,0:T(2,128)}, f32[2,2,1024]{2,1,0:T(2,128)S(1)}, u32[]{:S(2)}) copy-start(f32[2,2,1024]{2,1,0:T(2,128)S(1)} %reshape.71) | copy-start | bytes 49156
  286.1 6.6 %slice-start = ((s8[4816896]{0:T(1024)(128)(4,1)}), s8[4194304]{0:T(1024)(128)(4,1)S(1)}, s32[]{:S(2)}) async-start(s8[4816896]{0:T(1024)(128)(4,1)} %bitcast.16), calls=%async_computation | async-start | bytes 8388608
  287.4 5.2 %slice-start.1 = ((s8[4816896]{0:T(1024)(128)(4,1)}), s8[622592]{0:T(1024)(128)(4,1)S(1)}, s32[]{:S(2)}) async-start(s8[4816896]{0:T(1024)(128)(4,1)} %bitcast.16), calls=%async_computation.1 | async-start | bytes 1245184
